TPU v7x, 32 devices: a whole 2x2x4 slice. The times are simulated.
32 devices in a mesh: wide: 8 (over y, x, core), narrow: 4 (over z).
Axes of the slice: x: 2, y: 2, z: 4, core: 2. Of those that a mesh axis runs over, the one named last changes fastest.
Arguments:
- targets: bfloat16 [32, 512, 768], P('wide', 'narrow'), may hold values from -6 to 6
- memory: bfloat16 [32, 512, 768], P('wide', 'narrow'), may hold values from -6 to 6
- cotangent: bfloat16 [32, 512, 768], P('wide', 'narrow'), may hold values from -6 to 6
- target_segments: int32 [32, 512], P('wide', 'narrow'), may hold values from 0 to 3, as said below
- memory_segments: int32 [32, 512], P('wide', 'narrow'), may hold values from 0 to 3, as said below
- buckets: int32 [512, 512], P('narrow'), may hold values from 0 to 31
- attn_in: float32 [6, 768, 768], P(None, ('wide', 'narrow')), may hold values from -0.109375 to 0.109375
- attn_out: float32 [2, 768, 768], P(None, ('wide', 'narrow')), may hold values from -1.75 to 1.75
- gains: float32 [3, 768], P(None, ('wide', 'narrow')), may hold values from 0.5 to 1.5
- ff_in: float32 [2, 768, 2048], P(None, ('wide', 'narrow')), may hold values from -0.21875 to 0.21875
- ff_out: float32 [2048, 768], P(('wide', 'narrow')), may hold values from -0.125 to 0.125
- bias_table: float32 [32, 12], replicated, may hold values from -4 to 4
Outputs:
- output: bfloat16 [32, 512, 768], P('wide', 'narrow')
- grad_targets: bfloat16 [32, 512, 768], P('wide', 'narrow')
- grad_memory: bfloat16 [32, 512, 768], P('wide', 'narrow')
- grad_attn_in: float32 [6, 768, 768], P(None, ('wide', 'narrow'))
- grad_attn_out: float32 [2, 768, 768], P(None, ('wide', 'narrow'))
- grad_gains: float32 [3, 768], P(None, ('wide', 'narrow'))
- grad_ff_in: float32 [2, 768, 2048], P(None, ('wide', 'narrow'))
- grad_ff_out: float32 [2048, 768], P(('wide', 'narrow'))
- grad_table: float32 [32, 12], replicated
- attn_in_rows: float32 [6, 768], P(None, ('wide', 'narrow'))
- attn_in_cols: float32 [6, 768], replicated
- attn_out_rows: float32 [2, 768], P(None, ('wide', 'narrow'))
- attn_out_cols: float32 [2, 768], replicated
- ff_in_rows: float32 [2, 768], P(None, ('wide', 'narrow'))
- ff_in_cols: float32 [2, 2048], replicated
- ff_out_rows: float32 [2048], P(('wide', 'narrow'))
- ff_out_cols: float32 [768], replicated
- new_attn_in: float32 [6, 768, 768], P(None, ('wide', 'narrow'))
- new_attn_out: float32 [2, 768, 768], P(None, ('wide', 'narrow'))
- new_ff_in: float32 [2, 768, 2048], P(None, ('wide', 'narrow'))
- new_ff_out: float32 [2048, 768], P(('wide', 'narrow'))
- new_table: float32 [32, 12], replicated
Inputs may be any that keep to these rules, and one draw needn't show every extreme that they name: `target_segments`: along each row the document numbers never fall and every number 0 to 3 occurs. `memory_segments`: along each row the document numbers never fall and every number 0 to 3 occurs.
All inputs are finite; a program needn't handle non-finite values.
Results may differ from a plain program's by a relative error of at most 0.03.
The roundings to bfloat16 on the way count: a program that leaves them out, or rounds other values in their place, can miss the bound.
Values may be sent and summed in bfloat16 or wider, within the bound.
No kernel may reach another device: no remote copies, remote signals or barrier semaphores. Data moves between devices by JAX's collectives and lax.ppermute only.
A program may use at most 256 MiB of HBM per device.

v0:
```python
import jax
import jax.numpy as jnp
from jax import lax
from jax.sharding import PartitionSpec as P

highest = lax.Precision.HIGHEST


def gelu_tanh(pre_act):
    return (
        0.5
        * pre_act
        * (1.0 + jnp.tanh(0.7978845608028654 * (pre_act + 0.044715 * pre_act * pre_act * pre_act)))
    )


def norm_parts(values_in, gain_row):
    inv_rms = lax.rsqrt(jnp.mean(values_in * values_in, axis=-1, keepdims=True) + 1e-06)
    unit_rows = values_in * inv_rms
    return (unit_rows, inv_rms, (unit_rows * gain_row).astype(jnp.bfloat16))


def norm_back(incoming, unit_rows, inv_rms, gain_row):
    scaled = incoming * gain_row
    grad_gain = jnp.sum(incoming * unit_rows, axis=(0, 1))
    inner_mean = jnp.mean(scaled * unit_rows, axis=-1, keepdims=True)
    return (inv_rms * (scaled - unit_rows * inner_mean), grad_gain)


def forward_mul(left_rows, right_matrix):
    return jnp.einsum("rld,de->rle", left_rows, right_matrix, preferred_element_type=jnp.float32)


def back_mul(left_rows, right_matrix):
    return jnp.einsum("rle,de->rld", left_rows, right_matrix, preferred_element_type=jnp.float32)


def weight_mul(left_rows, right_rows):
    return jnp.einsum("rld,rle->de", left_rows, right_rows, preferred_element_type=jnp.float32)


def head_split(stacked, head_count):
    return stacked.reshape(
        stacked.shape[0], stacked.shape[1], head_count, stacked.shape[2] // head_count
    )


def masked_scores(query_rows, key_rows, extra_bias, allowed, head_count):
    raw_scores = (
        jnp.einsum(
            "gqhd,gkhd->ghqk",
            head_split(query_rows, head_count),
            head_split(key_rows, head_count),
            preferred_element_type=jnp.float32,
        )
        + extra_bias
    )
    return jnp.where(allowed[:, None], raw_scores, -1000000000.0)


def attend_block(query_rows, key_rows, value_rows, extra_bias, allowed, head_count):
    scores = masked_scores(query_rows, key_rows, extra_bias, allowed, head_count)
    row_peak = jnp.max(scores, axis=-1, keepdims=True)
    exponent = jnp.exp(scores - row_peak)
    row_total = jnp.sum(exponent, axis=-1, keepdims=True)
    soft_weights = (exponent / row_total).astype(jnp.bfloat16)
    mixed_heads = jnp.einsum(
        "ghqk,gkhd->gqhd",
        soft_weights,
        head_split(value_rows, head_count),
        preferred_element_type=jnp.float32,
    )
    return (mixed_heads.reshape(query_rows.shape).astype(jnp.bfloat16), row_peak, row_total)


def attend_back(
    query_rows,
    key_rows,
    value_rows,
    extra_bias,
    allowed,
    row_peak,
    row_total,
    grad_rows,
    head_count,
    want_bias,
):
    scores = masked_scores(query_rows, key_rows, extra_bias, allowed, head_count)
    soft_weights = jnp.exp(scores - row_peak) / row_total
    grad_heads = head_split(grad_rows, head_count)
    grad_probs = jnp.einsum(
        "gqhd,gkhd->ghqk",
        grad_heads,
        head_split(value_rows, head_count),
        preferred_element_type=jnp.float32,
    )
    grad_values = jnp.einsum(
        "ghqk,gqhd->gkhd",
        soft_weights.astype(jnp.bfloat16),
        grad_heads,
        preferred_element_type=jnp.float32,
    ).reshape(key_rows.shape)
    inner_sum = jnp.sum(soft_weights * grad_probs, axis=-1, keepdims=True)
    grad_scores = (soft_weights * (grad_probs - inner_sum)).astype(jnp.bfloat16)
    grad_queries = jnp.einsum(
        "ghqk,gkhd->gqhd",
        grad_scores,
        head_split(key_rows, head_count),
        preferred_element_type=jnp.float32,
    ).reshape(query_rows.shape)
    grad_keys = jnp.einsum(
        "ghqk,gqhd->gkhd",
        grad_scores,
        head_split(query_rows, head_count),
        preferred_element_type=jnp.float32,
    ).reshape(key_rows.shape)
    if want_bias:
        return (
            grad_queries,
            grad_keys,
            grad_values,
            jnp.sum(grad_scores.astype(jnp.float32), axis=0),
        )
    return (grad_queries, grad_keys, grad_values)


def local_stats(gradient):
    squares = gradient * gradient + 1e-30
    return (jnp.sum(squares, axis=-1), jnp.sum(squares, axis=-2))


def adafactor_step(gradient, weight, rows_stat, cols_stat, weight_rms):
    overall = jnp.sum(cols_stat, axis=-1)[..., None, None]
    estimate = rows_stat[..., :, None] * cols_stat[..., None, :] / overall
    return weight - 0.3 * weight_rms * gradient * lax.rsqrt(estimate)


def body(
    targets,
    memory,
    cotangent,
    target_segments,
    memory_segments,
    buckets,
    attn_in,
    attn_out,
    gains,
    ff_in,
    ff_out,
    bias_table,
):
    rows_here, target_local, model_width = targets.shape
    ff_width = ff_in.shape[2]
    head_count = bias_table.shape[1]
    bucket_count = bias_table.shape[0]
    block_rows = max(1, min(rows_here, 512 // target_local))
    while rows_here % block_rows:
        block_rows -= 1
    block_count = rows_here // block_rows

    def grouped(stacked):
        return stacked.reshape((block_count, block_rows) + stacked.shape[1:])

    def ungrouped(stacked):
        return stacked.reshape((rows_here,) + stacked.shape[2:])

    gathered_in, gathered_out, gathered_fin, gathered_fout, gathered_gain = (
        lax.all_gather(attn_in.astype(jnp.bfloat16), ("wide", "narrow"), axis=1, tiled=True),
        lax.all_gather(attn_out.astype(jnp.bfloat16), ("wide", "narrow"), axis=1, tiled=True),
        lax.all_gather(ff_in.astype(jnp.bfloat16), ("wide", "narrow"), axis=1, tiled=True),
        lax.all_gather(ff_out.astype(jnp.bfloat16), ("wide", "narrow"), axis=0, tiled=True),
        lax.all_gather(gains.astype(jnp.bfloat16), ("wide", "narrow"), axis=1, tiled=True),
    )
    gain_full = gathered_gain.astype(jnp.float32)
    query_start = lax.axis_index("narrow") * target_local
    query_pos = query_start + jnp.arange(target_local, dtype=jnp.int32)
    key_pos = jnp.arange(target_local * lax.axis_size("narrow"), dtype=jnp.int32)
    causal = query_pos[:, None] >= key_pos[None, :]
    one_hot = (
        buckets[:, :, None] == jnp.arange(bucket_count, dtype=jnp.int32)[None, None, :]
    ).astype(jnp.float32)
    rel_bias = jnp.einsum("qkb,bh->hqk", one_hot, bias_table, precision=highest)
    inputs_f = targets.astype(jnp.float32)
    unit_attn, scale_attn, normed_attn = norm_parts(inputs_f, gain_full[0])
    self_query = forward_mul(normed_attn, gathered_in[0]).astype(jnp.bfloat16)
    self_key = forward_mul(normed_attn, gathered_in[1]).astype(jnp.bfloat16)
    self_value = forward_mul(normed_attn, gathered_in[2]).astype(jnp.bfloat16)
    seg_target = target_segments.astype(jnp.bfloat16)
    self_keys_all, self_values_all, target_segs_all = (
        lax.all_gather(self_key, "narrow", axis=1, tiled=True),
        lax.all_gather(self_value, "narrow", axis=1, tiled=True),
        lax.all_gather(seg_target, "narrow", axis=1, tiled=True),
    )

    def self_mask(seg_query, seg_key):
        return causal[None] & (seg_query[:, :, None] == seg_key[:, None, :])

    def cross_mask(seg_query, seg_key):
        return seg_query[:, :, None] == seg_key[:, None, :]

    def self_forward(pieces):
        query_rows, key_rows, value_rows, seg_query, seg_key = pieces
        return attend_block(
            query_rows, key_rows, value_rows, rel_bias, self_mask(seg_query, seg_key), head_count
        )

    self_mixed, self_peak, self_total = lax.map(
        self_forward,
        (
            grouped(self_query),
            grouped(self_keys_all),
            grouped(self_values_all),
            grouped(seg_target),
            grouped(target_segs_all),
        ),
    )
    self_mixed = ungrouped(self_mixed)
    after_self = inputs_f + forward_mul(self_mixed, gathered_out[0])
    unit_cross, scale_cross, normed_cross = norm_parts(after_self, gain_full[1])
    cross_query = forward_mul(normed_cross, gathered_in[3]).astype(jnp.bfloat16)
    seg_memory = memory_segments.astype(jnp.bfloat16)
    cross_key = forward_mul(memory, gathered_in[4]).astype(jnp.bfloat16)
    cross_value = forward_mul(memory, gathered_in[5]).astype(jnp.bfloat16)
    cross_keys_all, cross_values_all, memory_segs_all = (
        lax.all_gather(cross_key, "narrow", axis=1, tiled=True),
        lax.all_gather(cross_value, "narrow", axis=1, tiled=True),
        lax.all_gather(seg_memory, "narrow", axis=1, tiled=True),
    )

    def cross_forward(pieces):
        query_rows, key_rows, value_rows, seg_query, seg_key = pieces
        return attend_block(
            query_rows, key_rows, value_rows, 0.0, cross_mask(seg_query, seg_key), head_count
        )

    cross_mixed, cross_peak, cross_total = lax.map(
        cross_forward,
        (
            grouped(cross_query),
            grouped(cross_keys_all),
            grouped(cross_values_all),
            grouped(seg_target),
            grouped(memory_segs_all),
        ),
    )
    cross_mixed = ungrouped(cross_mixed)
    after_cross = after_self + forward_mul(cross_mixed, gathered_out[1])
    unit_ffn, scale_ffn, normed_ffn = norm_parts(after_cross, gain_full[2])
    gate_proj = forward_mul(normed_ffn, gathered_fin[0])
    up_proj = forward_mul(normed_ffn, gathered_fin[1])
    activated, gelu_pull = jax.vjp(gelu_tanh, gate_proj)
    hidden_ff = (activated * up_proj).astype(jnp.bfloat16)
    output = (after_cross + forward_mul(hidden_ff, gathered_fout)).astype(jnp.bfloat16)
    cot_f = cotangent.astype(jnp.float32)
    grad_fout = weight_mul(hidden_ff, cotangent)
    grad_hidden = back_mul(cotangent, gathered_fout)
    grad_gate = gelu_pull(grad_hidden * up_proj)[0].astype(jnp.bfloat16)
    grad_up = (grad_hidden * activated).astype(jnp.bfloat16)
    grad_fin = jnp.stack([weight_mul(normed_ffn, grad_gate), weight_mul(normed_ffn, grad_up)])
    grad_normed_ffn = back_mul(grad_gate, gathered_fin[0]) + back_mul(grad_up, gathered_fin[1])
    back_ffn, gain_grad_ffn = norm_back(grad_normed_ffn, unit_ffn, scale_ffn, gain_full[2])
    grad_after_cross = cot_f + back_ffn
    branch_cross = grad_after_cross.astype(jnp.bfloat16)
    grad_out_cross = weight_mul(cross_mixed, branch_cross)
    grad_mixed_cross = back_mul(branch_cross, gathered_out[1]).astype(jnp.bfloat16)

    def cross_backward(pieces):
        query_rows, key_rows, value_rows, seg_query, seg_key, row_peak, row_total, grad_rows = (
            pieces
        )
        return attend_back(
            query_rows,
            key_rows,
            value_rows,
            0.0,
            cross_mask(seg_query, seg_key),
            row_peak,
            row_total,
            grad_rows,
            head_count,
            False,
        )

    cross_dq, cross_dk, cross_dv = lax.map(
        cross_backward,
        (
            grouped(cross_query),
            grouped(cross_keys_all),
            grouped(cross_values_all),
            grouped(seg_target),
            grouped(memory_segs_all),
            cross_peak,
            cross_total,
            grouped(grad_mixed_cross),
        ),
    )
    cross_key_sum, cross_value_sum = (
        lax.psum_scatter(
            ungrouped(cross_dk).astype(jnp.bfloat16), "narrow", scatter_dimension=1, tiled=True
        ).astype(jnp.float32),
        lax.psum_scatter(
            ungrouped(cross_dv).astype(jnp.bfloat16), "narrow", scatter_dimension=1, tiled=True
        ).astype(jnp.float32),
    )
    cross_key_low = cross_key_sum.astype(jnp.bfloat16)
    cross_value_low = cross_value_sum.astype(jnp.bfloat16)
    cross_query_low = ungrouped(cross_dq).astype(jnp.bfloat16)
    grad_q_cross = weight_mul(normed_cross, cross_query_low)
    grad_k_cross = weight_mul(memory, cross_key_low)
    grad_v_cross = weight_mul(memory, cross_value_low)
    grad_memory = (
        back_mul(cross_key_low, gathered_in[4]) + back_mul(cross_value_low, gathered_in[5])
    ).astype(jnp.bfloat16)
    back_cross, gain_grad_cross = norm_back(
        back_mul(cross_query_low, gathered_in[3]), unit_cross, scale_cross, gain_full[1]
    )
    grad_after_self = grad_after_cross + back_cross
    branch_self = grad_after_self.astype(jnp.bfloat16)
    grad_out_self = weight_mul(self_mixed, branch_self)
    grad_mixed_self = back_mul(branch_self, gathered_out[0]).astype(jnp.bfloat16)

    def self_backward(pieces):
        query_rows, key_rows, value_rows, seg_query, seg_key, row_peak, row_total, grad_rows = (
            pieces
        )
        return attend_back(
            query_rows,
            key_rows,
            value_rows,
            rel_bias,
            self_mask(seg_query, seg_key),
            row_peak,
            row_total,
            grad_rows,
            head_count,
            True,
        )

    self_dq, self_dk, self_dv, self_dbias = lax.map(
        self_backward,
        (
            grouped(self_query),
            grouped(self_keys_all),
            grouped(self_values_all),
            grouped(seg_target),
            grouped(target_segs_all),
            self_peak,
            self_total,
            grouped(grad_mixed_self),
        ),
    )
    self_key_sum, self_value_sum = (
        lax.psum_scatter(
            ungrouped(self_dk).astype(jnp.bfloat16), "narrow", scatter_dimension=1, tiled=True
        ).astype(jnp.float32),
        lax.psum_scatter(
            ungrouped(self_dv).astype(jnp.bfloat16), "narrow", scatter_dimension=1, tiled=True
        ).astype(jnp.float32),
    )
    self_key_low = self_key_sum.astype(jnp.bfloat16)
    self_value_low = self_value_sum.astype(jnp.bfloat16)
    self_query_low = ungrouped(self_dq).astype(jnp.bfloat16)
    grad_q_self = weight_mul(normed_attn, self_query_low)
    grad_k_self = weight_mul(normed_attn, self_key_low)
    grad_v_self = weight_mul(normed_attn, self_value_low)
    grad_normed_attn = (
        back_mul(self_query_low, gathered_in[0])
        + back_mul(self_key_low, gathered_in[1])
        + back_mul(self_value_low, gathered_in[2])
    )
    back_attn, gain_grad_attn = norm_back(grad_normed_attn, unit_attn, scale_attn, gain_full[0])
    grad_targets = (grad_after_self + back_attn).astype(jnp.bfloat16)
    table_part = jnp.einsum("qkb,hqk->bh", one_hot, jnp.sum(self_dbias, axis=0), precision=highest)
    grad_in_part = jnp.stack(
        [grad_q_self, grad_k_self, grad_v_self, grad_q_cross, grad_k_cross, grad_v_cross]
    )
    grad_out_part = jnp.stack([grad_out_self, grad_out_cross])
    gain_part = jnp.stack([gain_grad_attn, gain_grad_cross, gain_grad_ffn])
    sum_in, sum_out, sum_fin, sum_fout, sum_gain = (
        lax.psum_scatter(grad_in_part, ("wide", "narrow"), scatter_dimension=1, tiled=True),
        lax.psum_scatter(grad_out_part, ("wide", "narrow"), scatter_dimension=1, tiled=True),
        lax.psum_scatter(grad_fin, ("wide", "narrow"), scatter_dimension=1, tiled=True),
        lax.psum_scatter(grad_fout, ("wide", "narrow"), scatter_dimension=0, tiled=True),
        lax.psum_scatter(gain_part, ("wide", "narrow"), scatter_dimension=1, tiled=True),
    )
    in_rows, in_part = local_stats(sum_in)
    out_rows, out_part = local_stats(sum_out)
    fin_rows, fin_part = local_stats(sum_fin)
    fout_rows, fout_part = local_stats(sum_fout)
    in_square = jnp.sum(attn_in * attn_in, axis=(1, 2))
    out_square = jnp.sum(attn_out * attn_out, axis=(1, 2))
    fin_square = jnp.sum(ff_in * ff_in, axis=(1, 2))
    fout_square = jnp.sum(ff_out * ff_out).reshape(1)
    (
        in_cols,
        out_cols,
        fin_cols,
        fout_cols,
        grad_table,
        in_total,
        out_total,
        fin_total,
        fout_total,
    ) = lax.psum(
        (
            in_part,
            out_part,
            fin_part,
            fout_part,
            table_part,
            in_square,
            out_square,
            fin_square,
            fout_square,
        ),
        ("wide", "narrow"),
    )
    table_rows, table_cols = local_stats(grad_table)
    square_count = model_width * model_width
    in_rms = jnp.sqrt(in_total / square_count + 1e-06)[:, None, None]
    out_rms = jnp.sqrt(out_total / square_count + 1e-06)[:, None, None]
    fin_rms = jnp.sqrt(fin_total / (model_width * ff_width) + 1e-06)[:, None, None]
    fout_rms = jnp.sqrt(fout_total[0] / (model_width * ff_width) + 1e-06)
    table_rms = jnp.sqrt(jnp.mean(bias_table * bias_table) + 1e-06)
    new_in = adafactor_step(sum_in, attn_in, in_rows, in_cols, in_rms)
    new_out = adafactor_step(sum_out, attn_out, out_rows, out_cols, out_rms)
    new_fin = adafactor_step(sum_fin, ff_in, fin_rows, fin_cols, fin_rms)
    new_fout = adafactor_step(sum_fout, ff_out, fout_rows, fout_cols, fout_rms)
    new_table = adafactor_step(grad_table, bias_table, table_rows, table_cols, table_rms)
    return (
        output,
        grad_targets,
        grad_memory,
        sum_in,
        sum_out,
        sum_gain,
        sum_fin,
        sum_fout,
        grad_table,
        in_rows,
        in_cols,
        out_rows,
        out_cols,
        fin_rows,
        fin_cols,
        fout_rows,
        fout_cols,
        new_in,
        new_out,
        new_fin,
        new_fout,
        new_table,
    )


def solution(mesh):
    in_specs = (
        P("wide", "narrow", None),
        P("wide", "narrow", None),
        P("wide", "narrow", None),
        P("wide", "narrow"),
        P("wide", "narrow"),
        P("narrow", None),
        P(None, ("wide", "narrow"), None),
        P(None, ("wide", "narrow"), None),
        P(None, ("wide", "narrow")),
        P(None, ("wide", "narrow"), None),
        P(("wide", "narrow"), None),
        P(),
    )
    out_specs = (
        P("wide", "narrow", None),
        P("wide", "narrow", None),
        P("wide", "narrow", None),
        P(None, ("wide", "narrow"), None),
        P(None, ("wide", "narrow"), None),
        P(None, ("wide", "narrow")),
        P(None, ("wide", "narrow"), None),
        P(("wide", "narrow"), None),
        P(),
        P(None, ("wide", "narrow")),
        P(),
        P(None, ("wide", "narrow")),
        P(),
        P(None, ("wide", "narrow")),
        P(),
        P(("wide", "narrow")),
        P(),
        P(None, ("wide", "narrow"), None),
        P(None, ("wide", "narrow"), None),
        P(None, ("wide", "narrow"), None),
        P(("wide", "narrow"), None),
        P(),
    )
    return jax.shard_map(body, mesh=mesh, in_specs=in_specs, out_specs=out_specs, check_vma=False)
```

profile of v0, /device:TPU:0, one launch (start us, length us, event | category | flops | bytes accessed | tf_op | source)
XLA Modules:
  0.0 1469.8 jit_solution(9814787439451147837)
XLA Ops:
  10.5 70.3 %all-gather = bf16[32,24,3]{1,2,0:T(4,128)(2,1)S(1)} all-gather(bf16[1,24,3]{1,2,0:T(4,128)(2,1)S(1)} %convert_bitcast_fusion), channel_id=1, replica_groups=mesh['wide'=8,'narrow'=4] {'wide','narrow'}, dimensions={0}, use_global_device_ids=true | all-gather | bytes 4752 | tf_op jit(solution)/shard_map/all_gather | solution.py:172
  105.1 37.3 %copy.141 = pred[128,512,32]{1,2,0:T(32,128)(4,1)S(1)} copy(pred[128,512,32]{0,2,1:T(32,128)(4,1)S(1)} %iota_compare_fusion) | data formatting | bytes 4194304 | tf_op jit(solution)/shard_map/eq | solution.py:180
  148.4 9.3 all_gather.40
  157.8 8.5 all_gather.36
  175.0 12.2 fusion.92
  187.2 29.8 %all-gather.12.cloned.1.call-done = bf16[4,512,768]{2,1,0:T(8,128)(2,1)} async-done(((bf16[4,128,768]{2,1,0:T(8,128)(2,1)}), bf16[4,512,768]{2,1,0:T(8,128)(2,1)}) %all-gather.12.cloned.1.call-update) | async-done | bytes 3145744 | tf_op jit(solution)/shard_map/all_gather | solution.py:191
  221.6 8.8 fusion.54
  230.4 46.1 %all-gather.16.cloned.1.call-done = bf16[2,768,768]{2,1,0:T(8,128)(2,1)} async-done(((bf16[2,24,768]{2,1,0:T(8,128)(2,1)}), bf16[2,768,768]{2,1,0:T(8,128)(2,1)}) %all-gather.16.cloned.1.call-update) | async-done | bytes 2359312 | tf_op jit(solution)/shard_map/all_gather | solution.py:169
  283.5 57.4 %all-gather.18.cloned.1.call-done = bf16[4,512,768]{2,1,0:T(8,128)(2,1)} async-done(((bf16[4,128,768]{2,1,0:T(8,128)(2,1)}), bf16[4,512,768]{2,1,0:T(8,128)(2,1)}) %all-gather.18.cloned.1.call-update) | async-done | bytes 3145744 | tf_op jit(solution)/shard_map/all_gather | solution.py:226
  345.6 59.0 %all-gather.20.cloned.1.call-done = bf16[4,512,768]{2,1,0:T(8,128)(2,1)} async-done(((bf16[4,128,768]{2,1,0:T(8,128)(2,1)}), bf16[4,512,768]{2,1,0:T(8,128)(2,1)}) %all-gather.20.cloned.1.call-update) | async-done | bytes 3145744 | tf_op jit(solution)/shard_map/all_gather | solution.py:225
  409.4 10.6 fusion.93
  430.5 45.7 %all-gather.22.cloned.1.call-done = bf16[2,768,2048]{2,1,0:T(8,128)(2,1)} async-done(((bf16[2,24,2048]{2,1,0:T(8,128)(2,1)}), bf16[2,768,2048]{2,1,0:T(8,128)(2,1)}) %all-gather.22.cloned.1.call-update) | async-done | bytes 6291472 | tf_op jit(solution)/shard_map/all_gather | solution.py:170
  485.9 51.3 %all-gather.24.cloned.1.call-done = bf16[2048,768]{1,0:T(8,128)(2,1)} async-done(((bf16[64,768]{1,0:T(8,128)(2,1)}), bf16[2048,768]{1,0:T(8,128)(2,1)}) %all-gather.24.cloned.1.call-update) | async-done | bytes 3145744 | tf_op jit(solution)/shard_map/all_gather | solution.py:171
  537.2 10.4 multiply_convert_fusion.2
  563.2 13.3 multiply_reduce_fusion.1
  630.1 13.2 multiply_reduce_fusion
  696.3 11.5 pad_maximum_fusion
  727.1 54.1 %reduce-scatter.14.cloned.1.call-done = bf16[4,128,768]{2,1,0:T(8,128)(2,1)} async-done(((bf16[4,512,768]{2,1,0:T(8,128)(2,1)}), bf16[4,128,768]{2,1,0:T(8,128)(2,1)}) %reduce-scatter.14.cloned.1.call-update) | async-done | bytes 786448 | tf_op jit(solution)/shard_map/reduce_scatter | solution.py:353
  784.7 59.0 %reduce-scatter.16.cloned.1.call-done = bf16[4,128,768]{2,1,0:T(8,128)(2,1)} async-done(((bf16[4,512,768]{2,1,0:T(8,128)(2,1)}), bf16[4,128,768]{2,1,0:T(8,128)(2,1)}) %reduce-scatter.16.cloned.1.call-update) | async-done | bytes 786448 | tf_op jit(solution)/shard_map/reduce_scatter | solution.py:356
  879.0 77.9 %reduce-scatter.20.cloned.1.call-done = f32[2,24,768]{2,1,0:T(8,128)} async-done(((f32[2,768,768]{2,1,0:T(8,128)}), f32[2,24,768]{2,1,0:T(8,128)}) %reduce-scatter.20.cloned.1.call-update) | async-done | bytes 147472 | tf_op jit(solution)/shard_map/reduce_scatter | solution.py:381
  965.4 112.2 %reduce-scatter.24.cloned.1.call-done = f32[64,768]{1,0:T(8,128)} async-done(((f32[2048,768]{1,0:T(8,128)}), f32[64,768]{1,0:T(8,128)}) %reduce-scatter.24.cloned.1.call-update) | async-done | bytes 196624 | tf_op jit(solution)/shard_map/reduce_scatter | solution.py:383
  1078.8 160.0 %reduce-scatter.22.cloned.1.call-done = f32[2,24,2048]{2,1,0:T(8,128)} async-done(((f32[2,768,2048]{2,1,0:T(8,128)}), f32[2,24,2048]{2,1,0:T(8,128)}) %reduce-scatter.22.cloned.1.call-update) | async-done | bytes 393232 | tf_op jit(solution)/shard_map/reduce_scatter | solution.py:382
  1240.0 169.8 %reduce-scatter.18.cloned.1.call-done = f32[6,24,768]{2,1,0:T(8,128)} async-done(((f32[6,768,768]{2,1,0:T(8,128)}), f32[6,24,768]{2,1,0:T(8,128)}) %reduce-scatter.18.cloned.1.call-update) | async-done | bytes 442384 | tf_op jit(solution)/shard_map/reduce_scatter | solution.py:380
  1410.9 41.3 %all-reduce.1 = (f32[3,768]{1,0:T(4,128)S(1)}, f32[32,12]{0,1:T(8,128)S(1)}, f32[6,768]{1,0:T(8,128)S(1)}, f32[2,768]{1,0:T(2,128)S(1)}, f32[2,2048]{1,0:T(2,128...) all-reduce(f32[3,768]{1,0:T(4,128)} %pad_maximum_fusion.2, ...), channel_id=8, replica_groups=mesh['wide'=8,'narrow'=4] {'wide','narrow'}, use_global_device_ids=true, to_apply=%region_21.22.clone | all-reduce | flops 13707 | bytes 109656
  (293 shorter events, 284.2 us)
Async XLA Ops:
  7.2 87.6 %copy-start = (bf16[4,128,768]{2,1,0:T(8,128)(2,1)S(1)}, bf16[4,128,768]{2,1,0:T(8,128)(2,1)}, u32[]{:S(2)}) copy-start(bf16[4,128,768]{2,1,0:T(8,128)(2,1)} %param.13) | copy-start | bytes 2359300
  7.2 80.0 %all-gather.10.cloned.1.call-start = ((), (), s32[]{:S(2)}) async-start(), calls=%async_computation.8 | async-start | bytes 7299072 | tf_op jit(solution)/shard_map/all_gather | solution.py:168
  9.7 160.2 %all-gather.14.cloned.1.call-start = ((), (), s32[]{:S(2)}) async-start(), calls=%async_computation.10 | async-start | bytes 3932160 | tf_op jit(solution)/shard_map/all_gather | solution.py:190
  90.4 126.5 %all-gather.12.cloned.1.call-start = ((), (), s32[]{:S(2)}) async-start(), calls=%async_computation.9 | async-start | bytes 3932160 | tf_op jit(solution)/shard_map/all_gather | solution.py:191
  93.5 183.1 %all-gather.16.cloned.1.call-start = ((), (), s32[]{:S(2)}) async-start(), calls=%async_computation.11 | async-start | bytes 2433024 | tf_op jit(solution)/shard_map/all_gather | solution.py:169
  94.7 246.2 %all-gather.18.cloned.1.call-start = ((), (), s32[]{:S(2)}) async-start(), calls=%async_computation.12 | async-start | bytes 3932160 | tf_op jit(solution)/shard_map/all_gather | solution.py:226
  97.8 306.7 %all-gather.20.cloned.1.call-start = ((), (), s32[]{:S(2)}) async-start(), calls=%async_computation.13 | async-start | bytes 3932160 | tf_op jit(solution)/shard_map/all_gather | solution.py:225
  101.0 375.1 %all-gather.22.cloned.1.call-start = ((), (), s32[]{:S(2)}) async-start(), calls=%async_computation.14 | async-start | bytes 6488064 | tf_op jit(solution)/shard_map/all_gather | solution.py:170
  102.4 434.8 %all-gather.24.cloned.1.call-start = ((), (), s32[]{:S(2)}) async-start(), calls=%async_computation.15 | async-start | bytes 3244032 | tf_op jit(solution)/shard_map/all_gather | solution.py:171
  103.7 613.7 %reduce-scatter.26.cloned.1.call-start = ((), (), s32[]{:S(2)}) async-start(), calls=%async_computation.22 | async-start | bytes 3932160
  283.5 125.8 %copy-start.18 = (bf16[4,128,768]{1,2,0:T(8,128)(2,1)}, bf16[4,128,768]{1,2,0:T(8,128)(2,1)S(1)}, u32[]{:S(2)}) copy-start(bf16[4,128,768]{1,2,0:T(8,128)(2,1)S(1)} %copy.145) | copy-start | bytes 2359300
  597.0 125.3 %reduce-scatter.28.cloned.1.call-start = ((), (), s32[]{:S(2)}) async-start(), calls=%async_computation.23 | async-start | bytes 3932160
  615.0 166.3 %reduce-scatter.14.cloned.1.call-start = ((), (), s32[]{:S(2)}) async-start(), calls=%async_computation.16 | async-start | bytes 3932160 | tf_op jit(solution)/shard_map/reduce_scatter | solution.py:353
  660.1 183.7 %reduce-scatter.16.cloned.1.call-start = ((), (), s32[]{:S(2)}) async-start(), calls=%async_computation.17 | async-start | bytes 3932160 | tf_op jit(solution)/shard_map/reduce_scatter | solution.py:356
  673.2 283.7 %reduce-scatter.20.cloned.1.call-start = ((), (), s32[]{:S(2)}) async-start(), calls=%async_computation.19 | async-start | bytes 4866048 | tf_op jit(solution)/shard_map/reduce_scatter | solution.py:381
  679.2 398.4 %reduce-scatter.24.cloned.1.call-start = ((), (), s32[]{:S(2)}) async-start(), calls=%async_computation.21 | async-start | bytes 6488064 | tf_op jit(solution)/shard_map/reduce_scatter | solution.py:383
  685.5 553.2 %reduce-scatter.22.cloned.1.call-start = ((), (), s32[]{:S(2)}) async-start(), calls=%async_computation.20 | async-start | bytes 12976128 | tf_op jit(solution)/shard_map/reduce_scatter | solution.py:382
  707.8 701.9 %reduce-scatter.18.cloned.1.call-start = ((), (), s32[]{:S(2)}) async-start(), calls=%async_computation.18 | async-start | bytes 14598144 | tf_op jit(solution)/shard_map/reduce_scatter | solution.py:380
  964.0 496.4 %copy-start.36 = (f32[2,24,2048]{2,1,0:T(8,128)S(1)}, f32[2,24,2048]{2,1,0:T(8,128)}, u32[]{:S(2)}) copy-start(f32[2,24,2048]{2,1,0:T(8,128)} %param.21) | copy-start | bytes 1179652
  965.4 496.0 %copy-start.38 = (f32[64,768]{1,0:T(8,128)S(1)}, f32[64,768]{1,0:T(8,128)}, u32[]{:S(2)}) copy-start(f32[64,768]{1,0:T(8,128)} %param.22) | copy-start | bytes 589828
  1077.6 383.8 %copy-start.39 = (f32[64,768]{1,0:T(8,128)S(1)}, f32[64,768]{1,0:T(8,128)}, u32[]{:S(2)}) copy-start(f32[64,768]{1,0:T(8,128)} %reduce-scatter.24.cloned.1.call-done) | copy-start | bytes 589828
  1078.8 384.0 %copy-start.60 = (f32[64]{0:T(128)}, f32[64]{0:T(128)S(1)}, u32[]{:S(2)}) copy-start(f32[64]{0:T(128)S(1)} %get-tuple-element.159) | copy-start | bytes 772
  1238.7 221.7 %copy-start.34 = (f32[2,24,2048]{2,1,0:T(8,128)S(1)}, f32[2,24,2048]{2,1,0:T(8,128)}, u32[]{:S(2)}) copy-start(f32[2,24,2048]{2,1,0:T(8,128)} %reduce-scatter.22.cloned.1.call-done) | copy-start | bytes 1179652
  1239.9 222.8 %copy-start.57 = (f32[2,24]{1,0:T(2,128)}, f32[2,24]{1,0:T(2,128)S(1)}, u32[]{:S(2)}) copy-start(f32[2,24]{1,0:T(2,128)S(1)} %get-tuple-element.142) | copy-start | bytes 580
  (63 other events, 721.5 us)
Sparse Core Ops, SparseCore 0:
  11.7 75.4 all-gather.9
  90.5 62.0 all-gather.13
  154.7 62.1 all-gather.11
  220.4 56.0 all-gather.15
  278.6 62.3 all-gather.17
  342.4 62.1 all-gather.19
  408.0 68.0 all-gather.21
  479.6 57.5 all-gather.23
  597.1 59.0 reduce-scatter.25
  658.4 60.2 reduce-scatter.27
  721.0 60.2 reduce-scatter.13
  783.4 60.2 reduce-scatter.15
  849.8 107.0 reduce-scatter.19
  963.9 113.6 reduce-scatter.23
  1084.1 154.6 reduce-scatter.21
  1246.2 163.5 reduce-scatter.17
where the time goes:
time: 1480 us; the launch traced here: 1470 us
  waiting for transfers between devices  927 us (63%)
  matrix products  218 us (15%)
  blocking collectives  129 us (9%)
  local copies, waits for them, and re-layouts  120 us (8%)
  other arithmetic  56.7 us (4%)
  between operations  16.7 us (1%)
    reduce_scatter x1, waiting for transfers between devices, body(): lax.psum_scatter(grad_in_part, ('wide', 'narrow'), scatter_dimension=1, t...  170 us
    reduce_scatter x1, waiting for transfers between devices, body(): lax.psum_scatter(grad_fin, ('wide', 'narrow'), scatter_dimension=1, tiled...  160 us
    reduce_scatter x1, waiting for transfers between devices, body(): lax.psum_scatter(grad_fout, ('wide', 'narrow'), scatter_dimension=0, tile...  112 us
    reduce_scatter x1, waiting for transfers between devices, body(): lax.psum_scatter(grad_out_part, ('wide', 'narrow'), scatter_dimension=1,...  77.9 us
    all_gather x1, blocking collectives, body(): lax.all_gather(gains.astype(jnp.bfloat16), ('wide', 'narrow'), axis=1, ti...  70.3 us
    reduce_scatter x1, waiting for transfers between devices, body(): lax.psum_scatter(ungrouped(self_dv).astype(jnp.bfloat16), 'narrow', scatt...  59 us
    all_gather x1, waiting for transfers between devices, body(): lax.all_gather(cross_key, 'narrow', axis=1, tiled=True)  59 us
    all_gather x1, waiting for transfers between devices, body(): lax.all_gather(cross_value, 'narrow', axis=1, tiled=True)  57.4 us
  transfers between devices with their start and end apart: 16, of which 13 were waited for; matrix products, arithmetic and copies ran while one was open for 21% of the time, Pallas kernels for 0%

commit v1 on v0

--- a/solution.py
+++ b/solution.py
@@ -149,7 +149,18 @@
     ff_out,
     bias_table,
 ):
-    rows_here, target_local, model_width = targets.shape
+    model_width = targets.shape[2]
+
+    def whole_rows(stacked):
+        return lax.all_to_all(stacked, "narrow", split_axis=0, concat_axis=1, tiled=True)
+
+    def back_rows(stacked):
+        return lax.all_to_all(stacked, "narrow", split_axis=1, concat_axis=0, tiled=True)
+
+    targets, memory, cotangent = whole_rows(targets), whole_rows(memory), whole_rows(cotangent)
+    target_segments, memory_segments = whole_rows(target_segments), whole_rows(memory_segments)
+    buckets = lax.all_gather(buckets, "narrow", axis=0, tiled=True)
+    rows_here, target_local, _ = targets.shape
     ff_width = ff_in.shape[2]
     head_count = bias_table.shape[1]
     bucket_count = bias_table.shape[0]
@@ -172,10 +183,8 @@
         lax.all_gather(gains.astype(jnp.bfloat16), ("wide", "narrow"), axis=1, tiled=True),
     )
     gain_full = gathered_gain.astype(jnp.float32)
-    query_start = lax.axis_index("narrow") * target_local
-    query_pos = query_start + jnp.arange(target_local, dtype=jnp.int32)
-    key_pos = jnp.arange(target_local * lax.axis_size("narrow"), dtype=jnp.int32)
-    causal = query_pos[:, None] >= key_pos[None, :]
+    query_pos = jnp.arange(target_local, dtype=jnp.int32)
+    causal = query_pos[:, None] >= query_pos[None, :]
     one_hot = (
         buckets[:, :, None] == jnp.arange(bucket_count, dtype=jnp.int32)[None, None, :]
     ).astype(jnp.float32)
@@ -186,11 +195,7 @@
     self_key = forward_mul(normed_attn, gathered_in[1]).astype(jnp.bfloat16)
     self_value = forward_mul(normed_attn, gathered_in[2]).astype(jnp.bfloat16)
     seg_target = target_segments.astype(jnp.bfloat16)
-    self_keys_all, self_values_all, target_segs_all = (
-        lax.all_gather(self_key, "narrow", axis=1, tiled=True),
-        lax.all_gather(self_value, "narrow", axis=1, tiled=True),
-        lax.all_gather(seg_target, "narrow", axis=1, tiled=True),
-    )
+    self_keys_all, self_values_all, target_segs_all = self_key, self_value, seg_target
 
     def self_mask(seg_query, seg_key):
         return causal[None] & (seg_query[:, :, None] == seg_key[:, None, :])
@@ -221,11 +226,7 @@
     seg_memory = memory_segments.astype(jnp.bfloat16)
     cross_key = forward_mul(memory, gathered_in[4]).astype(jnp.bfloat16)
     cross_value = forward_mul(memory, gathered_in[5]).astype(jnp.bfloat16)
-    cross_keys_all, cross_values_all, memory_segs_all = (
-        lax.all_gather(cross_key, "narrow", axis=1, tiled=True),
-        lax.all_gather(cross_value, "narrow", axis=1, tiled=True),
-        lax.all_gather(seg_memory, "narrow", axis=1, tiled=True),
-    )
+    cross_keys_all, cross_values_all, memory_segs_all = cross_key, cross_value, seg_memory
 
     def cross_forward(pieces):
         query_rows, key_rows, value_rows, seg_query, seg_key = pieces
@@ -294,16 +295,8 @@
             grouped(grad_mixed_cross),
         ),
     )
-    cross_key_sum, cross_value_sum = (
-        lax.psum_scatter(
-            ungrouped(cross_dk).astype(jnp.bfloat16), "narrow", scatter_dimension=1, tiled=True
-        ).astype(jnp.float32),
-        lax.psum_scatter(
-            ungrouped(cross_dv).astype(jnp.bfloat16), "narrow", scatter_dimension=1, tiled=True
-        ).astype(jnp.float32),
-    )
-    cross_key_low = cross_key_sum.astype(jnp.bfloat16)
-    cross_value_low = cross_value_sum.astype(jnp.bfloat16)
+    cross_key_low = ungrouped(cross_dk).astype(jnp.bfloat16)
+    cross_value_low = ungrouped(cross_dv).astype(jnp.bfloat16)
     cross_query_low = ungrouped(cross_dq).astype(jnp.bfloat16)
     grad_q_cross = weight_mul(normed_cross, cross_query_low)
     grad_k_cross = weight_mul(memory, cross_key_low)
@@ -349,16 +342,8 @@
             grouped(grad_mixed_self),
         ),
     )
-    self_key_sum, self_value_sum = (
-        lax.psum_scatter(
-            ungrouped(self_dk).astype(jnp.bfloat16), "narrow", scatter_dimension=1, tiled=True
-        ).astype(jnp.float32),
-        lax.psum_scatter(
-            ungrouped(self_dv).astype(jnp.bfloat16), "narrow", scatter_dimension=1, tiled=True
-        ).astype(jnp.float32),
-    )
-    self_key_low = self_key_sum.astype(jnp.bfloat16)
-    self_value_low = self_value_sum.astype(jnp.bfloat16)
+    self_key_low = ungrouped(self_dk).astype(jnp.bfloat16)
+    self_value_low = ungrouped(self_dv).astype(jnp.bfloat16)
     self_query_low = ungrouped(self_dq).astype(jnp.bfloat16)
     grad_q_self = weight_mul(normed_attn, self_query_low)
     grad_k_self = weight_mul(normed_attn, self_key_low)
@@ -376,11 +361,17 @@
     )
     grad_out_part = jnp.stack([grad_out_self, grad_out_cross])
     gain_part = jnp.stack([gain_grad_attn, gain_grad_cross, gain_grad_ffn])
+    def scattered(part, dim):
+        total = lax.psum_scatter(
+            part.astype(jnp.bfloat16), ("wide", "narrow"), scatter_dimension=dim, tiled=True
+        )
+        return total.astype(jnp.float32)
+
     sum_in, sum_out, sum_fin, sum_fout, sum_gain = (
-        lax.psum_scatter(grad_in_part, ("wide", "narrow"), scatter_dimension=1, tiled=True),
-        lax.psum_scatter(grad_out_part, ("wide", "narrow"), scatter_dimension=1, tiled=True),
-        lax.psum_scatter(grad_fin, ("wide", "narrow"), scatter_dimension=1, tiled=True),
-        lax.psum_scatter(grad_fout, ("wide", "narrow"), scatter_dimension=0, tiled=True),
+        scattered(grad_in_part, 1),
+        scattered(grad_out_part, 1),
+        scattered(grad_fin, 1),
+        scattered(grad_fout, 0),
         lax.psum_scatter(gain_part, ("wide", "narrow"), scatter_dimension=1, tiled=True),
     )
     in_rows, in_part = local_stats(sum_in)
@@ -428,9 +419,9 @@
     new_fout = adafactor_step(sum_fout, ff_out, fout_rows, fout_cols, fout_rms)
     new_table = adafactor_step(grad_table, bias_table, table_rows, table_cols, table_rms)
     return (
-        output,
-        grad_targets,
-        grad_memory,
+        back_rows(output),
+        back_rows(grad_targets),
+        back_rows(grad_memory),
         sum_in,
         sum_out,
         sum_gain,

time: 1480 us -> 899 us (0.61)
  waiting for transfers between devices: 927 us -> 358 us
  local copies, waits for them, and re-layouts: 120 us -> 77.4 us
  starting transfers between devices: 1.05 us -> 25.5 us
  matrix products: 218 us -> 202 us
  other arithmetic: 56.7 us -> 72.5 us
    reduce_scatter x6 -> x1, waiting for transfers between devices: 633 us -> 28.1 us  [scattered(): lax.psum_scatter(part.astype(jnp.bfloat16), ('wide', 'narrow'), scatter_d...]
    unnamed x18 -> x12, waiting for transfers between devices: 0.26 us -> 243 us
    all_gather x4 -> x1, waiting for transfers between devices: 146 us -> 0.01 us  [body(): buckets = lax.all_gather(buckets, 'narrow', axis=0, tiled=True)]
    all_gather x1, waiting for transfers between devices: 46.1 us -> 0.01 us  [body(): lax.all_gather(attn_out.astype(jnp.bfloat16), ('wide', 'narrow'), axis=1,...]
    eq x1 -> x0, local copies, waits for them, and re-layouts: 37.3 us -> none  [body(): buckets[:, :, None]]
    all_gather x1, waiting for transfers between devices: 45.7 us -> 20.1 us  [body(): lax.all_gather(ff_in.astype(jnp.bfloat16), ('wide', 'narrow'), axis=1, ti...]
    all_to_all x0 -> x6, starting transfers between devices: none -> 24.9 us  [the longest x3 12.8 us: back_rows(): lax.all_to_all(stacked, 'narrow', split_axis=1, concat_axis=0, tiled=True)]
    all_to_all x0 -> x2, blocking collectives: none -> 20.5 us  [whole_rows(): lax.all_to_all(stacked, 'narrow', split_axis=0, concat_axis=1, tiled=True)]
  transfers between devices with their start and end apart: 16 -> 15, of which waited for: 13 -> 8; matrix products, arithmetic and copies ran while one was open for 21% -> 31% of each run, Pallas kernels for 0% -> 0%
where the time goes in v1:
time: 899 us; the launch traced here: 890 us
  waiting for transfers between devices  358 us (40%)
  matrix products  202 us (22%)
  blocking collectives  138 us (15%)
  local copies, waits for them, and re-layouts  77.4 us (9%)
  other arithmetic  72.5 us (8%)
  starting transfers between devices  25.5 us (3%)
  between operations  16.9 us (2%)
    unnamed x12, waiting for transfers between devices  243 us
    all_gather x1, blocking collectives, body(): lax.all_gather(gains.astype(jnp.bfloat16), ('wide', 'narrow'), axis=1, ti...  76 us
    unnamed x203, local copies, waits for them, and re-layouts  58.4 us
    all_gather x1, waiting for transfers between devices, body(): lax.all_gather(ff_out.astype(jnp.bfloat16), ('wide', 'narrow'), axis=0, t...  50.9 us
    unnamed x1, blocking collectives  41.6 us
    dot_general x11, matrix products, back_mul(): jnp.einsum('rle,de->rld', left_rows, right_matrix, preferred_element_type...  38.3 us
    dot_general x11, matrix products, forward_mul(): jnp.einsum('rld,de->rle', left_rows, right_matrix, preferred_element_type...  36.6 us
    reduce_scatter x1, waiting for transfers between devices, scattered(): lax.psum_scatter(part.astype(jnp.bfloat16), ('wide', 'narrow'), scatter_d...  28.1 us
  transfers between devices with their start and end apart: 15, of which 8 were waited for; matrix products, arithmetic and copies ran while one was open for 31% of the time, Pallas kernels for 0%

profile of v1, /device:TPU:0, one launch (start us, length us, event | category | flops | bytes accessed | tf_op | source)
XLA Modules:
  0.0 890.2 jit_solution(7666518663841934874)
XLA Ops:
  15.2 11.8 %all_to_all.92 = s32[4,1,128]{2,1,0:T(1,128)S(1)} all-to-all(s32[4,1,128]{2,1,0:T(1,128)} %bitcast.355), channel_id=1, replica_groups=mesh['wide'=8,'narrow'=4] {'narrow'}, dimensions={0} | all-to-all | bytes 4096 | tf_op jit(solution)/shard_map/all_to_all | solution.py:155
  27.0 8.7 all_to_all.93
  40.5 76.0 %all-gather = bf16[32,24,3]{1,2,0:T(4,128)(2,1)S(1)} all-gather(bf16[1,24,3]{1,2,0:T(4,128)(2,1)S(1)} %convert_bitcast_fusion), channel_id=1, replica_groups=mesh['wide'=8,'narrow'=4] {'wide','narrow'}, dimensions={0}, use_global_device_ids=true | all-gather | bytes 4752 | tf_op jit(solution)/shard_map/all_gather | solution.py:183
  125.0 13.7 %fusion.3 = f32[512,512,12]{0,2,1:T(8,128)} fusion(s32[512,512]{0,1:T(8,128)S(1)} %copy.142, f32[32,12]{0,1:T(8,128)S(1)} %copy-done.57), kind=kOutput, calls=%fused_computation.4 | convolution fusion | flops 1216348160 | bytes 13633024 | tf_op jit(solution)/shard_map/qkb,bh->hqk/dot_general | solution.py:191
  163.5 17.1 %fusion.6 = f32[12,512,512]{1,2,0:T(8,128)} fusion(f32[512,512,12]{0,2,1:T(8,128)} %fusion.3, pred[512,512]{0,1:T(8,128)(4,1)S(1)} %get-tuple-element.258, bf16[512,12,64]{0,2,1:T(8,128)(2,1)S(1)} %bitcast.300, bf16[512,12,64]{0,2,1:T(8,128)(2,1)S(1)} %bitcast.296), kind=kOutput, calls=%fused_computation.8 | convolution fusion | flops 408944640 | bytes 27000832 | tf_op jit(solution)/shard_map/while/body/eval_jaxpr/gqhd,gkhd->ghqk/dot_general | solution.py:50
  184.0 15.1 %fusion.102 = (f32[12,512]{1,0:T(8,128)S(1)}, f32[12,512,512]{1,2,0:T(8,128)}) fusion(f32[12,512,512]{1,2,0:T(8,128)} %fusion.6), kind=kOutput, calls=%fused_computation.197 | output fusion | flops 6291967 | bytes 25190400 | tf_op jit(solution)/shard_map/while/body/eval_jaxpr/sub | solution.py:64
  199.1 12.2 %fusion.60 = bf16[12,64,512]{2,1,0:T(8,128)(2,1)} fusion(bf16[512,12,64]{0,2,1:T(8,128)(2,1)S(1)} %bitcast.333, f32[12,512]{1,0:T(8,128)S(1)} %get-tuple-element.259, f32[12,512,512]{1,2,0:T(8,128)} %fusion.6), kind=kOutput, calls=%fused_computation.117 | convolution fusion | flops 412490240 | bytes 14180352 | tf_op jit(solution)/shard_map/while/body/eval_jaxpr/ghqk,gkhd->gqhd/dot_general | solution.py:67
  218.8 7.5 fusion.103
  235.2 20.1 %all-gather.13.cloned.1.call-done = bf16[2,768,2048]{2,1,0:T(8,128)(2,1)} async-done(((bf16[2,24,2048]{2,1,0:T(8,128)(2,1)}), bf16[2,768,2048]{2,1,0:T(8,128)(2,1)}) %all-gather.13.cloned.1.call-update) | async-done | bytes 6291472 | tf_op jit(solution)/shard_map/all_gather | solution.py:181
  265.3 50.9 %all-gather.15.cloned.1.call-done = bf16[2048,768]{1,0:T(8,128)(2,1)} async-done(((bf16[64,768]{1,0:T(8,128)(2,1)}), bf16[2048,768]{1,0:T(8,128)(2,1)}) %all-gather.15.cloned.1.call-update) | async-done | bytes 3145744 | tf_op jit(solution)/shard_map/all_gather | solution.py:182
  316.2 10.3 %multiply_convert_fusion.2 = (bf16[512,2048]{1,0:T(8,128)(2,1)S(1)}, bf16[512,2048]{1,0:T(8,128)(2,1)S(1)}, bf16[512,2048]{1,0:T(8,128)(2,1)}) fusion(f32[512,2048]{1,0:T(8,128)} %fusion.30, f32[512,2048]{1,0:T(8,128)} %fusion.32, bf16[512,768]{1,0:T(8,128)(2,1)} %bitcast.33, bf16[2048,768]{1,0:T(8,128)(2,1)} %all-gather.15.cloned.1.call-done), kind=kOutput, calls=%fused_computation.33 | convolution fusion | flops 1642070016 | bytes 18612224 | tf_op jit(solution)/shard_map/rle,de->rld/dot_general | solution.py:35
  341.7 10.4 %multiply_reduce_fusion.1 = (f32[12,512]{1,0:T(8,128)S(1)}, f32[12,512,512]{1,2,0:T(8,128)}) fusion(f32[12,512,512]{1,2,0:T(8,128)} %get-tuple-element.264, f32[12,512]{1,0:T(8,128)S(1)} %get-tuple-element.263, bf16[512,12,64]{0,2,1:T(8,128)(2,1)S(1)} %bitcast.335, bf16[512,12,64]{0,2,1:T(8,128)(2,1)S(1)} %bitcast.338), kind=kOutput, calls=%fused_computation.12 | convolution fusion | flops 412084224 | bytes 26787840 | tf_op jit(solution)/shard_map/while/body/eval_jaxpr/gqhd,gkhd->ghqk/dot_general | solution.py:91
  354.6 7.1 multiply_convert_fusion.1
  386.4 13.5 %copy.179 = bf16[2,768,2048]{2,0,1:T(2,128)(2,1)S(1)} copy(bf16[2,768,2048]{2,1,0:T(8,128)(2,1)S(1)} %pad_maximum_fusion) | data formatting | bytes 12582912
  400.0 6.7 copy.186
  409.8 11.1 %fusion.63 = bf16[12,64,512]{2,1,0:T(8,128)(2,1)} fusion(bf16[512,12,64]{0,2,1:T(8,128)(2,1)S(1)} %bitcast.339, f32[12,512]{1,0:T(8,128)S(1)} %get-tuple-element.259, f32[12,512,512]{1,2,0:T(8,128)} %fusion.6), kind=kOutput, calls=%fused_computation.118 | convolution fusion | flops 412490240 | bytes 14180352 | tf_op jit(solution)/shard_map/while/body/eval_jaxpr/ghqk,gqhd->gkhd/dot_general | solution.py:97
  422.1 10.6 %multiply_reduce_fusion = (f32[12,512]{1,0:T(8,128)S(1)}, f32[12,512,512]{1,2,0:T(8,128)}) fusion(f32[12,512,512]{1,2,0:T(8,128)} %get-tuple-element.260, f32[12,512]{1,0:T(8,128)S(1)} %get-tuple-element.259, bf16[512,12,64]{0,2,1:T(8,128)(2,1)} %bitcast.340, bf16[512,12,64]{0,2,1:T(8,128)(2,1)S(1)} %bitcast.334), kind=kOutput, calls=%fused_computation.10 | convolution fusion | flops 412084224 | bytes 26787840 | tf_op jit(solution)/shard_map/while/body/eval_jaxpr/gqhd,gkhd->ghqk/dot_general | solution.py:91
  434.3 7.0 multiply_convert_fusion
  531.1 12.1 %fusion.76 = f32[32,12]{0,1:T(8,128)S(1)} fusion(bf16[12,512,512]{1,2,0:T(8,128)(2,1)} %copy-done, s32[512,512]{0,1:T(8,128)S(1)} %copy-done.16), kind=kOutput, calls=%fused_computation.136 | convolution fusion | flops 209715200 | bytes 7341568 | tf_op jit(solution)/shard_map/qkb,hqk->bh/dot_general | solution.py:358
  548.4 6.6 all-to-all-done.6
  559.6 28.1 %reduce-scatter.12.cloned.1.call-done = bf16[64,768]{1,0:T(8,128)(2,1)} async-done(((bf16[2048,768]{1,0:T(8,128)(2,1)}), bf16[64,768]{1,0:T(8,128)(2,1)}) %reduce-scatter.12.cloned.1.call-update) | async-done | bytes 98320 | tf_op jit(solution)/shard_map/reduce_scatter | solution.py:365
  588.7 119.1 %reduce-scatter.18.cloned.1.call-done = bf16[24,4096]{1,0:T(8,128)(2,1)} async-done(((bf16[768,4096]{1,0:T(8,128)(2,1)}), bf16[24,4096]{1,0:T(8,128)(2,1)}) %reduce-scatter.18.cloned.1.call-update) | async-done | bytes 196624
  709.2 122.8 %reduce-scatter.14.cloned.1.call-done = bf16[24,4608]{1,0:T(8,128)(2,1)} async-done(((bf16[768,4608]{1,0:T(8,128)(2,1)}), bf16[24,4608]{1,0:T(8,128)(2,1)}) %reduce-scatter.14.cloned.1.call-update) | async-done | bytes 221200
  833.4 41.6 %all-reduce.1 = (f32[3,768]{1,0:T(4,128)S(1)}, f32[32,12]{0,1:T(8,128)S(1)}, f32[6,768]{1,0:T(8,128)S(1)}, f32[2,768]{1,0:T(2,128)S(1)}, f32[2,2048]{1,0:T(2,128...) all-reduce(f32[3,768]{1,0:T(4,128)S(1)} %pad_maximum_fusion.2, ...), channel_id=4, replica_groups=mesh['wide'=8,'narrow'=4] {'wide','narrow'}, use_global_device_ids=true, to_apply=%region_17.18.clone | all-reduce | flops 13707 | bytes 109656
  (338 shorter events, 233.1 us)
Async XLA Ops:
  7.2 116.2 %all-gather.9.cloned.1.call-start = ((), (), s32[]{:S(2)}) async-start(), calls=%async_computation.13 | async-start | bytes 1310720 | tf_op jit(solution)/shard_map/all_gather | solution.py:162
  7.9 130.8 %all-gather.7.cloned.1.call-start = ((), (), s32[]{:S(2)}) async-start(), calls=%async_computation.12 | async-start | bytes 7299072 | tf_op jit(solution)/shard_map/all_gather | solution.py:179
  10.4 200.8 %all-gather.11.cloned.1.call-start = ((), (), s32[]{:S(2)}) async-start(), calls=%async_computation.14 | async-start | bytes 2433024 | tf_op jit(solution)/shard_map/all_gather | solution.py:180
  12.7 242.7 %all-gather.13.cloned.1.call-start = ((), (), s32[]{:S(2)}) async-start(), calls=%async_computation.15 | async-start | bytes 6488064 | tf_op jit(solution)/shard_map/all_gather | solution.py:181
  35.7 82.3 %all-to-all-start = ((bf16[4,128,768]{2,1,0:T(8,128)(2,1)}), bf16[4,128,768]{2,1,0:T(8,128)(2,1)S(1)}, u32[]{:S(2)}, u32[]{:S(2)}) async-start(bf16[4,128,768]{2,1,0:T(8,128)(2,1)} %param.12), calls=%async_computation | async-start | bytes 1572864 | tf_op jit(solution)/shard_map/all_to_all | solution.py:155
  39.2 277.0 %all-gather.15.cloned.1.call-start = ((), (), s32[]{:S(2)}) async-start(), calls=%async_computation.16 | async-start | bytes 3244032 | tf_op jit(solution)/shard_map/all_gather | solution.py:182
  118.0 35.8 %all-to-all-start.2 = ((bf16[4,128,768]{2,1,0:T(8,128)(2,1)}), bf16[4,128,768]{2,1,0:T(8,128)(2,1)S(1)}, u32[]{:S(2)}, u32[]{:S(2)}) async-start(bf16[4,128,768]{2,1,0:T(8,128)(2,1)} %param.13), calls=%async_computation.2 | async-start | bytes 1572864 | tf_op jit(solution)/shard_map/all_to_all | solution.py:155
  153.8 111.5 %all-to-all-start.5 = ((bf16[4,128,768]{2,1,0:T(8,128)(2,1)}), bf16[4,128,768]{2,1,0:T(8,128)(2,1)}, u32[]{:S(2)}, u32[]{:S(2)}) async-start(bf16[4,128,768]{2,1,0:T(8,128)(2,1)} %param.14), calls=%async_computation.5 | async-start | bytes 1572864 | tf_op jit(solution)/shard_map/all_to_all | solution.py:155
  158.8 399.7 %reduce-scatter.16.cloned.1.call-start = ((), (), s32[]{:S(2)}) async-start(), calls=%async_computation.19 | async-start | bytes 2433024
  373.9 213.8 %reduce-scatter.12.cloned.1.call-start = ((), (), s32[]{:S(2)}) async-start(), calls=%async_computation.17 | async-start | bytes 3244032 | tf_op jit(solution)/shard_map/reduce_scatter | solution.py:365
  379.2 328.6 %reduce-scatter.18.cloned.1.call-start = ((), (), s32[]{:S(2)}) async-start(), calls=%async_computation.20 | async-start | bytes 6488064
  421.0 411.0 %reduce-scatter.14.cloned.1.call-start = ((), (), s32[]{:S(2)}) async-start(), calls=%async_computation.18 | async-start | bytes 7299072
  476.5 24.4 %all-to-all-start.4 = ((bf16[4,2,49152]{2,1,0:T(2,128)(2,1)}), bf16[4,2,49152]{2,1,0:T(2,128)(2,1)S(1)}, u32[]{:S(2)}, u32[]{:S(2)}) async-start(bf16[4,2,49152]{2,1,0:T(2,128)(2,1)} %reshape.1092), calls=%async_computation.4 | async-start | bytes 1572864 | tf_op jit(solution)/shard_map/all_to_all | solution.py:158
  500.9 24.4 %all-to-all-start.7 = ((bf16[4,2,49152]{2,1,0:T(2,128)(2,1)}), bf16[4,2,49152]{2,1,0:T(2,128)(2,1)}, u32[]{:S(2)}, u32[]{:S(2)}) async-start(bf16[4,2,49152]{2,1,0:T(2,128)(2,1)} %reshape.1096), calls=%async_computation.7 | async-start | bytes 1572864 | tf_op jit(solution)/shard_map/all_to_all | solution.py:158
  525.3 29.7 %all-to-all-start.6 = ((bf16[4,2,49152]{2,1,0:T(2,128)(2,1)}), bf16[4,2,49152]{2,1,0:T(2,128)(2,1)}, u32[]{:S(2)}, u32[]{:S(2)}) async-start(bf16[4,2,49152]{2,1,0:T(2,128)(2,1)} %reshape.1094), calls=%async_computation.6 | async-start | bytes 1572864 | tf_op jit(solution)/shard_map/all_to_all | solution.py:158
  557.5 275.9 %copy-start.70 = (f32[6]{0:T(128)S(1)}, f32[6]{0:T(128)}, u32[]{:S(2)}) copy-start(f32[6]{0:T(128)} %get-tuple-element.247) | copy-start | bytes 76
  557.5 321.8 %copy-start.50 = (f32[2,24,768]{2,1,0:T(8,128)S(1)}, f32[2,24,768]{2,1,0:T(8,128)}, u32[]{:S(2)}) copy-start(f32[2,24,768]{2,1,0:T(8,128)} %param.19) | copy-start | bytes 442372
  558.5 321.6 %copy-start.42 = (f32[64,768]{1,0:T(8,128)S(1)}, f32[64,768]{1,0:T(8,128)}, u32[]{:S(2)}) copy-start(f32[64,768]{1,0:T(8,128)} %param.22) | copy-start | bytes 589828
  558.5 323.0 %copy-start.26 = (f32[2,24,2048]{2,1,0:T(8,128)S(1)}, f32[2,24,2048]{2,1,0:T(8,128)}, u32[]{:S(2)}) copy-start(f32[2,24,2048]{2,1,0:T(8,128)} %param.21) | copy-start | bytes 1179652
  559.6 322.9 %copy-start.51 = (f32[2,24,768]{2,1,0:T(8,128)}, f32[2,24,768]{2,1,0:T(8,128)S(1)}, u32[]{:S(2)}) copy-start(f32[2,24,768]{2,1,0:T(8,128)S(1)} %get-tuple-element.242) | copy-start | bytes 442372
  559.6 322.9 %copy-start.67 = (f32[2,24]{1,0:T(2,128)}, f32[2,24]{1,0:T(2,128)S(1)}, u32[]{:S(2)}) copy-start(f32[2,24]{1,0:T(2,128)S(1)} %get-tuple-element.223) | copy-start | bytes 580
  588.7 293.8 %copy-start.43 = (f32[64,768]{1,0:T(8,128)}, f32[64,768]{1,0:T(8,128)S(1)}, u32[]{:S(2)}) copy-start(f32[64,768]{1,0:T(8,128)S(1)} %get-tuple-element.240) | copy-start | bytes 589828
  588.7 293.8 %copy-start.74 = (f32[64]{0:T(128)}, f32[64]{0:T(128)S(1)}, u32[]{:S(2)}) copy-start(f32[64]{0:T(128)S(1)} %get-tuple-element.221) | copy-start | bytes 772
  588.7 293.7 %copy-start.23 = (f32[6,24,768]{2,1,0:T(8,128)S(1)}, f32[6,24,768]{2,1,0:T(8,128)}, u32[]{:S(2)}) copy-start(f32[6,24,768]{2,1,0:T(8,128)} %param.18) | copy-start | bytes 1327108
  (83 other events, 1769.4 us)
Sparse Core Ops, SparseCore 0:
  9.6 30.7 all-gather.8
  44.0 73.3 all-gather.6
  121.1 61.5 all-gather.10
  186.0 69.2 all-gather.12
  258.6 57.5 all-gather.14
  374.0 97.9 reduce-scatter.15
  478.3 109.3 reduce-scatter.11
  594.2 113.6 reduce-scatter.17
  713.6 118.3 reduce-scatter.13

commit v2 on v1

v2 whole, which is shorter than its diff:
```python
import functools

import jax
import jax.numpy as jnp
from jax import lax
from jax.experimental import pallas as pl
from jax.experimental.pallas import tpu as pltpu
from jax.sharding import PartitionSpec as P

bf16, f32 = jnp.bfloat16, jnp.float32
BOTH = ("wide", "narrow")
NEG = -1e9
TILE = 256
MIB = 1 << 20


def dot_nn(left, right):
    return lax.dot_general(left, right, (((1,), (0,)), ((), ())), preferred_element_type=f32)


def dot_nt(left, right):
    return lax.dot_general(left, right, (((1,), (1,)), ((), ())), preferred_element_type=f32)


def unit_of(values):
    inv_rms = lax.rsqrt(jnp.mean(values * values, axis=-1, keepdims=True) + 1e-06)
    return values * inv_rms, inv_rms


def norm_back(incoming, values, gain_row):
    unit, inv_rms = unit_of(values)
    scaled = incoming * gain_row
    inner = jnp.mean(scaled * unit, axis=-1, keepdims=True)
    return inv_rms * (scaled - unit * inner), jnp.sum(incoming * unit, axis=0, keepdims=True)


def tiles_of(width):
    return [(start, min(TILE, width - start)) for start in range(0, width, TILE)]


def project(left, w_ref, index, store):
    for start, size in tiles_of(w_ref.shape[2]):
        store(start, size, dot_nn(left, w_ref[index, :, start : start + size]))


def half_lanes(second):
    lane = lax.broadcasted_iota(jnp.int32, (1, 128), 1)
    return ((lane >= 64) == bool(second)).astype(bf16)


def biased(table_row, index):
    spread = jnp.broadcast_to(table_row, (index.shape[0], 128))
    return jnp.concatenate(
        [
            jnp.take_along_axis(
                spread, index[:, at : at + 128], axis=1, mode="promise_in_bounds"
            )
            for at in range(0, index.shape[1], 128)
        ],
        axis=1,
    )


def query_blocks(keys, queries, causal):
    return [
        (at, min(keys, at + TILE) if causal else keys) for at in range(0, queries, TILE)
    ]


def attend(qkv_ref, extra_ref, table_ref, o_ref, peak_ref, inv_ref, ot_ref):
    causal = table_ref is not None
    keys = qkv_ref.shape[1]

    def pair(at_pair, carry):
        lanes = pl.ds(pl.multiple_of(at_pair * 128, 128), 128)
        query, key, value = (qkv_ref[i, :, lanes] for i in range(3))
        value_t = value.T
        for second in range(2):
            head = at_pair * 2 + second
            key_half = key * half_lanes(second)
            for start, last in query_blocks(keys, keys, causal):
                part = slice(start, start + TILE)
                scores = dot_nt(key_half[:last], query[part])
                if causal:
                    scores += biased(table_ref[pl.ds(head, 1), :], extra_ref[:last, part])
                else:
                    scores += extra_ref[:last, part]
                peak = jnp.max(scores, axis=0, keepdims=True)
                grown = jnp.exp(scores - peak)
                inverse = 1.0 / jnp.sum(grown, axis=0, keepdims=True)
                mixed = dot_nn(value_t[second * 64 : second * 64 + 64, :last], grown.astype(bf16))
                ot_ref[second * 64 : second * 64 + 64, part] = mixed * inverse
                peak_ref[head, :, part] = peak
                inv_ref[head, :, part] = inverse
        o_ref[:, lanes] = ot_ref[...].T.astype(bf16)
        return carry

    lax.fori_loop(0, qkv_ref.shape[2] // 128, pair, 0)


def attend_back(
    qkv_ref, extra_ref, table_ref, do_ref, dsum_ref, peak_ref, inv_ref,
    dqkv_ref, p_ref, ds_ref, dqt_ref, ds_out,
):
    causal = table_ref is not None
    keys = qkv_ref.shape[1]
    first_half = lax.broadcasted_iota(jnp.int32, (1, 128), 1) < 64

    def pair(at_pair, carry):
        lanes = pl.ds(pl.multiple_of(at_pair * 128, 128), 128)
        query, key, value = (qkv_ref[i, :, lanes] for i in range(3))
        grad = do_ref[:, lanes]
        key_t = key.T
        for second in range(2):
            head = at_pair * 2 + second
            half = half_lanes(second)
            key_half, value_half = key * half, value * half
            for start, last in query_blocks(keys, keys, causal):
                part = slice(start, start + TILE)
                scores = dot_nt(key_half[:last], query[part])
                if causal:
                    scores += biased(table_ref[pl.ds(head, 1), :], extra_ref[:last, part])
                else:
                    scores += extra_ref[:last, part]
                weights = jnp.exp(scores - peak_ref[head, :, part]) * inv_ref[head, :, part]
                grad_weights = dot_nt(value_half[:last], grad[part])
                grad_scores = (weights * (grad_weights - dsum_ref[head, :, part])).astype(bf16)
                p_ref[:last, part] = weights.astype(bf16)
                ds_ref[:last, part] = grad_scores
                dqt_ref[second * 64 : second * 64 + 64, part] = dot_nn(
                    key_t[second * 64 : second * 64 + 64, :last], grad_scores
                )
            for start in range(0, keys, TILE):
                rows = slice(start, start + TILE)
                begin = start if causal else 0
                d_value = dot_nn(p_ref[rows, begin:], grad[begin:]).astype(bf16)
                d_key = dot_nn(ds_ref[rows, begin:], query[begin:]).astype(bf16)
                if second:
                    d_value = jnp.where(first_half, dqkv_ref[2, rows, lanes], d_value)
                    d_key = jnp.where(first_half, dqkv_ref[1, rows, lanes], d_key)
                dqkv_ref[2, rows, lanes] = d_value
                dqkv_ref[1, rows, lanes] = d_key
            if ds_out is not None:
                ds_out[head] = ds_ref[...]
        dqkv_ref[0, :, lanes] = dqt_ref[...].T.astype(bf16)
        return carry

    if causal:
        p_ref[...] = jnp.zeros_like(p_ref)
        ds_ref[...] = jnp.zeros_like(ds_ref)
    lax.fori_loop(0, qkv_ref.shape[2] // 128, pair, 0)


def head_sums(grad, mixed, dsum_ref):
    heads = dsum_ref.shape[0]
    product = grad.astype(f32) * mixed.astype(f32)
    width = product.shape[1]
    pick = (
        lax.broadcasted_iota(jnp.int32, (16, width), 1) // (width // heads)
        == lax.broadcasted_iota(jnp.int32, (16, width), 0)
    ).astype(f32)
    sums = lax.dot_general(
        pick, product, (((1,), (1,)), ((), ())),
        preferred_element_type=f32, precision=lax.Precision.HIGHEST,
    )
    for head in range(heads):
        dsum_ref[head] = sums[head : head + 1]


def fold_rows(core, turned, turned_ref, out_ref, fold):
    if not fold:
        out_ref[...] = turned
        return
    turned_ref[...] = turned
    total = turned.shape[0]
    size = total // 8
    for group in range(4):
        for place, which in ((0, core), (1, 1 - core)):
            begin = pl.multiple_of(group * 2 * size + which * size, 16)
            to = place * (total // 2) + group * size
            out_ref[to : to + size, :] = turned_ref[pl.ds(begin, size), :]


def weight_grad(left_ref, right, keep_ref, send_ref, index):
    half = left_ref.shape[0] // 2
    for start, size in tiles_of(right.shape[1]):
        product = dot_nn(left_ref[...], right[:, start : start + size]).astype(bf16)
        keep_ref[index, :, start : start + size] = product[:half]
        send_ref[index, :, start : start + size] = product[half:]


def start_weights(place, pieces, target_ref, sems, only=None):
    rows = target_ref.shape[1] // len(pieces)
    copies = []
    for d, piece in enumerate(pieces):
        begin = pl.multiple_of((place ^ d) * rows, rows) if len(pieces) > 1 else 0
        source = piece if only is None else piece.at[only]
        copies.append(
            pltpu.make_async_copy(source, target_ref.at[:, pl.ds(begin, rows), :], sems.at[d])
        )
        copies[-1].start()
    return copies


def join_rows(place, pieces, target_ref):
    rows = pieces[0].shape[0]
    for d, piece in enumerate(pieces):
        target_ref[pl.ds(pl.multiple_of((place ^ d) * rows, 16), rows), :] = piece[...]


def split_rows(place, source_ref, pieces):
    rows = pieces[0].shape[0]
    for d, piece in enumerate(pieces):
        piece[...] = source_ref[pl.ds(pl.multiple_of((place ^ d) * rows, 16), rows), :].astype(
            piece.dtype
        )


def first_kernel(at_ref, *refs, pieces, narrow, chunk):
    x_refs, refs = refs[:narrow], refs[narrow:]
    w_refs, refs = refs[:pieces], refs[pieces:]
    (extra_ref, table_ref, g_ref, x_ref, h_ref, qkv_ref, o_ref, peak_ref, inv_ref,
     ot_ref, w_ref, sems) = refs
    copies = start_weights(at_ref[3], w_refs, w_ref, sems)
    join_rows(at_ref[2], x_refs, x_ref)
    width = x_ref.shape[1]
    pick = (
        lax.broadcasted_iota(jnp.int32, (8, width), 1) % chunk
        == lax.broadcasted_iota(jnp.int32, (8, width), 0)
    ).astype(bf16)
    unit, _ = unit_of(x_ref[...].astype(f32))
    for copy in copies:
        copy.wait()
    gains = dot_nn(pick, w_ref[3])
    g_ref[...] = gains
    h_ref[...] = (unit * gains[0:1]).astype(bf16)
    for i in range(3):
        def store(start, size, product, i=i):
            qkv_ref[i, :, start : start + size] = product.astype(bf16)

        project(h_ref[...], w_ref, i, store)
    attend(qkv_ref, extra_ref, table_ref, o_ref, peak_ref, inv_ref, ot_ref)


def second_kernel(at_ref, *refs, pieces, narrow):
    m_refs, refs = refs[:narrow], refs[narrow:]
    w_refs, refs = refs[:pieces], refs[pieces:]
    (x_ref, o1_ref, extra_ref, g_ref, m_ref, x1_ref, h_ref, qkv_ref, o_ref, x2_ref, h3_ref,
     peak_ref, inv_ref, ot_ref, w_ref, sems) = refs
    copies = start_weights(at_ref[3], w_refs, w_ref, sems)
    join_rows(at_ref[2], m_refs, m_ref)
    for copy in copies:
        copy.wait()

    def store_x1(start, size, product):
        part = slice(start, start + size)
        x1_ref[:, part] = x_ref[:, part].astype(f32) + product

    project(o1_ref[...], w_ref, 0, store_x1)
    unit, _ = unit_of(x1_ref[...])
    h_ref[...] = (unit * g_ref[1:2, :]).astype(bf16)
    for i in range(3):
        def store(start, size, product, i=i):
            qkv_ref[i, :, start : start + size] = product.astype(bf16)

        project(m_ref[...] if i else h_ref[...], w_ref, i + 1, store)
    attend(qkv_ref, extra_ref, None, o_ref, peak_ref, inv_ref, ot_ref)

    def store_x2(start, size, product):
        part = slice(start, start + size)
        x2_ref[:, part] = x1_ref[:, part] + product

    project(o_ref[...], w_ref, 4, store_x2)
    unit, _ = unit_of(x2_ref[...])
    h3_ref[...] = (unit * g_ref[2:3, :]).astype(bf16)


def prepare_kernel(at_ref, *refs, narrow, bucket_count):
    in_refs, (index_ref, mask_ref, seg_ref, near_ref) = refs[:narrow], refs[narrow:]
    local = in_refs[0].shape[0] - 16
    for d, ref in enumerate(in_refs):
        lanes = pl.ds(pl.multiple_of((at_ref[2] ^ d) * local, 128), local)
        near_ref[:, lanes] = ref[:local, :].astype(f32).T
        tail = ref[local:, :].astype(f32)
        seg_ref[0:8, lanes] = jnp.broadcast_to(tail[0:1, :local], (8, local))
        seg_ref[8:16, lanes] = jnp.broadcast_to(tail[0:1, local : 2 * local], (8, local))
    seg = seg_ref[...]
    seg_t = seg.T
    tokens = near_ref.shape[0]
    key = lax.broadcasted_iota(jnp.int32, (tokens, tokens), 0)
    query = lax.broadcasted_iota(jnp.int32, (tokens, tokens), 1)
    allowed = (key <= query) & (seg_t[:, 0:1] == seg[0:1, :])
    index_ref[...] = jnp.where(allowed, near_ref[...], float(bucket_count)).astype(jnp.int32)
    mask_ref[...] = jnp.where(seg_t[:, 8:9] == seg[0:1, :], 0.0, NEG)


def order_kernel(at_ref, *refs):
    pieces, out_ref = refs[:-1], refs[-1]
    for d, piece in enumerate(pieces):
        if piece.ndim == 2:
            out_ref[at_ref[2] ^ d] = piece[...]
        else:
            out_ref[:, at_ref[2] ^ d] = piece[...]


def spread_kernel(at_ref, *refs, count):
    for i in range(count):
        keep_ref, recv_ref = refs[2 * i : 2 * i + 2]
        rows = keep_ref.shape[1] // 4
        for d in range(4):
            part = pl.ds(pl.multiple_of((at_ref[1] ^ d) * rows, 16), rows)
            out_ref = refs[2 * count + 4 * i + d]
            total = keep_ref[:, part, :].astype(f32) + recv_ref[:, part, :].astype(f32)
            out_ref[...] = total.astype(out_ref.dtype)


def narrow_kernel(at_ref, *refs, count, narrow):
    outs, scratch = refs[4 * count : (4 + narrow) * count], refs[(4 + narrow) * count :]
    for i in range(count):
        first, second, third, fourth = (ref[...].astype(f32) for ref in refs[4 * i : 4 * i + 4])
        scratch[i][...] = (first + second) + (third + fourth)
        rows = scratch[i].shape[1] // narrow
        for d in range(narrow):
            part = pl.ds(pl.multiple_of((at_ref[2] ^ d) * rows, 8), rows)
            out_ref = outs[narrow * i + d]
            out_ref[...] = scratch[i][:, part, :].astype(out_ref.dtype)


def total_kernel(*refs, count, narrow):
    for i in range(count):
        total = refs[narrow * i][...]
        for ref in refs[narrow * i + 1 : narrow * i + narrow]:
            total = total + ref[...].astype(f32)
        total_ref, rows_ref, cols_ref = refs[narrow * count + 3 * i : narrow * count + 3 * i + 3]
        total_ref[...] = total
        squares = total * total + 1e-30
        rows_ref[...] = jnp.sum(squares, axis=-1, keepdims=True)
        cols_ref[...] = jnp.sum(squares, axis=1, keepdims=True)


def ffn_kernel(at_ref, *refs, fold, narrow):
    c_refs, refs = refs[:narrow], refs[narrow:]
    (x2_ref, h_ref, g_ref, gate_ref, up_ref, wout_ref), refs = refs[:6], refs[6:]
    out_refs, refs = refs[:narrow], refs[narrow:]
    (dx_ref, dg_ref, kin_ref, sin_ref, kout_ref, sout_ref, acc_ref, dh_ref, turned_ref, ht_ref,
     gout_ref, c_ref) = refs
    step, steps = pl.program_id(0), pl.num_programs(0)
    core = at_ref[0]

    @pl.when(step == 0)
    def _():
        join_rows(at_ref[2], c_refs, c_ref)
        acc_ref[...] = x2_ref[...]
        dh_ref[...] = jnp.zeros_like(dh_ref)
        fold_rows(core, h_ref[...].T, turned_ref, ht_ref, fold)

    hidden_in, cot = h_ref[...], c_ref[...]
    for block in range(gate_ref.shape[0]):
        size = gate_ref.shape[2]
        part = slice(block * size, (block + 1) * size)
        gate = dot_nn(hidden_in, gate_ref[block])
        up = dot_nn(hidden_in, up_ref[block])
        square = gate * gate
        bent = jnp.tanh(0.7978845608028654 * (gate + 0.044715 * square * gate))
        plus = 0.5 * (1.0 + bent)
        act = gate * plus
        slope = plus + 0.5 * gate * (1.0 - bent * bent) * (
            0.7978845608028654 + (3 * 0.044715 * 0.7978845608028654) * square
        )
        hidden = (act * up).astype(bf16)
        down = jnp.concatenate([wout_ref[i, part, :] for i in range(wout_ref.shape[0])], axis=1)
        acc_ref[...] += dot_nn(hidden, down)
        grad = dot_nt(cot, down)
        d_gate = (grad * up * slope).astype(bf16)
        d_up = (grad * act).astype(bf16)
        dh_ref[...] += dot_nt(d_gate, gate_ref[block]) + dot_nt(d_up, up_ref[block])
        half = ht_ref.shape[0] // 2
        for index, right in ((0, d_gate), (1, d_up)):
            product = dot_nn(ht_ref[...], right).astype(bf16)
            kin_ref[index, :, part] = product[:half]
            sin_ref[index, :, part] = product[half:]
        gout_ref[part, :] = dot_nn(hidden.T, cot).astype(bf16)
    rows = gout_ref.shape[0] // 2
    kept = pl.multiple_of(core * rows, 16) if fold else 0
    sent = pl.multiple_of((1 - core) * rows, 16) if fold else rows
    kout_ref[...] = gout_ref[pl.ds(kept, rows), :]
    sout_ref[...] = gout_ref[pl.ds(sent, rows), :]

    @pl.when(step == steps - 1)
    def _():
        split_rows(at_ref[2], acc_ref, out_refs)
        back, d_gain = norm_back(dh_ref[...], x2_ref[...], g_ref[2:3, :])
        dx_ref[...] = cot.astype(f32) + back
        dg_ref[...] = d_gain


def cross_back_kernel(at_ref, *refs, pieces, narrow, fold):
    w_refs, refs = refs[:pieces], refs[pieces:]
    (dx2_ref, o_ref, h_ref, m_ref, x1_ref, o1_ref, qkv_ref, extra_ref, g_ref, peak_ref,
     inv_ref), refs = refs[:11], refs[11:]
    gm_refs, refs = refs[:narrow], refs[narrow:]
    (dx1_ref, dg_ref, keep_ref, send_ref, do_ref, dqkv_ref, dsum_ref, p_ref, ds_ref, dqt_ref,
     turned_ref, left_ref, gm_ref, w_ref, sems) = refs
    core = at_ref[0]
    copies = start_weights(at_ref[3], w_refs, w_ref, sems)
    branch = dx2_ref[...].astype(bf16)
    for copy in copies:
        copy.wait()
    for start, size in tiles_of(o_ref.shape[1]):
        do_ref[:, start : start + size] = dot_nt(
            branch, w_ref[4, start : start + size, :]
        ).astype(bf16)
    head_sums(do_ref[...], o_ref[...], dsum_ref)
    fold_rows(core, o_ref[...].T, turned_ref, left_ref, fold)
    weight_grad(left_ref, branch, keep_ref, send_ref, 4)
    attend_back(qkv_ref, extra_ref, None, do_ref, dsum_ref, peak_ref, inv_ref, dqkv_ref, p_ref,
                ds_ref, dqt_ref, None)
    fold_rows(core, h_ref[...].T, turned_ref, left_ref, fold)
    weight_grad(left_ref, dqkv_ref[0], keep_ref, send_ref, 1)
    fold_rows(core, m_ref[...].T, turned_ref, left_ref, fold)
    for i in (1, 2):
        weight_grad(left_ref, dqkv_ref[i], keep_ref, send_ref, i + 1)
    for start, size in tiles_of(o_ref.shape[1]):
        rows = slice(start, start + size)
        gm_ref[:, rows] = (
            dot_nt(dqkv_ref[1], w_ref[2, rows, :]) + dot_nt(dqkv_ref[2], w_ref[3, rows, :])
        ).astype(bf16)
        dx1_ref[:, rows] = dot_nt(dqkv_ref[0], w_ref[1, rows, :])
    split_rows(at_ref[2], gm_ref, gm_refs)
    back, d_gain = norm_back(dx1_ref[...], x1_ref[...], g_ref[1:2, :])
    d_x1 = dx2_ref[...] + back
    dx1_ref[...] = d_x1
    dg_ref[...] = d_gain
    fold_rows(core, o1_ref[...].T, turned_ref, left_ref, fold)
    weight_grad(left_ref, d_x1.astype(bf16), keep_ref, send_ref, 0)


def self_back_kernel(at_ref, *refs, pieces, narrow, fold):
    w_refs, refs = refs[:pieces], refs[pieces:]
    wo_refs, refs = refs[:pieces], refs[pieces:]
    (dx1_ref, o_ref, h_ref, x_ref, qkv_ref, extra_ref, table_ref, g_ref, peak_ref,
     inv_ref), refs = refs[:10], refs[10:]
    gx_refs, refs = refs[:narrow], refs[narrow:]
    (dg_ref, keep_ref, send_ref, ds_out, do_ref, dqkv_ref, dsum_ref, p_ref, ds_ref, dqt_ref,
     turned_ref, left_ref, dh_ref, w_ref, wo_ref, sems, wo_sems) = refs
    core = at_ref[0]
    wo_copies = start_weights(at_ref[3], wo_refs, wo_ref, wo_sems, pl.ds(0, 1))
    copies = start_weights(at_ref[3], w_refs, w_ref, sems, pl.ds(0, 3))
    branch = dx1_ref[...].astype(bf16)
    for copy in wo_copies:
        copy.wait()
    for start, size in tiles_of(o_ref.shape[1]):
        do_ref[:, start : start + size] = dot_nt(
            branch, wo_ref[0, start : start + size, :]
        ).astype(bf16)
    head_sums(do_ref[...], o_ref[...], dsum_ref)
    attend_back(qkv_ref, extra_ref, table_ref, do_ref, dsum_ref, peak_ref, inv_ref, dqkv_ref,
                p_ref, ds_ref, dqt_ref, ds_out)
    fold_rows(core, h_ref[...].T, turned_ref, left_ref, fold)
    for i in range(3):
        weight_grad(left_ref, dqkv_ref[i], keep_ref, send_ref, i)
    for copy in copies:
        copy.wait()
    for start, size in tiles_of(o_ref.shape[1]):
        rows = slice(start, start + size)
        dh_ref[:, rows] = (
            dot_nt(dqkv_ref[0], w_ref[0, rows, :])
            + dot_nt(dqkv_ref[1], w_ref[1, rows, :])
            + dot_nt(dqkv_ref[2], w_ref[2, rows, :])
        )
    back, d_gain = norm_back(dh_ref[...], x_ref[...].astype(f32), g_ref[0:1, :])
    dh_ref[...] = dx1_ref[...] + back
    split_rows(at_ref[2], dh_ref, gx_refs)
    dg_ref[...] = d_gain


def table_kernel(ds_ref, index_ref, out_ref, acc_ref, *, buckets):
    heads, keys, queries = ds_ref.shape
    acc_ref[...] = jnp.zeros_like(acc_ref)

    def group(at, carry):
        rows = pl.ds(pl.multiple_of(at * 16, 16), 16)
        index = index_ref[rows, :]
        grads = ds_ref[:, rows, :].reshape(heads * 16, queries)
        hot = jnp.concatenate(
            [(index == b).astype(f32).astype(bf16) for b in range(buckets)], axis=0
        )
        acc_ref[...] += dot_nt(grads, hot)
        return carry

    lax.fori_loop(0, keys // 16, group, 0)
    shape = acc_ref.shape
    same = (
        lax.broadcasted_iota(jnp.int32, shape, 0) % 16
        == lax.broadcasted_iota(jnp.int32, shape, 1) % 16
    )
    kept = jnp.where(same, acc_ref[...], 0.0).reshape(heads, 16, shape[1]).sum(axis=1)
    gather = (
        lax.broadcasted_iota(jnp.int32, (shape[1], 128), 0) // 16
        == lax.broadcasted_iota(jnp.int32, (shape[1], 128), 1)
    ).astype(f32)
    out_ref[...] = lax.dot_general(
        kept, gather, (((1,), (0,)), ((), ())),
        preferred_element_type=f32, precision=lax.Precision.HIGHEST,
    )


def call(kernel, outs, scratch, limit, *args, scalars=1, loose=(), flops=0):
    spaces = [
        pltpu.SMEM if i < scalars else pl.ANY if i in loose else pltpu.VMEM
        for i in range(len(args))
    ]
    moved = sum(a.size * a.dtype.itemsize for a in (*args, *outs))
    return pl.pallas_call(
        kernel,
        out_shape=outs,
        in_specs=[pl.BlockSpec(memory_space=space) for space in spaces],
        out_specs=[pl.BlockSpec(memory_space=pltpu.VMEM)] * len(outs),
        scratch_shapes=scratch,
        compiler_params=pltpu.CompilerParams(vmem_limit_bytes=limit * MIB),
        cost_estimate=pl.CostEstimate(flops=flops, bytes_accessed=moved, transcendentals=0),
    )(*args)


def shape_of(shape, dtype):
    return jax.ShapeDtypeStruct(tuple(shape), dtype)


def permuted(value, wide_bits, narrow_bits):
    wide, narrow = lax.axis_size("wide"), lax.axis_size("narrow")
    pairs = [
        (w * narrow + n, (w ^ wide_bits) * narrow + (n ^ narrow_bits))
        for w in range(wide)
        for n in range(narrow)
    ]
    return lax.ppermute(value, BOTH, pairs)


def ordered(at, pieces):
    first = pieces[0]
    if first.ndim == 2:
        shape = (len(pieces),) + first.shape
    else:
        shape = first.shape[:1] + (len(pieces),) + first.shape[1:]
    return call(order_kernel, [shape_of(shape, first.dtype)], [], 16, at, *pieces)[0]


def gathered(at, local, fast):
    if not fast:
        return [lax.all_gather(local, BOTH, axis=1, tiled=True)]
    narrow = lax.axis_size("narrow")
    near = [local] + [permuted(local, 0, d) for d in range(1, narrow)]
    stack = ordered(at, near)
    stack = stack.reshape(stack.shape[0], -1, stack.shape[3])
    plane = [stack] + [permuted(stack, 2 * d, 0) for d in range(1, 4)]
    return [piece for part in plane for piece in (part, permuted(part, 1, 0))]


def local_stats(gradient):
    squares = gradient * gradient + 1e-30
    return (jnp.sum(squares, axis=-1), jnp.sum(squares, axis=-2))


def scattered(at, pairs, fast, narrow):
    if not fast:
        results = []
        for keep, send in pairs:
            whole = jnp.concatenate([keep, send], axis=1)
            if keep.shape[0] == 4:
                whole = whole.reshape(1, -1, whole.shape[2])
            total = lax.psum_scatter(whole, BOTH, scatter_dimension=1, tiled=True).astype(f32)
            results.append((total, *local_stats(total)))
        return results
    count = len(pairs)
    keeps, sends = [], []
    for keep, send in pairs:
        stack = 1 if keep.shape[0] == 4 else keep.shape[0]
        keeps.append(keep.reshape(stack, -1, keep.shape[2]))
        sends.append(send.reshape(keeps[-1].shape))
    flat = [v for keep, send in zip(keeps, sends) for v in (keep, permuted(send, 1, 0))]
    outs = [
        shape_of((k.shape[0], k.shape[1] // 4, k.shape[2]), bf16 if d else f32)
        for k in keeps
        for d in range(4)
    ]
    parts = call(functools.partial(spread_kernel, count=count), outs, [], 40, at, *flat)
    parts = [permuted(v, 2 * (i % 4), 0) if i % 4 else v for i, v in enumerate(parts)]
    wholes = [(k.shape[0], k.shape[1] // 4, k.shape[2]) for k in keeps]
    outs = [
        shape_of((k, rows // narrow, cols), bf16 if d else f32)
        for k, rows, cols in wholes
        for d in range(narrow)
    ]
    parts = call(
        functools.partial(narrow_kernel, count=count, narrow=narrow),
        outs, [pltpu.VMEM(shape, f32) for shape in wholes], 32, at, *parts,
    )
    parts = [permuted(v, 0, i % narrow) if i % narrow else v for i, v in enumerate(parts)]
    outs = []
    for k, rows, cols in wholes:
        rows //= narrow
        outs += [
            shape_of((k, rows, cols), f32), shape_of((k, rows, 1), f32), shape_of((k, 1, cols), f32)
        ]
    flat = call(
        functools.partial(total_kernel, count=count, narrow=narrow), outs, [], 16, *parts, scalars=0
    )
    return [
        (flat[3 * i], flat[3 * i + 1][:, :, 0], flat[3 * i + 2][:, 0]) for i in range(count)
    ]


def summed_all(parts, fast):
    if not fast:
        return lax.psum(parts, BOTH)
    sizes = [v.size for v in parts]
    flat = jnp.concatenate([v.reshape(-1) for v in parts])
    flat = jnp.pad(flat, (0, -flat.size % 1024)).reshape(-1, 128)
    for bits in (1, 2, 4):
        flat = flat + permuted(flat, bits, 0)
    flat = (flat + permuted(flat, 0, 1)) + (permuted(flat, 0, 2) + permuted(flat, 0, 3))
    flat = flat.reshape(-1)
    results, at = [], 0
    for part, size in zip(parts, sizes):
        results.append(flat[at : at + size].reshape(part.shape))
        at += size
    return results


def adafactor_step(gradient, weight, rows_stat, cols_stat, weight_rms):
    overall = jnp.sum(cols_stat, axis=-1)[..., None, None]
    estimate = rows_stat[..., :, None] * cols_stat[..., None, :] / overall
    return weight - 0.3 * weight_rms * gradient * lax.rsqrt(estimate)


def body(
    targets, memory, cotangent, target_segments, memory_segments, buckets,
    attn_in, attn_out, gains, ff_in, ff_out, bias_table,
):
    wide, narrow = lax.axis_size("wide"), lax.axis_size("narrow")
    at_wide, at_narrow = lax.axis_index("wide"), lax.axis_index("narrow")
    fast = wide == 8 and narrow == 4
    at = jnp.stack([at_wide % 2, at_wide // 2, at_narrow, at_wide]).astype(jnp.int32)
    width, ff_width = attn_in.shape[2], ff_in.shape[2]
    bucket_count, heads = bias_table.shape
    chunk = gains.shape[1]
    local_tokens = targets.shape[1]
    tokens = local_tokens * narrow
    assert targets.shape[0] == narrow

    def row_pieces(stacked):
        return [
            permuted(lax.dynamic_index_in_dim(stacked, at_narrow ^ d, 0, False), 0, d)
            if d
            else lax.dynamic_index_in_dim(stacked, at_narrow, 0, False)
            for d in range(narrow)
        ]

    def to_owners(pieces):
        return ordered(at, [permuted(v, 0, d) if d else v for d, v in enumerate(pieces)])

    x_pieces = row_pieces(targets)
    device = at_wide * narrow + at_narrow
    gain_rows = lax.dynamic_update_slice(
        jnp.zeros((chunk, width), bf16), gains.astype(bf16), (0, device * chunk)
    )
    w_first = gathered(at, jnp.concatenate([attn_in[:3].astype(bf16), gain_rows[None]]), fast)
    segments = jnp.concatenate([target_segments, memory_segments], axis=1).astype(bf16)
    segments = jnp.pad(segments, ((0, 0), (0, buckets.shape[1] - segments.shape[1])))
    near = jnp.concatenate(
        [
            jnp.broadcast_to(buckets.astype(bf16)[None], (narrow,) + buckets.shape),
            jnp.broadcast_to(segments[:, None], (narrow, 16, buckets.shape[1])),
        ],
        axis=1,
    )
    index, cross_mask = call(
        functools.partial(prepare_kernel, narrow=narrow, bucket_count=bucket_count),
        [shape_of((tokens, tokens), jnp.int32), shape_of((tokens, tokens), f32)],
        [pltpu.VMEM((16, tokens), f32), pltpu.VMEM((tokens, tokens), f32)],
        24, at, *row_pieces(near),
    )
    table = jnp.concatenate(
        [bias_table.T, jnp.full((heads, 128 - bucket_count), NEG, f32)], axis=1
    )
    m_pieces = row_pieces(memory)
    w_second = gathered(
        at, jnp.concatenate([attn_out[:1], attn_in[3:], attn_out[1:]]).astype(bf16), fast
    )
    c_pieces = row_pieces(cotangent)
    lanes = TILE
    fin_blocks = ff_in.astype(bf16).reshape(2, chunk, ff_width // lanes, lanes)
    fin_blocks = fin_blocks.transpose(0, 2, 1, 3).reshape(-1, chunk, lanes)
    out_rows_here = ff_out.shape[0]
    fout_blocks = ff_out.astype(bf16).reshape(out_rows_here, width // lanes, lanes)
    fout_blocks = fout_blocks.transpose(1, 0, 2).reshape(-1, chunk, lanes)
    w_ffn = lax.all_gather(
        jnp.concatenate([fin_blocks, fout_blocks]), BOTH, axis=1, tiled=True
    )
    w_fout = w_ffn[fin_blocks.shape[0] :].reshape(-1, wide * narrow, chunk, lanes)
    w_fout = w_fout.transpose(1, 0, 2, 3).reshape(wide * narrow, -1, out_rows_here, lanes)
    w_fout = w_fout.transpose(1, 0, 2, 3).reshape(-1, ff_width, lanes)

    row16 = shape_of((tokens, width), bf16)
    row32 = shape_of((tokens, width), f32)
    three = shape_of((3, tokens, width), bf16)
    stat = shape_of((heads, 1, tokens), f32)
    gain_out = shape_of((1, width), f32)
    piece16 = shape_of((local_tokens, width), bf16)
    pair_t = pltpu.VMEM((128, tokens), f32)
    pieces = len(w_first)
    weights = lambda count: pltpu.VMEM((count, width, width), bf16)
    sems = pltpu.SemaphoreType.DMA((pieces,))
    g, x, h1, qkv1, o1, peak1, inv1 = call(
        functools.partial(first_kernel, pieces=pieces, narrow=narrow, chunk=chunk),
        [shape_of((8, width), f32), row16, row16, three, row16, stat, stat],
        [pair_t, weights(4), sems], 48,
        at, *x_pieces, *w_first, index, table,
        loose=range(1 + narrow, 1 + narrow + pieces),
    )
    m, x1, h2, qkv2, o2, x2, h3, peak2, inv2 = call(
        functools.partial(second_kernel, pieces=pieces, narrow=narrow),
        [row16, row32, row16, three, row16, row32, row16, stat, stat],
        [pair_t, weights(5), sems], 48,
        at, *m_pieces, *w_second, x, o1, cross_mask, g,
        loose=range(1 + narrow, 1 + narrow + pieces),
    )

    steps = 4
    part = ff_width // steps
    blocks = part // lanes
    half = width // 2
    whole = lambda shape: pl.BlockSpec(shape, lambda i: (0,) * len(shape))
    outs = pl.pallas_call(
        functools.partial(ffn_kernel, fold=fast, narrow=narrow),
        grid=(steps,),
        in_specs=[pl.BlockSpec(memory_space=pltpu.SMEM)]
        + [whole((local_tokens, width))] * narrow
        + [
            whole((tokens, width)), whole((tokens, width)), whole((8, width)),
            pl.BlockSpec((blocks, width, lanes), lambda i: (i, 0, 0)),
            pl.BlockSpec((blocks, width, lanes), lambda i: (i + steps, 0, 0)),
            pl.BlockSpec((width // lanes, part, lanes), lambda i: (0, i, 0)),
        ],
        out_specs=[whole((local_tokens, width))] * narrow
        + [
            whole((tokens, width)), whole((1, width)),
            pl.BlockSpec((2, half, part), lambda i: (0, 0, i)),
            pl.BlockSpec((2, half, part), lambda i: (0, 0, i)),
            pl.BlockSpec((None, part // 2, width), lambda i: (i, 0, 0)),
            pl.BlockSpec((None, part // 2, width), lambda i: (i, 0, 0)),
        ],
        out_shape=[piece16] * narrow
        + [
            row32, gain_out,
            shape_of((2, half, ff_width), bf16), shape_of((2, half, ff_width), bf16),
            shape_of((steps, part // 2, width), bf16), shape_of((steps, part // 2, width), bf16),
        ],
        scratch_shapes=[
            pltpu.VMEM((tokens, width), f32), pltpu.VMEM((tokens, width), f32),
            pltpu.VMEM((width, tokens), bf16), pltpu.VMEM((width, tokens), bf16),
            pltpu.VMEM((part, width), bf16), pltpu.VMEM((tokens, width), bf16),
        ],
        compiler_params=pltpu.CompilerParams(vmem_limit_bytes=48 * MIB),
        cost_estimate=pl.CostEstimate(
            flops=18 * tokens * width * ff_width, bytes_accessed=20 * MIB, transcendentals=0
        ),
    )(at, *c_pieces, x2, h3, g, w_ffn, w_ffn, w_fout)
    output = to_owners(outs[:narrow])
    dx2, gain3, keep_fin, send_fin, keep_fout, send_fout = outs[narrow:]
    (sum_fin, fin_rows, fin_part), (sum_fout, fout_rows, fout_part) = scattered(
        at, [(keep_fin, send_fin), (keep_fout, send_fout)], fast, narrow
    )

    square = pltpu.VMEM((tokens, tokens), bf16)
    back_scratch = [
        pltpu.VMEM((tokens, width), bf16), pltpu.VMEM((3, tokens, width), bf16),
        pltpu.VMEM((heads, 1, tokens), f32), square, square, pair_t,
        pltpu.VMEM((width, tokens), bf16), pltpu.VMEM((width, tokens), bf16),
    ]
    grads = lambda count: shape_of((count, half, width), bf16)
    outs = call(
        functools.partial(cross_back_kernel, pieces=pieces, narrow=narrow, fold=fast),
        [piece16] * narrow + [row32, gain_out, grads(5), grads(5)],
        back_scratch + [pltpu.VMEM((tokens, width), bf16), weights(5), sems], 52,
        at, *w_second, dx2, o2, h2, m, x1, o1, qkv2, cross_mask, g, peak2, inv2,
        loose=range(1, 1 + pieces),
    )
    grad_memory = to_owners(outs[:narrow])
    dx1, gain2, keep_second, send_second = outs[narrow:]
    ((sum_second, second_rows, second_part),) = scattered(
        at, [(keep_second, send_second)], fast, narrow
    )
    outs = call(
        functools.partial(self_back_kernel, pieces=pieces, narrow=narrow, fold=fast),
        [piece16] * narrow
        + [gain_out, grads(3), grads(3), shape_of((heads, tokens, tokens), bf16)],
        back_scratch + [pltpu.VMEM((tokens, width), f32), weights(3), weights(1), sems, sems], 60,
        at, *w_first, *w_second, dx1, o1, h1, x, qkv1, index, table, g, peak1, inv1,
        loose=range(1, 1 + 2 * pieces),
    )
    grad_targets = to_owners(outs[:narrow])
    gain1, keep_first, send_first, ds = outs[narrow:]
    ((sum_first, first_rows, first_part),) = scattered(
        at, [(keep_first, send_first)], fast, narrow
    )
    (table_part,) = call(
        functools.partial(table_kernel, buckets=bucket_count),
        [shape_of((heads, 128), f32)],
        [pltpu.VMEM((heads * 16, bucket_count * 16), f32)], 32, ds, index, scalars=0,
    )
    table_part = table_part[:, :bucket_count].T

    def regroup(first, second):
        return jnp.concatenate([first, second[1:4]]), jnp.stack([second[0], second[4]])

    sum_in, sum_out = regroup(sum_first, sum_second)
    in_rows, out_rows = regroup(first_rows, second_rows)
    in_part, out_part = regroup(first_part, second_part)
    sum_fout, fout_rows, fout_part = sum_fout[0], fout_rows[0], fout_part[0]
    gain_part = jnp.concatenate([gain1, gain2, gain3])
    in_square = jnp.sum(attn_in * attn_in, axis=(1, 2))
    out_square = jnp.sum(attn_out * attn_out, axis=(1, 2))
    fin_square = jnp.sum(ff_in * ff_in, axis=(1, 2))
    fout_square = jnp.sum(ff_out * ff_out).reshape(1)
    (
        sum_gain, in_cols, out_cols, fin_cols, fout_cols, grad_table,
        in_total, out_total, fin_total, fout_total,
    ) = summed_all(
        (
            gain_part, in_part, out_part, fin_part, fout_part, table_part,
            in_square, out_square, fin_square, fout_square,
        ),
        fast,
    )
    sum_gain = lax.dynamic_slice_in_dim(sum_gain, device * chunk, chunk, 1)
    table_rows, table_cols = local_stats(grad_table)
    in_rms = jnp.sqrt(in_total / (width * width) + 1e-06)[:, None, None]
    out_rms = jnp.sqrt(out_total / (width * width) + 1e-06)[:, None, None]
    fin_rms = jnp.sqrt(fin_total / (width * ff_width) + 1e-06)[:, None, None]
    fout_rms = jnp.sqrt(fout_total[0] / (width * ff_width) + 1e-06)
    table_rms = jnp.sqrt(jnp.mean(bias_table * bias_table) + 1e-06)
    return (
        output, grad_targets, grad_memory,
        sum_in, sum_out, sum_gain, sum_fin, sum_fout, grad_table,
        in_rows, in_cols, out_rows, out_cols, fin_rows, fin_cols, fout_rows, fout_cols,
        adafactor_step(sum_in, attn_in, in_rows, in_cols, in_rms),
        adafactor_step(sum_out, attn_out, out_rows, out_cols, out_rms),
        adafactor_step(sum_fin, ff_in, fin_rows, fin_cols, fin_rms),
        adafactor_step(sum_fout, ff_out, fout_rows, fout_cols, fout_rms),
        adafactor_step(grad_table, bias_table, table_rows, table_cols, table_rms),
    )


def solution(mesh):
    in_specs = (
        P("wide", "narrow", None),
        P("wide", "narrow", None),
        P("wide", "narrow", None),
        P("wide", "narrow"),
        P("wide", "narrow"),
        P("narrow", None),
        P(None, ("wide", "narrow"), None),
        P(None, ("wide", "narrow"), None),
        P(None, ("wide", "narrow")),
        P(None, ("wide", "narrow"), None),
        P(("wide", "narrow"), None),
        P(),
    )
    out_specs = (
        P("wide", "narrow", None),
        P("wide", "narrow", None),
        P("wide", "narrow", None),
        P(None, ("wide", "narrow"), None),
        P(None, ("wide", "narrow"), None),
        P(None, ("wide", "narrow")),
        P(None, ("wide", "narrow"), None),
        P(("wide", "narrow"), None),
        P(),
        P(None, ("wide", "narrow")),
        P(),
        P(None, ("wide", "narrow")),
        P(),
        P(None, ("wide", "narrow")),
        P(),
        P(("wide", "narrow")),
        P(),
        P(None, ("wide", "narrow"), None),
        P(None, ("wide", "narrow"), None),
        P(None, ("wide", "narrow"), None),
        P(("wide", "narrow"), None),
        P(),
    )
    return jax.shard_map(body, mesh=mesh, in_specs=in_specs, out_specs=out_specs, check_vma=False)
```

time: 899 us -> 587 us (0.65)
  matrix products: 202 us -> 0 us
  Pallas kernels: 0 us -> 154 us
  waiting for transfers between devices: 358 us -> 205 us
  blocking collectives: 138 us -> 0 us
  starting transfers between devices: 25.5 us -> 107 us
  other arithmetic: 72.5 us -> 19.8 us
    unnamed x12 -> x1, waiting for transfers between devices: 243 us -> 0.02 us
    ppermute x0 -> x75, waiting for transfers between devices: none -> 205 us  [permuted(): return lax.ppermute(value, BOTH, pairs)]
    dot_general x46 -> x0, matrix products: 195 us -> none  [the longest x11 38.3 us: back_mul(): jnp.einsum('rle,de->rld', left_rows, right_matrix, preferred_element_type...]
    pallas_call x0 -> x21, Pallas kernels: none -> 154 us  [the longest x20 130 us: call(): pl.pallas_call(kernel, out_shape=outs, in_specs=[pl.BlockSpec(memory_spac...]
    ppermute x0 -> x75, starting transfers between devices: none -> 107 us  [permuted(): return lax.ppermute(value, BOTH, pairs)]
    all_gather x1 -> x0, blocking collectives: 76 us -> none  [body(): lax.all_gather(gains.astype(jnp.bfloat16), ('wide', 'narrow'), axis=1, ti...]
    all_gather x5 -> x1, waiting for transfers between devices: 71.1 us -> 0.01 us  [body(): lax.all_gather(jnp.concatenate([fin_blocks, fout_blocks]), BOTH, axis=1,...]
    unnamed x1 -> x0, blocking collectives: 41.6 us -> none
  transfers between devices with their start and end apart: 15 -> 76, of which waited for: 8 -> 25; matrix products, arithmetic and copies ran while one was open for 31% -> 3% of each run, Pallas kernels for 0% -> 17%
where the time goes in v2:
time: 587 us; the launch traced here: 577 us
  waiting for transfers between devices  205 us (35%)
  Pallas kernels  154 us (26%)
  starting transfers between devices  107 us (18%)
  local copies, waits for them, and re-layouts  75.1 us (13%)
  other arithmetic  19.8 us (3%)
  between operations  16.7 us (3%)
    ppermute x75, waiting for transfers between devices, permuted(): return lax.ppermute(value, BOTH, pairs)  205 us
    pallas_call x20, Pallas kernels, call(): pl.pallas_call(kernel, out_shape=outs, in_specs=[pl.BlockSpec(memory_spac...  130 us
    ppermute x75, starting transfers between devices, permuted(): return lax.ppermute(value, BOTH, pairs)  107 us
    unnamed x274, local copies, waits for them, and re-layouts  57.6 us
    pallas_call x1, Pallas kernels, body(): pl.pallas_call(functools.partial(ffn_kernel, fold=fast, narrow=narrow), g...  23.6 us
  transfers between devices with their start and end apart: 76, of which 25 were waited for; matrix products, arithmetic and copies ran while one was open for 3% of the time, Pallas kernels for 17%

profile of v2, /device:TPU:0, one launch (start us, length us, event | category | flops | bytes accessed | tf_op | source)
XLA Modules:
  0.0 576.5 jit_solution(9556479513702603303)
XLA Ops:
  24.8 7.0 %collective-permute-done.30.refs_2_ = bf16[144,512]{1,0:T(8,128)(2,1)S(1)} collective-permute-done((bf16[144,512]{1,0:T(8,128)(2,1)S(1)}, bf16[144,512]{1,0:T(8,128)(2,1)S(1)}, u32[]{:S(2)}, u32[]{:S(2)}) %collective-permute-start.30) | collective-permute-done | bytes 147488 | tf_op jit(solution)/shard_map/ppermute | solution.py:536
  34.1 4.8 collective-permute-start.7
  44.3 11.2 %collective-permute-done.20.refs_2_ = bf16[4,24,768]{2,1,0:T(8,128)(2,1)S(1)} collective-permute-done((bf16[4,24,768]{2,1,0:T(8,128)(2,1)S(1)}, bf16[4,24,768]{2,1,0:T(8,128)(2,1)S(1)}, u32[]{:S(2)}, u32[]{:S(2)}) %collective-permute-start.20) | collective-permute-done | bytes 147488 | tf_op jit(solution)/shard_map/ppermute | solution.py:536
  56.1 5.1 collective-permute-start.17
  63.4 9.9 %collective-permute-done.7.refs_2_ = bf16[5,24,768]{2,1,0:T(8,128)(2,1)S(1)} collective-permute-done((bf16[5,24,768]{2,1,0:T(8,128)(2,1)S(1)}, bf16[5,24,768]{2,1,0:T(8,128)(2,1)S(1)}, u32[]{:S(2)}, u32[]{:S(2)}) %collective-permute-start.7) | collective-permute-done | bytes 184352 | tf_op jit(solution)/shard_map/ppermute | solution.py:536
  80.9 12.0 %collective-permute-done.17.refs_2_ = bf16[128,768]{1,0:T(8,128)(2,1)S(1)} collective-permute-done((bf16[128,768]{1,0:T(8,128)(2,1)}, bf16[128,768]{1,0:T(8,128)(2,1)S(1)}, u32[]{:S(2)}, u32[]{:S(2)}) %collective-permute-start.17) | collective-permute-done | bytes 196640 | tf_op jit(solution)/shard_map/ppermute | solution.py:536
  98.0 21.8 %collective-permute-done.4.refs_2_ = bf16[128,768]{1,0:T(8,128)(2,1)S(1)} collective-permute-done((bf16[128,768]{1,0:T(8,128)(2,1)S(1)}, bf16[128,768]{1,0:T(8,128)(2,1)S(1)}, u32[]{:S(2)}, u32[]{:S(2)}) %collective-permute-start.4) | collective-permute-done | bytes 196640 | tf_op jit(solution)/shard_map/ppermute | solution.py:536
  124.1 7.2 %collective-permute-done.5.refs_3_ = bf16[128,768]{1,0:T(8,128)(2,1)S(1)} collective-permute-done((bf16[128,768]{1,0:T(8,128)(2,1)S(1)}, bf16[128,768]{1,0:T(8,128)(2,1)S(1)}, u32[]{:S(2)}, u32[]{:S(2)}) %collective-permute-start.5) | collective-permute-done | bytes 196640 | tf_op jit(solution)/shard_map/ppermute | solution.py:536
  135.3 14.0 %collective-permute-done.10.refs_6_.refs_2_.refs_10_ = bf16[5,96,768]{2,1,0:T(8,128)(2,1)S(1)} collective-permute-done((bf16[5,96,768]{2,1,0:T(8,128)(2,1)S(1)}, bf16[5,96,768]{2,1,0:T(8,128)(2,1)S(1)}, u32[]{:S(2)}, u32[]{:S(2)}) %collective-permute-start.10) | collective-permute-done | bytes 737312 | tf_op jit(solution)/shard_map/ppermute | solution.py:536
  149.3 9.3 %collective-permute-done.12.refs_8_.refs_4_.refs_12_ = bf16[5,96,768]{2,1,0:T(8,128)(2,1)S(1)} collective-permute-done((bf16[5,96,768]{2,1,0:T(8,128)(2,1)S(1)}, bf16[5,96,768]{2,1,0:T(8,128)(2,1)S(1)}, u32[]{:S(2)}, u32[]{:S(2)}) %collective-permute-start.12) | collective-permute-done | bytes 737312 | tf_op jit(solution)/shard_map/ppermute | solution.py:536
  175.2 15.7 %shard_map.294 = (f32[8,768]{1,0:T(8,128)S(1)}, bf16[512,768]{1,0:T(8,128)(2,1)}, bf16[512,768]{1,0:T(8,128)(2,1)}, bf16[3,512,768]{2,1,0:T(8,128)(2,1)}, bf16[5...) custom-call(s32[4]{0:T(128)S(1)} %pad_add_fusion.at_ref, ...), custom_call_target="tpu_custom_call" | custom-call | bytes 11352080 | tf_op jit(solution)/shard_map/pallas_call | solution.py:514
  198.0 20.9 %shard_map.295 = (bf16[512,768]{1,0:T(8,128)(2,1)}, f32[512,768]{1,0:T(8,128)}, bf16[512,768]{1,0:T(8,128)(2,1)}, bf16[3,512,768]{2,1,0:T(8,128)(2,1)}, bf16[512...) custom-call(s32[4]{0:T(128)S(1)} %pad_add_fusion.at_ref, ...), custom_call_target="tpu_custom_call" | custom-call | bytes 18030608 | tf_op jit(solution)/shard_map/pallas_call | solution.py:514
  228.4 23.6 %shard_map.296 = (bf16[128,768]{1,0:T(8,128)(2,1)S(1)}, bf16[128,768]{1,0:T(8,128)(2,1)}, bf16[128,768]{1,0:T(8,128)(2,1)}, bf16[128,768]{1,0:T(8,128)(2,1)}, f3...) custom-call(s32[4]{0:T(128)S(1)} %pad_add_fusion.at_ref, ...), custom_call_target="tpu_custom_call" | custom-call | flops 14495514624 | bytes 20971520 | tf_op jit(solution)/shard_map/pallas_call | solution.py:734
  255.0 28.7 %shard_map.298 = (bf16[128,768]{1,0:T(8,128)(2,1)S(1)}, bf16[128,768]{1,0:T(8,128)(2,1)S(1)}, bf16[128,768]{1,0:T(8,128)(2,1)S(1)}, bf16[128,768]{1,0:T(8,128)(2...) custom-call(s32[4]{0:T(128)S(1)} %pad_add_fusion.at_ref, ...), custom_call_target="tpu_custom_call" | custom-call | bytes 23931920 | tf_op jit(solution)/shard_map/pallas_call | solution.py:514
  284.8 28.3 %shard_map.299 = (bf16[128,768]{1,0:T(8,128)(2,1)}, bf16[128,768]{1,0:T(8,128)(2,1)}, bf16[128,768]{1,0:T(8,128)(2,1)}, bf16[128,768]{1,0:T(8,128)(2,1)}, f32[1,...) custom-call(s32[4]{0:T(128)} %copy-done.78, ...), custom_call_target="tpu_custom_call" | custom-call | bytes 28656656 | tf_op jit(solution)/shard_map/pallas_call | solution.py:514
  314.3 6.3 %collective-permute-done.38.refs_1_ = bf16[128,768]{1,0:T(8,128)(2,1)S(1)} collective-permute-done((bf16[128,768]{1,0:T(8,128)(2,1)S(1)}, bf16[128,768]{1,0:T(8,128)(2,1)S(1)}, u32[]{:S(2)}, u32[]{:S(2)}) %collective-permute-start.38) | collective-permute-done | bytes 196640 | tf_op jit(solution)/shard_map/ppermute | solution.py:536
  322.5 9.2 %collective-permute-done.39.refs_2_ = bf16[128,768]{1,0:T(8,128)(2,1)S(1)} collective-permute-done((bf16[128,768]{1,0:T(8,128)(2,1)S(1)}, bf16[128,768]{1,0:T(8,128)(2,1)S(1)}, u32[]{:S(2)}, u32[]{:S(2)}) %collective-permute-start.39) | collective-permute-done | bytes 196640 | tf_op jit(solution)/shard_map/ppermute | solution.py:536
  334.1 6.3 %collective-permute-done.40.refs_3_ = bf16[128,768]{1,0:T(8,128)(2,1)S(1)} collective-permute-done((bf16[128,768]{1,0:T(8,128)(2,1)S(1)}, bf16[128,768]{1,0:T(8,128)(2,1)S(1)}, u32[]{:S(2)}, u32[]{:S(2)}) %collective-permute-start.40) | collective-permute-done | bytes 196640 | tf_op jit(solution)/shard_map/ppermute | solution.py:536
  369.0 33.3 %collective-permute-done.44.refs_3_ = bf16[3,96,768]{2,1,0:T(8,128)(2,1)S(1)} collective-permute-done((bf16[3,96,768]{2,1,0:T(8,128)(2,1)S(1)}, bf16[3,96,768]{2,1,0:T(8,128)(2,1)S(1)}, u32[]{:S(2)}, u32[]{:S(2)}) %collective-permute-start.44) | collective-permute-done | bytes 442400 | tf_op jit(solution)/shard_map/ppermute | solution.py:536
  420.0 11.3 %shard_map.311 = f32[12,128]{1,0:T(8,128)S(1)} custom-call(bf16[12,512,512]{2,1,0:T(8,128)(2,1)S(1)} %copy-done.9, s32[512,512]{1,0:T(8,128)S(1)} %copy-done.2), custom_call_target="tpu_custom_call" | custom-call | bytes 7346176 | tf_op jit(solution)/shard_map/pallas_call | solution.py:514
  452.5 5.0 collective-permute-done.53.refs_2_
  482.7 17.3 %collective-permute-done.61.refs_6_ = bf16[1,256,768]{2,1,0:T(8,128)(2,1)S(1)} collective-permute-done((bf16[1,256,768]{2,1,0:T(8,128)(2,1)}, bf16[1,256,768]{2,1,0:T(8,128)(2,1)S(1)}, u32[]{:S(2)}, u32[]{:S(2)}) %collective-permute-start.61) | collective-permute-done | bytes 393248 | tf_op jit(solution)/shard_map/ppermute | solution.py:536
  513.3 8.8 %collective-permute-done.66.refs_5_ = bf16[1,64,768]{2,1,0:T(8,128)(2,1)S(1)} collective-permute-done((bf16[1,64,768]{2,1,0:T(8,128)(2,1)}, bf16[1,64,768]{2,1,0:T(8,128)(2,1)S(1)}, u32[]{:S(2)}, u32[]{:S(2)}) %collective-permute-start.66) | collective-permute-done | bytes 98336 | tf_op jit(solution)/shard_map/ppermute | solution.py:536
  525.5 7.8 %collective-permute-done.67.refs_6_ = bf16[1,64,768]{2,1,0:T(8,128)(2,1)S(1)} collective-permute-done((bf16[1,64,768]{2,1,0:T(8,128)(2,1)}, bf16[1,64,768]{2,1,0:T(8,128)(2,1)S(1)}, u32[]{:S(2)}, u32[]{:S(2)}) %collective-permute-start.67) | collective-permute-done | bytes 98336 | tf_op jit(solution)/shard_map/ppermute | solution.py:536
  (510 shorter events, 234.9 us)
Async XLA Ops:
  7.2 216.7 %all-gather.2.cloned.1.call-start = ((), (), s32[]{:S(2)}) async-start(), calls=%async_computation | async-start | bytes 9732096 | tf_op jit(solution)/shard_map/all_gather | solution.py:697
  19.6 41.5 %collective-permute-start.6 = (bf16[5,24,768]{2,1,0:T(8,128)(2,1)S(1)}, bf16[5,24,768]{2,1,0:T(8,128)(2,1)S(1)}, u32[]{:S(2)}, u32[]{:S(2)}) collective-permute-start(bf16[5,24,768]{2,1,0:T(8,128)(2,1)S(1)} %pad_maximum_fusion.2.refs_0_), channel_id=1, source_target_pairs={{0,1},{1,0},{2,3},{3,2},{4,5},{5,4},{6,7},{7,6},{8,9},{9,8},{10,11... | collective-permute-start | bytes 552968 | tf_op jit(solution)/shard_map/ppermute | solution.py:536
  34.1 39.1 %collective-permute-start.7 = (bf16[5,24,768]{2,1,0:T(8,128)(2,1)S(1)}, bf16[5,24,768]{2,1,0:T(8,128)(2,1)S(1)}, u32[]{:S(2)}, u32[]{:S(2)}) collective-permute-start(bf16[5,24,768]{2,1,0:T(8,128)(2,1)S(1)} %pad_maximum_fusion.2.refs_0_), channel_id=1, source_target_pairs={{0,2},{1,3},{2,0},{3,1},{4,6},{5,7},{6,4},{7,5},{8,10},{9,11},{10,... | collective-permute-start | bytes 552968 | tf_op jit(solution)/shard_map/ppermute | solution.py:536
  40.3 37.0 %collective-permute-start.8 = (bf16[5,24,768]{2,1,0:T(8,128)(2,1)S(1)}, bf16[5,24,768]{2,1,0:T(8,128)(2,1)S(1)}, u32[]{:S(2)}, u32[]{:S(2)}) collective-permute-start(bf16[5,24,768]{2,1,0:T(8,128)(2,1)S(1)} %pad_maximum_fusion.2.refs_0_), channel_id=1, source_target_pairs={{0,3},{1,2},{2,1},{3,0},{4,7},{5,6},{6,5},{7,4},{8,11},{9,10},{10,... | collective-permute-start | bytes 552968 | tf_op jit(solution)/shard_map/ppermute | solution.py:536
  77.3 54.9 %collective-permute-start.23 = (bf16[4,96,768]{2,1,0:T(8,128)(2,1)S(1)}, bf16[4,96,768]{2,1,0:T(8,128)(2,1)S(1)}, u32[]{:S(2)}, u32[]{:S(2)}) collective-permute-start(bf16[4,96,768]{2,1,0:T(8,128)(2,1)S(1)} %bitcast.92), channel_id=1, source_target_pairs={{0,8},{1,9},{2,10},{3,11},{4,12},{5,13},{6,14},{7,15},{8,0},{9,1},... | collective-permute-start | bytes 1769480 | tf_op jit(solution)/shard_map/ppermute | solution.py:536
  79.4 54.9 %collective-permute-start.25 = (bf16[4,96,768]{2,1,0:T(8,128)(2,1)S(1)}, bf16[4,96,768]{2,1,0:T(8,128)(2,1)S(1)}, u32[]{:S(2)}, u32[]{:S(2)}) collective-permute-start(bf16[4,96,768]{2,1,0:T(8,128)(2,1)S(1)} %bitcast.93), channel_id=1, source_target_pairs={{0,16},{1,17},{2,18},{3,19},{4,20},{5,21},{6,22},{7,23},{8,24},{9,... | collective-permute-start | bytes 1769480 | tf_op jit(solution)/shard_map/ppermute | solution.py:536
  93.6 41.2 %collective-permute-start.27 = (bf16[4,96,768]{2,1,0:T(8,128)(2,1)S(1)}, bf16[4,96,768]{2,1,0:T(8,128)(2,1)S(1)}, u32[]{:S(2)}, u32[]{:S(2)}) collective-permute-start(bf16[4,96,768]{2,1,0:T(8,128)(2,1)S(1)} %bitcast.94), channel_id=1, source_target_pairs={{0,24},{1,25},{2,26},{3,27},{4,28},{5,29},{6,30},{7,31},{8,16},{9,... | collective-permute-start | bytes 1769480 | tf_op jit(solution)/shard_map/ppermute | solution.py:536
  159.1 38.0 %collective-permute-start.13 = (bf16[5,96,768]{2,1,0:T(8,128)(2,1)S(1)}, bf16[5,96,768]{2,1,0:T(8,128)(2,1)S(1)}, u32[]{:S(2)}, u32[]{:S(2)}) collective-permute-start(bf16[5,96,768]{2,1,0:T(8,128)(2,1)S(1)} %collective-permute-done.12.refs_8_.refs_4_.refs_12_), channel_id=1, source_target_pairs={{0,4},{1,5},{2,6},{3,7},{4,0},{5,1},{6,2},{7,3},{8,12},{9,13},{10,... | collective-permute-start | bytes 2211848 | tf_op jit(solution)/shard_map/ppermute | solution.py:536
  159.2 37.9 %collective-permute-start.15 = (bf16[5,96,768]{2,1,0:T(8,128)(2,1)S(1)}, bf16[5,96,768]{2,1,0:T(8,128)(2,1)S(1)}, u32[]{:S(2)}, u32[]{:S(2)}) collective-permute-start(bf16[5,96,768]{2,1,0:T(8,128)(2,1)S(1)} %collective-permute-done.14.refs_10_.refs_6_.refs_14_), channel_id=1, source_target_pairs={{0,4},{1,5},{2,6},{3,7},{4,0},{5,1},{6,2},{7,3},{8,12},{9,13},{10,... | collective-permute-start | bytes 2211848 | tf_op jit(solution)/shard_map/ppermute | solution.py:536
  161.8 66.6 %collective-permute-start = (bf16[128,768]{1,0:T(8,128)(2,1)}, bf16[128,768]{1,0:T(8,128)(2,1)}, u32[]{:S(2)}, u32[]{:S(2)}) collective-permute-start(bf16[128,768]{1,0:T(8,128)(2,1)} %get-tuple-element.237), channel_id=1, source_target_pairs={{0,1},{1,0},{2,3},{3,2},{4,5},{5,4},{6,7},{7,6},{8,9},{9,8},{10,11... | collective-permute-start | bytes 589832 | tf_op jit(solution)/shard_map/ppermute | solution.py:536
  165.9 62.4 %collective-permute-start.1 = (bf16[128,768]{1,0:T(8,128)(2,1)}, bf16[128,768]{1,0:T(8,128)(2,1)}, u32[]{:S(2)}, u32[]{:S(2)}) collective-permute-start(bf16[128,768]{1,0:T(8,128)(2,1)} %get-tuple-element.239), channel_id=1, source_target_pairs={{0,2},{1,3},{2,0},{3,1},{4,6},{5,7},{6,4},{7,5},{8,10},{9,11},{10,... | collective-permute-start | bytes 589832 | tf_op jit(solution)/shard_map/ppermute | solution.py:536
  167.3 61.0 %collective-permute-start.2 = (bf16[128,768]{1,0:T(8,128)(2,1)}, bf16[128,768]{1,0:T(8,128)(2,1)}, u32[]{:S(2)}, u32[]{:S(2)}) collective-permute-start(bf16[128,768]{1,0:T(8,128)(2,1)} %get-tuple-element.236), channel_id=1, source_target_pairs={{0,3},{1,2},{2,1},{3,0},{4,7},{5,6},{6,5},{7,4},{8,11},{9,10},{10,... | collective-permute-start | bytes 589832 | tf_op jit(solution)/shard_map/ppermute | solution.py:536
  284.3 70.0 %collective-permute-start.48 = (bf16[5,384,768]{2,1,0:T(8,128)(2,1)}, bf16[5,384,768]{2,1,0:T(8,128)(2,1)S(1)}, u32[]{:S(2)}, u32[]{:S(2)}) collective-permute-start(bf16[5,384,768]{2,1,0:T(8,128)(2,1)} %get-tuple-element.154), channel_id=1, source_target_pairs={{0,4},{1,5},{2,6},{3,7},{4,0},{5,1},{6,2},{7,3},{8,12},{9,13},{10,... | collective-permute-start | bytes 8847368 | tf_op jit(solution)/shard_map/ppermute | solution.py:536
  284.3 118.8 %collective-permute-start.55 = (bf16[2,384,2048]{2,1,0:T(8,128)(2,1)}, bf16[2,384,2048]{2,1,0:T(8,128)(2,1)}, u32[]{:S(2)}, u32[]{:S(2)}) collective-permute-start(bf16[2,384,2048]{2,1,0:T(8,128)(2,1)} %get-tuple-element.170), channel_id=1, source_target_pairs={{0,4},{1,5},{2,6},{3,7},{4,0},{5,1},{6,2},{7,3},{8,12},{9,13},{10,... | collective-permute-start | bytes 9437192 | tf_op jit(solution)/shard_map/ppermute | solution.py:536
  313.2 48.7 %collective-permute-start.56 = (bf16[1,1024,768]{2,1,0:T(8,128)(2,1)}, bf16[1,1024,768]{2,1,0:T(8,128)(2,1)S(1)}, u32[]{:S(2)}, u32[]{:S(2)}) collective-permute-start(bf16[1,1024,768]{2,1,0:T(8,128)(2,1)} %bitcast.114), channel_id=1, source_target_pairs={{0,4},{1,5},{2,6},{3,7},{4,0},{5,1},{6,2},{7,3},{8,12},{9,13},{10,... | collective-permute-start | bytes 4718600 | tf_op jit(solution)/shard_map/ppermute | solution.py:536
  361.5 43.9 %collective-permute-start.49 = (bf16[5,96,768]{2,1,0:T(8,128)(2,1)S(1)}, bf16[5,96,768]{2,1,0:T(8,128)(2,1)S(1)}, u32[]{:S(2)}, u32[]{:S(2)}) collective-permute-start(bf16[5,96,768]{2,1,0:T(8,128)(2,1)S(1)} %get-tuple-element.156), channel_id=1, source_target_pairs={{0,8},{1,9},{2,10},{3,11},{4,12},{5,13},{6,14},{7,15},{8,0},{9,1},... | collective-permute-start | bytes 2211848 | tf_op jit(solution)/shard_map/ppermute | solution.py:536
  363.1 50.5 %collective-permute-start.50 = (bf16[5,96,768]{2,1,0:T(8,128)(2,1)}, bf16[5,96,768]{2,1,0:T(8,128)(2,1)}, u32[]{:S(2)}, u32[]{:S(2)}) collective-permute-start(bf16[5,96,768]{2,1,0:T(8,128)(2,1)} %get-tuple-element.157), channel_id=1, source_target_pairs={{0,16},{1,17},{2,18},{3,19},{4,20},{5,21},{6,22},{7,23},{8,24},{9,... | collective-permute-start | bytes 2211848 | tf_op jit(solution)/shard_map/ppermute | solution.py:536
  365.3 48.3 %collective-permute-start.51 = (bf16[5,96,768]{2,1,0:T(8,128)(2,1)}, bf16[5,96,768]{2,1,0:T(8,128)(2,1)}, u32[]{:S(2)}, u32[]{:S(2)}) collective-permute-start(bf16[5,96,768]{2,1,0:T(8,128)(2,1)} %get-tuple-element.158), channel_id=1, source_target_pairs={{0,24},{1,25},{2,26},{3,27},{4,28},{5,29},{6,30},{7,31},{8,16},{9,... | collective-permute-start | bytes 2211848 | tf_op jit(solution)/shard_map/ppermute | solution.py:536
  403.1 39.6 %collective-permute-start.33 = (bf16[128,768]{1,0:T(8,128)(2,1)}, bf16[128,768]{1,0:T(8,128)(2,1)}, u32[]{:S(2)}, u32[]{:S(2)}) collective-permute-start(bf16[128,768]{1,0:T(8,128)(2,1)} %get-tuple-element.119), channel_id=1, source_target_pairs={{0,2},{1,3},{2,0},{3,1},{4,6},{5,7},{6,4},{7,5},{8,10},{9,11},{10,... | collective-permute-start | bytes 589832 | tf_op jit(solution)/shard_map/ppermute | solution.py:536
  405.4 37.9 %collective-permute-start.34 = (bf16[128,768]{1,0:T(8,128)(2,1)}, bf16[128,768]{1,0:T(8,128)(2,1)}, u32[]{:S(2)}, u32[]{:S(2)}) collective-permute-start(bf16[128,768]{1,0:T(8,128)(2,1)} %get-tuple-element.120), channel_id=1, source_target_pairs={{0,3},{1,2},{2,1},{3,0},{4,7},{5,6},{6,5},{7,4},{8,11},{9,10},{10,... | collective-permute-start | bytes 589832 | tf_op jit(solution)/shard_map/ppermute | solution.py:536
  442.7 38.5 %collective-permute-start.60 = (bf16[1,256,768]{2,1,0:T(8,128)(2,1)}, bf16[1,256,768]{2,1,0:T(8,128)(2,1)S(1)}, u32[]{:S(2)}, u32[]{:S(2)}) collective-permute-start(bf16[1,256,768]{2,1,0:T(8,128)(2,1)} %get-tuple-element.178), channel_id=1, source_target_pairs={{0,8},{1,9},{2,10},{3,11},{4,12},{5,13},{6,14},{7,15},{8,0},{9,1},... | collective-permute-start | bytes 1179656 | tf_op jit(solution)/shard_map/ppermute | solution.py:536
  450.5 49.5 %collective-permute-start.57 = (bf16[2,96,2048]{2,1,0:T(8,128)(2,1)}, bf16[2,96,2048]{2,1,0:T(8,128)(2,1)S(1)}, u32[]{:S(2)}, u32[]{:S(2)}) collective-permute-start(bf16[2,96,2048]{2,1,0:T(8,128)(2,1)} %copy-done.99), channel_id=1, source_target_pairs={{0,8},{1,9},{2,10},{3,11},{4,12},{5,13},{6,14},{7,15},{8,0},{9,1},... | collective-permute-start | bytes 2359304 | tf_op jit(solution)/shard_map/ppermute | solution.py:536
  451.8 48.2 %collective-permute-start.58 = (bf16[2,96,2048]{2,1,0:T(8,128)(2,1)}, bf16[2,96,2048]{2,1,0:T(8,128)(2,1)}, u32[]{:S(2)}, u32[]{:S(2)}) collective-permute-start(bf16[2,96,2048]{2,1,0:T(8,128)(2,1)} %copy-done.98), channel_id=1, source_target_pairs={{0,16},{1,17},{2,18},{3,19},{4,20},{5,21},{6,22},{7,23},{8,24},{9,... | collective-permute-start | bytes 2359304 | tf_op jit(solution)/shard_map/ppermute | solution.py:536
  457.6 42.4 %collective-permute-start.59 = (bf16[2,96,2048]{2,1,0:T(8,128)(2,1)}, bf16[2,96,2048]{2,1,0:T(8,128)(2,1)}, u32[]{:S(2)}, u32[]{:S(2)}) collective-permute-start(bf16[2,96,2048]{2,1,0:T(8,128)(2,1)} %copy-done.97), channel_id=1, source_target_pairs={{0,24},{1,25},{2,26},{3,27},{4,28},{5,29},{6,30},{7,31},{8,16},{9,... | collective-permute-start | bytes 2359304 | tf_op jit(solution)/shard_map/ppermute | solution.py:536
  (188 other events, 3101.2 us)
Sparse Core Ops, SparseCore 0:
  11.9 132.0 all-gather.1

commit v3 on v2

--- a/solution.py
+++ b/solution.py
@@ -1,4 +1,5 @@
 import functools
+import math
 
 import jax
 import jax.numpy as jnp
@@ -181,12 +182,13 @@
             out_ref[to : to + size, :] = turned_ref[pl.ds(begin, size), :]
 
 
-def weight_grad(left_ref, right, keep_ref, send_ref, index):
+def weight_grad(left_ref, right_ref, keep_ref, send_ref, index):
     half = left_ref.shape[0] // 2
-    for start, size in tiles_of(right.shape[1]):
-        product = dot_nn(left_ref[...], right[:, start : start + size]).astype(bf16)
-        keep_ref[index, :, start : start + size] = product[:half]
-        send_ref[index, :, start : start + size] = product[half:]
+    for start, size in tiles_of(right_ref.shape[1]):
+        part = slice(start, start + size)
+        right = right_ref[:, part]
+        keep_ref[index, :, part] = dot_nn(left_ref[:half], right).astype(bf16)
+        send_ref[index, :, part] = dot_nn(left_ref[half:], right).astype(bf16)
 
 
 def start_weights(place, pieces, target_ref, sems, only=None):
@@ -202,10 +204,39 @@
     return copies
 
 
-def join_rows(place, pieces, target_ref):
-    rows = pieces[0].shape[0]
+def join_rows(place, pieces, which, target_ref):
+    rows = pieces[0].shape[1]
     for d, piece in enumerate(pieces):
-        target_ref[pl.ds(pl.multiple_of((place ^ d) * rows, 16), rows), :] = piece[...]
+        target_ref[pl.ds(pl.multiple_of((place ^ d) * rows, 16), rows), :] = piece[which]
+
+
+def join_blocks(place, pieces, target_ref):
+    blocks = target_ref.shape[1] // TILE
+    rows = target_ref.shape[0] // len(pieces)
+    for d, piece in enumerate(pieces):
+        to = pl.ds(pl.multiple_of((place ^ d) * rows, 16), rows)
+        for j in range(blocks):
+            target_ref[to, j * TILE : (j + 1) * TILE] = piece[j * rows : (j + 1) * rows, :]
+
+
+def pack_kernel(at_ref, x_ref, m_ref, c_ref, buckets_ref, seg_t_ref, seg_m_ref, *outs, narrow):
+    local, width = x_ref.shape[1:]
+    for d in range(narrow):
+        first, both = outs[d], outs[narrow + d]
+        row = at_ref[2] ^ d
+        both[0] = m_ref[row]
+        both[1] = c_ref[row]
+        begin = 0
+        for j in range(width // TILE):
+            first[begin : begin + local, :] = x_ref[row, :, j * TILE : (j + 1) * TILE]
+            begin += local
+        for j in range(buckets_ref.shape[1] // TILE):
+            part = buckets_ref[:, j * TILE : (j + 1) * TILE]
+            first[begin : begin + local, :] = part.astype(f32).astype(bf16)
+            begin += local
+        for i, ref in enumerate((seg_t_ref, seg_m_ref)):
+            seg = jnp.broadcast_to(ref[pl.ds(row, 1), :].astype(f32), (16, local))
+            first[begin : begin + 16, i * local : (i + 1) * local] = seg.astype(bf16)
 
 
 def split_rows(place, source_ref, pieces):
@@ -222,7 +253,7 @@
     (extra_ref, table_ref, g_ref, x_ref, h_ref, qkv_ref, o_ref, peak_ref, inv_ref,
      ot_ref, w_ref, sems) = refs
     copies = start_weights(at_ref[3], w_refs, w_ref, sems)
-    join_rows(at_ref[2], x_refs, x_ref)
+    join_blocks(at_ref[2], x_refs, x_ref)
     width = x_ref.shape[1]
     pick = (
         lax.broadcasted_iota(jnp.int32, (8, width), 1) % chunk
@@ -245,10 +276,11 @@
 def second_kernel(at_ref, *refs, pieces, narrow):
     m_refs, refs = refs[:narrow], refs[narrow:]
     w_refs, refs = refs[:pieces], refs[pieces:]
-    (x_ref, o1_ref, extra_ref, g_ref, m_ref, x1_ref, h_ref, qkv_ref, o_ref, x2_ref, h3_ref,
+    (x_ref, o1_ref, extra_ref, g_ref, m_ref, c_ref, x1_ref, h_ref, qkv_ref, o_ref, x2_ref, h3_ref,
      peak_ref, inv_ref, ot_ref, w_ref, sems) = refs
     copies = start_weights(at_ref[3], w_refs, w_ref, sems)
-    join_rows(at_ref[2], m_refs, m_ref)
+    join_rows(at_ref[2], m_refs, 0, m_ref)
+    join_rows(at_ref[2], m_refs, 1, c_ref)
     for copy in copies:
         copy.wait()
 
@@ -275,18 +307,23 @@
     h3_ref[...] = (unit * g_ref[2:3, :]).astype(bf16)
 
 
-def prepare_kernel(at_ref, *refs, narrow, bucket_count):
+def prepare_kernel(at_ref, *refs, narrow, bucket_count, skip):
     in_refs, (index_ref, mask_ref, seg_ref, near_ref) = refs[:narrow], refs[narrow:]
-    local = in_refs[0].shape[0] - 16
+    tokens = near_ref.shape[0]
+    local = tokens // narrow
     for d, ref in enumerate(in_refs):
         lanes = pl.ds(pl.multiple_of((at_ref[2] ^ d) * local, 128), local)
-        near_ref[:, lanes] = ref[:local, :].astype(f32).T
-        tail = ref[local:, :].astype(f32)
-        seg_ref[0:8, lanes] = jnp.broadcast_to(tail[0:1, :local], (8, local))
-        seg_ref[8:16, lanes] = jnp.broadcast_to(tail[0:1, local : 2 * local], (8, local))
+        begin = skip
+        for j in range(tokens // TILE):
+            near_ref[j * TILE : (j + 1) * TILE, lanes] = (
+                ref[begin : begin + local, :].astype(f32).T
+            )
+            begin += local
+        tail = ref[begin : begin + 16, :].astype(f32)
+        seg_ref[0:8, lanes] = tail[:8, :local]
+        seg_ref[8:16, lanes] = tail[:8, local : 2 * local]
     seg = seg_ref[...]
     seg_t = seg.T
-    tokens = near_ref.shape[0]
     key = lax.broadcasted_iota(jnp.int32, (tokens, tokens), 0)
     query = lax.broadcasted_iota(jnp.int32, (tokens, tokens), 1)
     allowed = (key <= query) & (seg_t[:, 0:1] == seg[0:1, :])
@@ -294,72 +331,138 @@
     mask_ref[...] = jnp.where(seg_t[:, 8:9] == seg[0:1, :], 0.0, NEG)
 
 
-def order_kernel(at_ref, *refs):
-    pieces, out_ref = refs[:-1], refs[-1]
+def order_kernel(at_ref, *refs, outs):
+    pieces, out_refs = refs[:-outs], refs[-outs:]
     for d, piece in enumerate(pieces):
         if piece.ndim == 2:
-            out_ref[at_ref[2] ^ d] = piece[...]
+            out_refs[0][at_ref[2] ^ d] = piece[...]
+            continue
+        begin = 0
+        for out_ref in out_refs:
+            size = out_ref.shape[0]
+            out_ref[:, at_ref[2] ^ d] = piece[begin : begin + size]
+            begin += size
+
+
+def read_part(refs, group):
+    if len(refs) == 1:
+        count, rows, cols = refs[0].shape
+        rows //= 4
+        part = pl.ds(pl.multiple_of(group * rows, 16), rows)
+        return refs[0][:, part, :].astype(f32).reshape(count * rows, cols)
+    fin, fout = refs
+    rows, rows_out = fin.shape[1] // 4, fout.shape[1] // 4
+    part = pl.ds(pl.multiple_of(group * rows, 16), rows)
+    part_out = pl.ds(pl.multiple_of(group * rows_out, 16), rows_out)
+    pieces = [
+        fin[i, part, at : at + TILE].astype(f32)
+        for i in range(fin.shape[0])
+        for at in range(0, fin.shape[2], TILE)
+    ]
+    pieces += [
+        fout[0, part_out, at : at + TILE].astype(f32) for at in range(0, fout.shape[2], TILE)
+    ]
+    return jnp.concatenate(pieces, axis=0)
+
+
+def spread_kernel(at_ref, *refs, count):
+    keeps, recvs = refs[:count], refs[count : 2 * count]
+    own_ref, kept_x, kept_y, to_x, to_y = refs[2 * count :]
+    half = own_ref.shape[0] // 2
+    for d in range(4):
+        total = read_part(keeps, at_ref[1] ^ d) + read_part(recvs, at_ref[1] ^ d)
+        if d == 0:
+            own_ref[...] = total
+        elif d == 1:
+            to_x[0] = total[:half].astype(bf16)
+            kept_x[...] = total[half:]
+        elif d == 2:
+            to_y[0] = total[half:].astype(bf16)
+            kept_y[...] = total[:half]
         else:
-            out_ref[:, at_ref[2] ^ d] = piece[...]
-
-
-def spread_kernel(at_ref, *refs, count):
-    for i in range(count):
-        keep_ref, recv_ref = refs[2 * i : 2 * i + 2]
-        rows = keep_ref.shape[1] // 4
-        for d in range(4):
-            part = pl.ds(pl.multiple_of((at_ref[1] ^ d) * rows, 16), rows)
-            out_ref = refs[2 * count + 4 * i + d]
-            total = keep_ref[:, part, :].astype(f32) + recv_ref[:, part, :].astype(f32)
-            out_ref[...] = total.astype(out_ref.dtype)
-
-
-def narrow_kernel(at_ref, *refs, count, narrow):
-    outs, scratch = refs[4 * count : (4 + narrow) * count], refs[(4 + narrow) * count :]
-    for i in range(count):
-        first, second, third, fourth = (ref[...].astype(f32) for ref in refs[4 * i : 4 * i + 4])
-        scratch[i][...] = (first + second) + (third + fourth)
-        rows = scratch[i].shape[1] // narrow
-        for d in range(narrow):
-            part = pl.ds(pl.multiple_of((at_ref[2] ^ d) * rows, 8), rows)
-            out_ref = outs[narrow * i + d]
-            out_ref[...] = scratch[i][:, part, :].astype(out_ref.dtype)
-
-
-def total_kernel(*refs, count, narrow):
-    for i in range(count):
-        total = refs[narrow * i][...]
-        for ref in refs[narrow * i + 1 : narrow * i + narrow]:
-            total = total + ref[...].astype(f32)
-        total_ref, rows_ref, cols_ref = refs[narrow * count + 3 * i : narrow * count + 3 * i + 3]
-        total_ref[...] = total
-        squares = total * total + 1e-30
+            to_x[1] = total[:half].astype(bf16)
+            to_y[1] = total[half:].astype(bf16)
+
+
+def middle_kernel(own_ref, kept_x, kept_y, from_x, from_y, sum_ref, to_x, to_y):
+    half = own_ref.shape[0] // 2
+    sum_ref[:half, :] = own_ref[:half, :] + from_x[0].astype(f32)
+    sum_ref[half:, :] = own_ref[half:, :] + from_y[0].astype(f32)
+    to_y[...] = (kept_y[...] + from_x[1].astype(f32)).astype(bf16)
+    to_x[...] = (kept_x[...] + from_y[1].astype(f32)).astype(bf16)
+
+
+def narrow_kernel(at_ref, own_ref, from_x, from_y, *refs, narrow, spots):
+    outs, sum_ref = refs[:-1], refs[-1]
+    half = own_ref.shape[0] // 2
+    sum_ref[:half, :] = own_ref[:half, :] + from_y[...].astype(f32)
+    sum_ref[half:, :] = own_ref[half:, :] + from_x[...].astype(f32)
+    for d, out_ref in enumerate(outs):
+        place = at_ref[2] ^ d
+        out_ref[...] = jnp.concatenate(
+            [
+                sum_ref[pl.ds(start + pl.multiple_of(place * rows, 8), rows), :]
+                for start, rows in spots
+            ],
+            axis=0,
+        ).astype(out_ref.dtype)
+
+
+def total_kernel(*refs, narrow):
+    total = refs[0][...]
+    for ref in refs[1:narrow]:
+        total = total + ref[...].astype(f32)
+    outs = refs[narrow:]
+    at = 0
+    for total_ref, rows_ref, cols_ref in zip(*(outs[i::3] for i in range(3))):
+        count, rows, cols = total_ref.shape
+        block = total.shape[1]
+        if cols == block:
+            total_ref[...] = total[at : at + count * rows].reshape(count, rows, cols)
+            at += count * rows
+        else:
+            for i in range(count):
+                for j in range(cols // block):
+                    total_ref[i, :, j * block : (j + 1) * block] = total[at : at + rows]
+                    at += rows
+        squares = total_ref[...]
+        squares = squares * squares + 1e-30
         rows_ref[...] = jnp.sum(squares, axis=-1, keepdims=True)
         cols_ref[...] = jnp.sum(squares, axis=1, keepdims=True)
 
 
-def ffn_kernel(at_ref, *refs, fold, narrow):
-    c_refs, refs = refs[:narrow], refs[narrow:]
-    (x2_ref, h_ref, g_ref, gate_ref, up_ref, wout_ref), refs = refs[:6], refs[6:]
+def ffn_kernel(at_ref, *refs, fold, narrow, pieces, first_out):
+    c_ref, refs = refs[0], refs[1:]
+    fin_refs, refs = refs[:pieces], refs[pieces:]
+    fout_refs, refs = refs[:pieces], refs[pieces:]
+    (x2_ref, h_ref, g_ref), refs = refs[:3], refs[3:]
     out_refs, refs = refs[:narrow], refs[narrow:]
     (dx_ref, dg_ref, kin_ref, sin_ref, kout_ref, sout_ref, acc_ref, dh_ref, turned_ref, ht_ref,
-     gout_ref, c_ref) = refs
+     gout_ref, fin_ref, fout_ref, fin_sems, fout_sems) = refs
     step, steps = pl.program_id(0), pl.num_programs(0)
     core = at_ref[0]
 
     @pl.when(step == 0)
     def _():
-        join_rows(at_ref[2], c_refs, c_ref)
+        copies = start_weights(at_ref[3], fin_refs, fin_ref, fin_sems, pl.ds(0, fin_ref.shape[0]))
+        copies += start_weights(
+            at_ref[3], fout_refs, fout_ref, fout_sems, pl.ds(first_out, fout_ref.shape[0])
+        )
         acc_ref[...] = x2_ref[...]
         dh_ref[...] = jnp.zeros_like(dh_ref)
         fold_rows(core, h_ref[...].T, turned_ref, ht_ref, fold)
+        for copy in copies:
+            copy.wait()
 
     hidden_in, cot = h_ref[...], c_ref[...]
-    for block in range(gate_ref.shape[0]):
-        size = gate_ref.shape[2]
+    size = fin_ref.shape[2]
+    blocks = gout_ref.shape[0] // size
+    for block in range(blocks):
         part = slice(block * size, (block + 1) * size)
-        gate = dot_nn(hidden_in, gate_ref[block])
-        up = dot_nn(hidden_in, up_ref[block])
+        at_gate = step * blocks + block
+        at_up = fin_ref.shape[0] // 2 + at_gate
+        gate = dot_nn(hidden_in, fin_ref[at_gate])
+        up = dot_nn(hidden_in, fin_ref[at_up])
         square = gate * gate
         bent = jnp.tanh(0.7978845608028654 * (gate + 0.044715 * square * gate))
         plus = 0.5 * (1.0 + bent)
@@ -368,12 +471,15 @@
             0.7978845608028654 + (3 * 0.044715 * 0.7978845608028654) * square
         )
         hidden = (act * up).astype(bf16)
-        down = jnp.concatenate([wout_ref[i, part, :] for i in range(wout_ref.shape[0])], axis=1)
+        down_rows = pl.ds(pl.multiple_of(at_gate * size, size), size)
+        down = jnp.concatenate(
+            [fout_ref[i, down_rows, :] for i in range(fout_ref.shape[0])], axis=1
+        )
         acc_ref[...] += dot_nn(hidden, down)
         grad = dot_nt(cot, down)
         d_gate = (grad * up * slope).astype(bf16)
         d_up = (grad * act).astype(bf16)
-        dh_ref[...] += dot_nt(d_gate, gate_ref[block]) + dot_nt(d_up, up_ref[block])
+        dh_ref[...] += dot_nt(d_gate, fin_ref[at_gate]) + dot_nt(d_up, fin_ref[at_up])
         half = ht_ref.shape[0] // 2
         for index, right in ((0, d_gate), (1, d_up)):
             product = dot_nn(ht_ref[...], right).astype(bf16)
@@ -394,74 +500,72 @@
         dg_ref[...] = d_gain
 
 
-def cross_back_kernel(at_ref, *refs, pieces, narrow, fold):
+def attend_back_kernel(at_ref, *refs, pieces, which, causal):
     w_refs, refs = refs[:pieces], refs[pieces:]
-    (dx2_ref, o_ref, h_ref, m_ref, x1_ref, o1_ref, qkv_ref, extra_ref, g_ref, peak_ref,
-     inv_ref), refs = refs[:11], refs[11:]
-    gm_refs, refs = refs[:narrow], refs[narrow:]
-    (dx1_ref, dg_ref, keep_ref, send_ref, do_ref, dqkv_ref, dsum_ref, p_ref, ds_ref, dqt_ref,
-     turned_ref, left_ref, gm_ref, w_ref, sems) = refs
-    core = at_ref[0]
-    copies = start_weights(at_ref[3], w_refs, w_ref, sems)
-    branch = dx2_ref[...].astype(bf16)
+    table_ref = None
+    if causal:
+        table_ref, refs = refs[0], refs[1:]
+    dx_ref, o_ref, qkv_ref, extra_ref, peak_ref, inv_ref, dqkv_ref = refs[:7]
+    ds_out, refs = (refs[7], refs[8:]) if causal else (None, refs[7:])
+    do_ref, dsum_ref, p_ref, ds_ref, dqt_ref, w_ref, sems = refs
+    copies = start_weights(at_ref[3], w_refs, w_ref, sems, pl.ds(which, 1))
+    branch = dx_ref[...].astype(bf16)
     for copy in copies:
         copy.wait()
     for start, size in tiles_of(o_ref.shape[1]):
         do_ref[:, start : start + size] = dot_nt(
-            branch, w_ref[4, start : start + size, :]
+            branch, w_ref[0, start : start + size, :]
         ).astype(bf16)
     head_sums(do_ref[...], o_ref[...], dsum_ref)
+    attend_back(qkv_ref, extra_ref, table_ref, do_ref, dsum_ref, peak_ref, inv_ref, dqkv_ref,
+                p_ref, ds_ref, dqt_ref, ds_out)
+
+
+def second_back_kernel(at_ref, *refs, pieces, narrow, fold):
+    w_refs, refs = refs[:pieces], refs[pieces:]
+    (dqkv_ref, dx2_ref, o_ref, h_ref, m_ref, x1_ref, o1_ref, g_ref), refs = refs[:8], refs[8:]
+    gm_refs, refs = refs[:narrow], refs[narrow:]
+    (dx1_ref, dg_ref, keep_ref, send_ref, turned_ref, left_ref, gm_ref, w_ref, sems) = refs
+    core = at_ref[0]
+    copies = start_weights(at_ref[3], w_refs, w_ref, sems, pl.ds(1, 3))
+    gm_ref[...] = dx2_ref[...].astype(bf16)
     fold_rows(core, o_ref[...].T, turned_ref, left_ref, fold)
-    weight_grad(left_ref, branch, keep_ref, send_ref, 4)
-    attend_back(qkv_ref, extra_ref, None, do_ref, dsum_ref, peak_ref, inv_ref, dqkv_ref, p_ref,
-                ds_ref, dqt_ref, None)
+    for copy in copies:
+        copy.wait()
+    weight_grad(left_ref, gm_ref, keep_ref, send_ref, 4)
     fold_rows(core, h_ref[...].T, turned_ref, left_ref, fold)
-    weight_grad(left_ref, dqkv_ref[0], keep_ref, send_ref, 1)
+    weight_grad(left_ref, dqkv_ref.at[0], keep_ref, send_ref, 1)
     fold_rows(core, m_ref[...].T, turned_ref, left_ref, fold)
     for i in (1, 2):
-        weight_grad(left_ref, dqkv_ref[i], keep_ref, send_ref, i + 1)
+        weight_grad(left_ref, dqkv_ref.at[i], keep_ref, send_ref, i + 1)
     for start, size in tiles_of(o_ref.shape[1]):
         rows = slice(start, start + size)
         gm_ref[:, rows] = (
-            dot_nt(dqkv_ref[1], w_ref[2, rows, :]) + dot_nt(dqkv_ref[2], w_ref[3, rows, :])
+            dot_nt(dqkv_ref[1], w_ref[1, rows, :]) + dot_nt(dqkv_ref[2], w_ref[2, rows, :])
         ).astype(bf16)
-        dx1_ref[:, rows] = dot_nt(dqkv_ref[0], w_ref[1, rows, :])
+        dx1_ref[:, rows] = dot_nt(dqkv_ref[0], w_ref[0, rows, :])
     split_rows(at_ref[2], gm_ref, gm_refs)
     back, d_gain = norm_back(dx1_ref[...], x1_ref[...], g_ref[1:2, :])
     d_x1 = dx2_ref[...] + back
     dx1_ref[...] = d_x1
     dg_ref[...] = d_gain
+    gm_ref[...] = d_x1.astype(bf16)
     fold_rows(core, o1_ref[...].T, turned_ref, left_ref, fold)
-    weight_grad(left_ref, d_x1.astype(bf16), keep_ref, send_ref, 0)
-
-
-def self_back_kernel(at_ref, *refs, pieces, narrow, fold):
+    weight_grad(left_ref, gm_ref, keep_ref, send_ref, 0)
+
+
+def first_back_kernel(at_ref, *refs, pieces, narrow, fold):
     w_refs, refs = refs[:pieces], refs[pieces:]
-    wo_refs, refs = refs[:pieces], refs[pieces:]
-    (dx1_ref, o_ref, h_ref, x_ref, qkv_ref, extra_ref, table_ref, g_ref, peak_ref,
-     inv_ref), refs = refs[:10], refs[10:]
+    (dqkv_ref, h_ref, dx1_ref, x_ref, g_ref), refs = refs[:5], refs[5:]
     gx_refs, refs = refs[:narrow], refs[narrow:]
-    (dg_ref, keep_ref, send_ref, ds_out, do_ref, dqkv_ref, dsum_ref, p_ref, ds_ref, dqt_ref,
-     turned_ref, left_ref, dh_ref, w_ref, wo_ref, sems, wo_sems) = refs
-    core = at_ref[0]
-    wo_copies = start_weights(at_ref[3], wo_refs, wo_ref, wo_sems, pl.ds(0, 1))
+    dg_ref, keep_ref, send_ref, turned_ref, left_ref, dh_ref, w_ref, sems = refs
     copies = start_weights(at_ref[3], w_refs, w_ref, sems, pl.ds(0, 3))
-    branch = dx1_ref[...].astype(bf16)
-    for copy in wo_copies:
-        copy.wait()
-    for start, size in tiles_of(o_ref.shape[1]):
-        do_ref[:, start : start + size] = dot_nt(
-            branch, wo_ref[0, start : start + size, :]
-        ).astype(bf16)
-    head_sums(do_ref[...], o_ref[...], dsum_ref)
-    attend_back(qkv_ref, extra_ref, table_ref, do_ref, dsum_ref, peak_ref, inv_ref, dqkv_ref,
-                p_ref, ds_ref, dqt_ref, ds_out)
-    fold_rows(core, h_ref[...].T, turned_ref, left_ref, fold)
-    for i in range(3):
-        weight_grad(left_ref, dqkv_ref[i], keep_ref, send_ref, i)
+    fold_rows(at_ref[0], h_ref[...].T, turned_ref, left_ref, fold)
     for copy in copies:
         copy.wait()
-    for start, size in tiles_of(o_ref.shape[1]):
+    for i in range(3):
+        weight_grad(left_ref, dqkv_ref.at[i], keep_ref, send_ref, i)
+    for start, size in tiles_of(h_ref.shape[1]):
         rows = slice(start, start + size)
         dh_ref[:, rows] = (
             dot_nt(dqkv_ref[0], w_ref[0, rows, :])
@@ -505,20 +609,38 @@
     )
 
 
-def call(kernel, outs, scratch, limit, *args, scalars=1, loose=(), flops=0):
+def cost_of(us):
+    return pl.CostEstimate(flops=int(us * 1.15e9), bytes_accessed=MIB, transcendentals=0)
+
+
+def room_for(arrays, scratch):
+    size = sum(v.size * v.dtype.itemsize for v in arrays)
+    for ref in scratch:
+        shape = getattr(ref, "shape", ())
+        if ref.memory_space == pltpu.VMEM:
+            rows = -(-shape[-2] // 8) * 8
+            size += math.prod(shape[:-2]) * rows * shape[-1] * jnp.dtype(ref.dtype).itemsize
+    return (size // MIB + 8) * MIB
+
+
+def call(kernel, outs, scratch, *args, scalars=1, loose=(), us=2, name=None):
     spaces = [
         pltpu.SMEM if i < scalars else pl.ANY if i in loose else pltpu.VMEM
         for i in range(len(args))
     ]
-    moved = sum(a.size * a.dtype.itemsize for a in (*args, *outs))
     return pl.pallas_call(
         kernel,
         out_shape=outs,
         in_specs=[pl.BlockSpec(memory_space=space) for space in spaces],
         out_specs=[pl.BlockSpec(memory_space=pltpu.VMEM)] * len(outs),
         scratch_shapes=scratch,
-        compiler_params=pltpu.CompilerParams(vmem_limit_bytes=limit * MIB),
-        cost_estimate=pl.CostEstimate(flops=flops, bytes_accessed=moved, transcendentals=0),
+        compiler_params=pltpu.CompilerParams(
+            vmem_limit_bytes=room_for(
+                [v for v, space in zip(args, spaces) if space == pltpu.VMEM] + list(outs), scratch
+            )
+        ),
+        cost_estimate=cost_of(us),
+        name=name,
     )(*args)
 
 
@@ -536,24 +658,20 @@
     return lax.ppermute(value, BOTH, pairs)
 
 
-def ordered(at, pieces):
+def after(value, *done):
+    return lax.optimization_barrier((value, *done))[0]
+
+
+def ordered(at, pieces, shares=None):
     first = pieces[0]
     if first.ndim == 2:
-        shape = (len(pieces),) + first.shape
+        shapes = [(len(pieces),) + first.shape]
     else:
-        shape = first.shape[:1] + (len(pieces),) + first.shape[1:]
-    return call(order_kernel, [shape_of(shape, first.dtype)], [], 16, at, *pieces)[0]
-
-
-def gathered(at, local, fast):
-    if not fast:
-        return [lax.all_gather(local, BOTH, axis=1, tiled=True)]
-    narrow = lax.axis_size("narrow")
-    near = [local] + [permuted(local, 0, d) for d in range(1, narrow)]
-    stack = ordered(at, near)
-    stack = stack.reshape(stack.shape[0], -1, stack.shape[3])
-    plane = [stack] + [permuted(stack, 2 * d, 0) for d in range(1, 4)]
-    return [piece for part in plane for piece in (part, permuted(part, 1, 0))]
+        shapes = [(k, len(pieces)) + first.shape[1:] for k in shares]
+    outs = [shape_of(shape, first.dtype) for shape in shapes]
+    return call(
+        functools.partial(order_kernel, outs=len(outs)), outs, [], at, *pieces, us=1, name="order"
+    )
 
 
 def local_stats(gradient):
@@ -561,53 +679,95 @@
     return (jnp.sum(squares, axis=-1), jnp.sum(squares, axis=-2))
 
 
-def scattered(at, pairs, fast, narrow):
-    if not fast:
-        results = []
-        for keep, send in pairs:
-            whole = jnp.concatenate([keep, send], axis=1)
-            if keep.shape[0] == 4:
-                whole = whole.reshape(1, -1, whole.shape[2])
-            total = lax.psum_scatter(whole, BOTH, scatter_dimension=1, tiled=True).astype(f32)
-            results.append((total, *local_stats(total)))
-        return results
-    count = len(pairs)
-    keeps, sends = [], []
-    for keep, send in pairs:
-        stack = 1 if keep.shape[0] == 4 else keep.shape[0]
-        keeps.append(keep.reshape(stack, -1, keep.shape[2]))
-        sends.append(send.reshape(keeps[-1].shape))
-    flat = [v for keep, send in zip(keeps, sends) for v in (keep, permuted(send, 1, 0))]
-    outs = [
-        shape_of((k.shape[0], k.shape[1] // 4, k.shape[2]), bf16 if d else f32)
-        for k in keeps
-        for d in range(4)
-    ]
-    parts = call(functools.partial(spread_kernel, count=count), outs, [], 40, at, *flat)
-    parts = [permuted(v, 2 * (i % 4), 0) if i % 4 else v for i, v in enumerate(parts)]
-    wholes = [(k.shape[0], k.shape[1] // 4, k.shape[2]) for k in keeps]
-    outs = [
-        shape_of((k, rows // narrow, cols), bf16 if d else f32)
-        for k, rows, cols in wholes
-        for d in range(narrow)
-    ]
-    parts = call(
-        functools.partial(narrow_kernel, count=count, narrow=narrow),
-        outs, [pltpu.VMEM(shape, f32) for shape in wholes], 32, at, *parts,
-    )
-    parts = [permuted(v, 0, i % narrow) if i % narrow else v for i, v in enumerate(parts)]
-    outs = []
-    for k, rows, cols in wholes:
-        rows //= narrow
-        outs += [
-            shape_of((k, rows, cols), f32), shape_of((k, rows, 1), f32), shape_of((k, 1, cols), f32)
+class Scatter:
+    def __init__(self, at, pairs, fast, narrow):
+        self.at, self.fast, self.narrow, self.pairs = at, fast, narrow, pairs
+        if not fast:
+            return
+        keeps = [keep.reshape(-1, keep.shape[1], keep.shape[2]) for keep, _ in pairs]
+        sends = [send for _, send in pairs]
+        if len(pairs) == 2:
+            keeps[1] = keeps[1].reshape(1, -1, keeps[1].shape[2])
+            sends[1] = sends[1].reshape(keeps[1].shape)
+        self.shapes = [(k.shape[0], k.shape[1] // 4, k.shape[2]) for k in keeps]
+        size = sum(k.size for k in keeps) // 4
+        cols = TILE if len(pairs) == 2 else keeps[0].shape[2]
+        self.rows, self.cols = size // cols, cols
+        half = (self.rows // 2, cols)
+        recvs = [permuted(send, 1, 0) for send in sends]
+        self.own, self.kept_x, self.kept_y, to_x, to_y = call(
+            functools.partial(spread_kernel, count=len(pairs)),
+            [shape_of((self.rows, cols), f32), shape_of(half, f32), shape_of(half, f32),
+             shape_of((2,) + half, bf16), shape_of((2,) + half, bf16)],
+            [], at, *keeps, *recvs, us=3, name="spread",
+        )
+        self.out = (to_x, to_y)
+        self.done = self.own
+
+    def middle(self, *done):
+        if not self.fast:
+            return
+        self.own = after(self.own, *done)
+        half = (self.rows // 2, self.cols)
+        from_x, from_y = permuted(self.out[0], 2, 0), permuted(self.out[1], 4, 0)
+        self.own, to_x, to_y = call(
+            middle_kernel,
+            [shape_of((self.rows, self.cols), f32), shape_of(half, bf16), shape_of(half, bf16)],
+            [], self.own, self.kept_x, self.kept_y, from_x, from_y, scalars=0, name="middle",
+        )
+        self.out = (to_x, to_y)
+        self.done = self.own
+
+    def narrowed(self, *done):
+        if not self.fast:
+            return
+        self.own = after(self.own, *done)
+        from_x, from_y = permuted(self.out[0], 2, 0), permuted(self.out[1], 4, 0)
+        if len(self.shapes) == 2:
+            (k, rows, cols), (_, rows_out, cols_out) = self.shapes
+            sizes = [rows] * (k * cols // TILE) + [rows_out] * (cols_out // TILE)
+        else:
+            sizes = [self.shapes[0][1]] * self.shapes[0][0]
+        spots, begin = [], 0
+        for size in sizes:
+            spots.append((begin, size // self.narrow))
+            begin += size
+        share = (self.rows // self.narrow, self.cols)
+        self.out = call(
+            functools.partial(narrow_kernel, narrow=self.narrow, spots=spots),
+            [shape_of(share, bf16 if d else f32) for d in range(self.narrow)],
+            [pltpu.VMEM((self.rows, self.cols), f32)], self.at, self.own, from_x, from_y,
+            name="narrow",
+        )
+        self.done = self.out[0]
+
+    def total(self, *done):
+        if not self.fast:
+            results = []
+            for keep, send in self.pairs:
+                whole = jnp.concatenate([keep, send], axis=1)
+                if keep.shape[0] == 4:
+                    whole = whole.reshape(1, -1, whole.shape[2])
+                total = lax.psum_scatter(whole, BOTH, scatter_dimension=1, tiled=True).astype(f32)
+                results.append((total, *local_stats(total)))
+            return results
+        parts = [permuted(v, 0, d) if d else v for d, v in enumerate(self.out)]
+        parts[0] = after(parts[0], *done)
+        outs = []
+        for k, rows, cols in self.shapes:
+            rows //= self.narrow
+            outs += [
+                shape_of((k, rows, cols), f32), shape_of((k, rows, 1), f32),
+                shape_of((k, 1, cols), f32),
+            ]
+        flat = call(
+            functools.partial(total_kernel, narrow=self.narrow), outs, [], *parts, scalars=0,
+            name="total",
+        )
+        return [
+            (flat[3 * i], flat[3 * i + 1][:, :, 0], flat[3 * i + 2][:, 0])
+            for i in range(len(self.shapes))
         ]
-    flat = call(
-        functools.partial(total_kernel, count=count, narrow=narrow), outs, [], 16, *parts, scalars=0
-    )
-    return [
-        (flat[3 * i], flat[3 * i + 1][:, :, 0], flat[3 * i + 2][:, 0]) for i in range(count)
-    ]
 
 
 def summed_all(parts, fast):
@@ -648,65 +808,86 @@
     tokens = local_tokens * narrow
     assert targets.shape[0] == narrow
 
-    def row_pieces(stacked):
-        return [
-            permuted(lax.dynamic_index_in_dim(stacked, at_narrow ^ d, 0, False), 0, d)
-            if d
-            else lax.dynamic_index_in_dim(stacked, at_narrow, 0, False)
-            for d in range(narrow)
-        ]
-
-    def to_owners(pieces):
-        return ordered(at, [permuted(v, 0, d) if d else v for d, v in enumerate(pieces)])
-
-    x_pieces = row_pieces(targets)
+    def over_narrow(pieces):
+        return [permuted(v, 0, d) if d else v for d, v in enumerate(pieces)]
+
+    def to_owners(pieces, *done):
+        pieces = over_narrow(pieces)
+        return ordered(at, [after(pieces[0], *done)] + pieces[1:])[0]
+
     device = at_wide * narrow + at_narrow
     gain_rows = lax.dynamic_update_slice(
         jnp.zeros((chunk, width), bf16), gains.astype(bf16), (0, device * chunk)
     )
-    w_first = gathered(at, jnp.concatenate([attn_in[:3].astype(bf16), gain_rows[None]]), fast)
-    segments = jnp.concatenate([target_segments, memory_segments], axis=1).astype(bf16)
-    segments = jnp.pad(segments, ((0, 0), (0, buckets.shape[1] - segments.shape[1])))
-    near = jnp.concatenate(
+    local_weights = jnp.concatenate(
         [
-            jnp.broadcast_to(buckets.astype(bf16)[None], (narrow,) + buckets.shape),
-            jnp.broadcast_to(segments[:, None], (narrow, 16, buckets.shape[1])),
-        ],
-        axis=1,
-    )
-    index, cross_mask = call(
-        functools.partial(prepare_kernel, narrow=narrow, bucket_count=bucket_count),
-        [shape_of((tokens, tokens), jnp.int32), shape_of((tokens, tokens), f32)],
-        [pltpu.VMEM((16, tokens), f32), pltpu.VMEM((tokens, tokens), f32)],
-        24, at, *row_pieces(near),
-    )
-    table = jnp.concatenate(
-        [bias_table.T, jnp.full((heads, 128 - bucket_count), NEG, f32)], axis=1
-    )
-    m_pieces = row_pieces(memory)
-    w_second = gathered(
-        at, jnp.concatenate([attn_out[:1], attn_in[3:], attn_out[1:]]).astype(bf16), fast
-    )
-    c_pieces = row_pieces(cotangent)
+            attn_in[:3].astype(bf16), gain_rows[None], attn_out[:1].astype(bf16),
+            attn_in[3:].astype(bf16), attn_out[1:].astype(bf16),
+        ]
+    )
+    piece16 = shape_of((local_tokens, width), bf16)
+    near_rows = local_tokens * (width + tokens) // TILE + 16
+    packed = call(
+        functools.partial(pack_kernel, narrow=narrow),
+        [shape_of((near_rows, TILE), bf16)] * narrow
+        + [shape_of((2, local_tokens, width), bf16)] * narrow,
+        [], at, targets, memory, cotangent, buckets, target_segments, memory_segments,
+        us=4, name="pack",
+    )
+    near, later = packed[:narrow], packed[narrow:]
     lanes = TILE
     fin_blocks = ff_in.astype(bf16).reshape(2, chunk, ff_width // lanes, lanes)
     fin_blocks = fin_blocks.transpose(0, 2, 1, 3).reshape(-1, chunk, lanes)
     out_rows_here = ff_out.shape[0]
     fout_blocks = ff_out.astype(bf16).reshape(out_rows_here, width // lanes, lanes)
     fout_blocks = fout_blocks.transpose(1, 0, 2).reshape(-1, chunk, lanes)
-    w_ffn = lax.all_gather(
-        jnp.concatenate([fin_blocks, fout_blocks]), BOTH, axis=1, tiled=True
-    )
-    w_fout = w_ffn[fin_blocks.shape[0] :].reshape(-1, wide * narrow, chunk, lanes)
-    w_fout = w_fout.transpose(1, 0, 2, 3).reshape(wide * narrow, -1, out_rows_here, lanes)
-    w_fout = w_fout.transpose(1, 0, 2, 3).reshape(-1, ff_width, lanes)
-
+    fin_count, fout_count = fin_blocks.shape[0], fout_blocks.shape[0]
+    ffn_local = jnp.concatenate([fin_blocks, fout_blocks])
+
+    def regroup_out(stack, owners):
+        stack = stack.reshape(fout_count, owners, chunk, lanes).transpose(1, 0, 2, 3)
+        stack = stack.reshape(owners, width // lanes, out_rows_here, lanes)
+        return stack.transpose(1, 0, 2, 3).reshape(width // lanes, -1, lanes)
+
+    def over_plane(stack):
+        return [stack] + [permuted(stack, 2 * d, 0) for d in range(1, 4)]
+
+    def with_other_core(plane, *done):
+        return [
+            piece for part in plane for piece in (part, permuted(after(part, *done), 1, 0))
+        ]
+
+    if fast:
+        stacks = ordered(at, over_narrow([local_weights] * narrow), (4, 5))
+        stacks = [v.reshape(v.shape[0], -1, width) for v in stacks]
+        near = [near[0]] + [after(v, stacks[0]) for v in near[1:]]
+        plane_first = over_plane(stacks[0])
+        w_first = with_other_core(plane_first)
+        plane_second = over_plane(after(stacks[1], *plane_first[1:]))
+    else:
+        every = lax.all_gather(local_weights, BOTH, axis=1, tiled=True)
+        w_first, w_second = [every[:4]], [every[4:]]
+    near = over_narrow(near)
+    index, cross_mask = call(
+        functools.partial(
+            prepare_kernel, narrow=narrow, bucket_count=bucket_count,
+            skip=local_tokens * width // TILE,
+        ),
+        [shape_of((tokens, tokens), jnp.int32), shape_of((tokens, tokens), f32)],
+        [pltpu.VMEM((16, tokens), f32), pltpu.VMEM((tokens, tokens), f32)],
+        at, *near, us=3, name="prepare",
+    )
+    if fast:
+        ffn_local = after(ffn_local, index)
+        ffn_near = over_narrow([ffn_local] * narrow)
+    table = jnp.concatenate(
+        [bias_table.T, jnp.full((heads, 128 - bucket_count), NEG, f32)], axis=1
+    )
     row16 = shape_of((tokens, width), bf16)
     row32 = shape_of((tokens, width), f32)
     three = shape_of((3, tokens, width), bf16)
     stat = shape_of((heads, 1, tokens), f32)
     gain_out = shape_of((1, width), f32)
-    piece16 = shape_of((local_tokens, width), bf16)
     pair_t = pltpu.VMEM((128, tokens), f32)
     pieces = len(w_first)
     weights = lambda count: pltpu.VMEM((count, width, width), bf16)
@@ -714,34 +895,50 @@
     g, x, h1, qkv1, o1, peak1, inv1 = call(
         functools.partial(first_kernel, pieces=pieces, narrow=narrow, chunk=chunk),
         [shape_of((8, width), f32), row16, row16, three, row16, stat, stat],
-        [pair_t, weights(4), sems], 48,
-        at, *x_pieces, *w_first, index, table,
-        loose=range(1 + narrow, 1 + narrow + pieces),
-    )
-    m, x1, h2, qkv2, o2, x2, h3, peak2, inv2 = call(
+        [pair_t, weights(4), sems],
+        at, *near, *w_first, index, table,
+        loose=range(1 + narrow, 1 + narrow + pieces), us=16, name="first",
+    )
+    if fast:
+        w_second = with_other_core(plane_second, h1)
+        ffn_near[0] = after(ffn_near[0], h1)
+        (stack,) = ordered(at, ffn_near, (fin_count + fout_count,))
+        stack = stack.reshape(fin_count + fout_count, -1, lanes)
+        stack_out = regroup_out(stack[fin_count:], narrow).reshape(fout_count, -1, lanes)
+        stack = jnp.concatenate([stack[:fin_count], stack_out])
+        later = [later[0]] + [after(v, stack) for v in later[1:]]
+        plane_ffn = over_plane(after(stack, *plane_second[1:]))
+        o1 = after(o1, plane_ffn[1], plane_ffn[2])
+    later = over_narrow(later)
+    m, c, x1, h2, qkv2, o2, x2, h3, peak2, inv2 = call(
         functools.partial(second_kernel, pieces=pieces, narrow=narrow),
-        [row16, row32, row16, three, row16, row32, row16, stat, stat],
-        [pair_t, weights(5), sems], 48,
-        at, *m_pieces, *w_second, x, o1, cross_mask, g,
-        loose=range(1 + narrow, 1 + narrow + pieces),
-    )
-
+        [row16, row16, row32, row16, three, row16, row32, row16, stat, stat],
+        [pair_t, weights(5), sems],
+        at, *later, *w_second, x, o1, cross_mask, g,
+        loose=range(1 + narrow, 1 + narrow + pieces), us=21, name="second",
+    )
+
+    if fast:
+        ffn_pieces = with_other_core(plane_ffn, x2)
+        w_fin = ffn_pieces
+        w_fout = [v.reshape(-1, narrow * out_rows_here, lanes) for v in ffn_pieces]
+    else:
+        every = lax.all_gather(ffn_local, BOTH, axis=1, tiled=True)
+        w_fin, w_fout = [every], [regroup_out(every[fin_count:], wide * narrow)]
     steps = 4
     part = ff_width // steps
-    blocks = part // lanes
     half = width // 2
     whole = lambda shape: pl.BlockSpec(shape, lambda i: (0,) * len(shape))
     outs = pl.pallas_call(
-        functools.partial(ffn_kernel, fold=fast, narrow=narrow),
+        functools.partial(
+            ffn_kernel, fold=fast, narrow=narrow, pieces=pieces,
+            first_out=w_fout[0].shape[0] - width // lanes,
+        ),
         grid=(steps,),
         in_specs=[pl.BlockSpec(memory_space=pltpu.SMEM)]
-        + [whole((local_tokens, width))] * narrow
-        + [
-            whole((tokens, width)), whole((tokens, width)), whole((8, width)),
-            pl.BlockSpec((blocks, width, lanes), lambda i: (i, 0, 0)),
-            pl.BlockSpec((blocks, width, lanes), lambda i: (i + steps, 0, 0)),
-            pl.BlockSpec((width // lanes, part, lanes), lambda i: (0, i, 0)),
-        ],
+        + [whole((tokens, width))]
+        + [pl.BlockSpec(memory_space=pl.ANY)] * (2 * pieces)
+        + [whole((tokens, width)), whole((tokens, width)), whole((8, width))],
         out_specs=[whole((local_tokens, width))] * narrow
         + [
             whole((tokens, width)), whole((1, width)),
@@ -759,57 +956,92 @@
         scratch_shapes=[
             pltpu.VMEM((tokens, width), f32), pltpu.VMEM((tokens, width), f32),
             pltpu.VMEM((width, tokens), bf16), pltpu.VMEM((width, tokens), bf16),
-            pltpu.VMEM((part, width), bf16), pltpu.VMEM((tokens, width), bf16),
+            pltpu.VMEM((part, width), bf16),
+            pltpu.VMEM((fin_count, width, lanes), bf16),
+            pltpu.VMEM((width // lanes, ff_width, lanes), bf16), sems, sems,
         ],
-        compiler_params=pltpu.CompilerParams(vmem_limit_bytes=48 * MIB),
-        cost_estimate=pl.CostEstimate(
-            flops=18 * tokens * width * ff_width, bytes_accessed=20 * MIB, transcendentals=0
-        ),
-    )(at, *c_pieces, x2, h3, g, w_ffn, w_ffn, w_fout)
-    output = to_owners(outs[:narrow])
+        compiler_params=pltpu.CompilerParams(vmem_limit_bytes=40 * MIB),
+        cost_estimate=cost_of(24),
+        name="ffn",
+    )(at, c, *w_fin, *w_fout, x2, h3, g)
+    out_pieces = outs[:narrow]
     dx2, gain3, keep_fin, send_fin, keep_fout, send_fout = outs[narrow:]
-    (sum_fin, fin_rows, fin_part), (sum_fout, fout_rows, fout_part) = scattered(
-        at, [(keep_fin, send_fin), (keep_fout, send_fout)], fast, narrow
-    )
-
+    ffn_sum = Scatter(at, [(keep_fin, send_fin), (keep_fout, send_fout)], fast, narrow)
+    if fast:
+        dx2 = after(dx2, ffn_sum.done)
     square = pltpu.VMEM((tokens, tokens), bf16)
-    back_scratch = [
-        pltpu.VMEM((tokens, width), bf16), pltpu.VMEM((3, tokens, width), bf16),
-        pltpu.VMEM((heads, 1, tokens), f32), square, square, pair_t,
-        pltpu.VMEM((width, tokens), bf16), pltpu.VMEM((width, tokens), bf16),
+    attend_scratch = [
+        pltpu.VMEM((tokens, width), bf16), pltpu.VMEM((heads, 1, tokens), f32), square, square,
+        pair_t, weights(1), sems,
     ]
+    turned = pltpu.VMEM((width, tokens), bf16)
     grads = lambda count: shape_of((count, half, width), bf16)
+    (dqkv2,) = call(
+        functools.partial(attend_back_kernel, pieces=pieces, which=4, causal=False),
+        [three], attend_scratch,
+        at, *w_second, dx2, o2, qkv2, cross_mask, peak2, inv2,
+        loose=range(1, 1 + pieces), us=18, name="cross_back",
+    )
+    output = to_owners(out_pieces, dqkv2)
+    ffn_sum.middle(dqkv2)
+    if fast:
+        dqkv2 = after(dqkv2, ffn_sum.done, output)
     outs = call(
-        functools.partial(cross_back_kernel, pieces=pieces, narrow=narrow, fold=fast),
+        functools.partial(second_back_kernel, pieces=pieces, narrow=narrow, fold=fast),
         [piece16] * narrow + [row32, gain_out, grads(5), grads(5)],
-        back_scratch + [pltpu.VMEM((tokens, width), bf16), weights(5), sems], 52,
-        at, *w_second, dx2, o2, h2, m, x1, o1, qkv2, cross_mask, g, peak2, inv2,
-        loose=range(1, 1 + pieces),
-    )
-    grad_memory = to_owners(outs[:narrow])
+        [turned, turned, pltpu.VMEM((tokens, width), bf16), weights(3), sems],
+        at, *w_second, dqkv2, dx2, o2, h2, m, x1, o1, g,
+        loose=range(1, 1 + pieces), us=12, name="second_back",
+    )
+    gm_pieces = outs[:narrow]
     dx1, gain2, keep_second, send_second = outs[narrow:]
-    ((sum_second, second_rows, second_part),) = scattered(
-        at, [(keep_second, send_second)], fast, narrow
-    )
+    ffn_sum.narrowed(gain2)
+    if fast:
+        send_second = after(send_second, ffn_sum.done)
+    second_sum = Scatter(at, [(keep_second, send_second)], fast, narrow)
+    if fast:
+        dx1 = after(dx1, second_sum.done, ffn_sum.done)
+    dqkv1, ds = call(
+        functools.partial(attend_back_kernel, pieces=pieces, which=0, causal=True),
+        [three, shape_of((heads, tokens, tokens), bf16)], attend_scratch,
+        at, *w_second, table, dx1, o1, qkv1, index, peak1, inv1,
+        loose=range(1, 1 + pieces), us=20, name="self_back",
+    )
+    (sum_fin, fin_rows, fin_part), (sum_fout, fout_rows, fout_part) = ffn_sum.total(dqkv1)
+    second_sum.middle(dqkv1)
+    if fast:
+        dqkv1 = after(dqkv1, sum_fin, second_sum.done)
     outs = call(
-        functools.partial(self_back_kernel, pieces=pieces, narrow=narrow, fold=fast),
-        [piece16] * narrow
-        + [gain_out, grads(3), grads(3), shape_of((heads, tokens, tokens), bf16)],
-        back_scratch + [pltpu.VMEM((tokens, width), f32), weights(3), weights(1), sems, sems], 60,
-        at, *w_first, *w_second, dx1, o1, h1, x, qkv1, index, table, g, peak1, inv1,
-        loose=range(1, 1 + 2 * pieces),
-    )
-    grad_targets = to_owners(outs[:narrow])
-    gain1, keep_first, send_first, ds = outs[narrow:]
-    ((sum_first, first_rows, first_part),) = scattered(
-        at, [(keep_first, send_first)], fast, narrow
-    )
+        functools.partial(first_back_kernel, pieces=pieces, narrow=narrow, fold=fast),
+        [piece16] * narrow + [gain_out, grads(3), grads(3)],
+        [turned, turned, pltpu.VMEM((tokens, width), f32), weights(3), sems],
+        at, *w_first, dqkv1, h1, dx1, x, g,
+        loose=range(1, 1 + pieces), us=9, name="first_back",
+    )
+    gx_pieces = outs[:narrow]
+    gain1, keep_first, send_first = outs[narrow:]
+    grad_memory = to_owners(gm_pieces, gain1)
+    second_sum.narrowed(gain1, grad_memory)
+    if fast:
+        send_first = after(send_first, second_sum.done)
+    first_sum = Scatter(at, [(keep_first, send_first)], fast, narrow)
+    if fast:
+        ds = after(ds, first_sum.done, second_sum.done, grad_memory)
     (table_part,) = call(
         functools.partial(table_kernel, buckets=bucket_count),
         [shape_of((heads, 128), f32)],
-        [pltpu.VMEM((heads * 16, bucket_count * 16), f32)], 32, ds, index, scalars=0,
-    )
+        [pltpu.VMEM((heads * 16, bucket_count * 16), f32)], ds, index, scalars=0, us=11,
+        name="table",
+    )
+    first_sum.middle(table_part)
+    ((sum_second, second_rows, second_part),) = second_sum.total(table_part)
+    if fast:
+        gx_pieces = [after(v, sum_second) for v in gx_pieces]
+    grad_targets = to_owners(gx_pieces)
+    first_sum.narrowed()
+    ((sum_first, first_rows, first_part),) = first_sum.total()
     table_part = table_part[:, :bucket_count].T
+
 
     def regroup(first, second):
         return jnp.concatenate([first, second[1:4]]), jnp.stack([second[0], second[4]])

time: 587 us -> 446 us (0.76)
  waiting for transfers between devices: 205 us -> 161 us
  local copies, waits for them, and re-layouts: 75.1 us -> 39 us
  Pallas kernels: 154 us -> 130 us
  starting transfers between devices: 107 us -> 88 us
  between operations: 16.7 us -> 3.95 us
    ppermute x75 -> x73, waiting for transfers between devices: 205 us -> 161 us  [permuted(): return lax.ppermute(value, BOTH, pairs)]
    unnamed x274 -> x229, local copies, waits for them, and re-layouts: 57.6 us -> 31.9 us
    pallas_call x20 -> x26, Pallas kernels: 130 us -> 107 us  [call(): pl.pallas_call(kernel, out_shape=outs, in_specs=[pl.BlockSpec(memory_spac...]
    ppermute x75 -> x73, starting transfers between devices: 107 us -> 88 us  [permuted(): return lax.ppermute(value, BOTH, pairs)]
  transfers between devices with their start and end apart: 76 -> 73, of which waited for: 25 -> 34; matrix products, arithmetic and copies ran while one was open for 3% -> 2% of each run, Pallas kernels for 17% -> 24%
where the time goes in v3:
time: 446 us; the launch traced here: 438 us
  waiting for transfers between devices  161 us (36%)
  Pallas kernels  130 us (29%)
  starting transfers between devices  88 us (20%)
  local copies, waits for them, and re-layouts  39 us (9%)
  other arithmetic  15.2 us (3%)
    ppermute x73, waiting for transfers between devices, permuted(): return lax.ppermute(value, BOTH, pairs)  161 us
    pallas_call x26, Pallas kernels, call(): pl.pallas_call(kernel, out_shape=outs, in_specs=[pl.BlockSpec(memory_spac...  107 us
    ppermute x73, starting transfers between devices, permuted(): return lax.ppermute(value, BOTH, pairs)  88 us
    unnamed x229, local copies, waits for them, and re-layouts  31.9 us
    pallas_call x1, Pallas kernels, body(): pl.pallas_call(functools.partial(ffn_kernel, fold=fast, narrow=narrow, pi...  23.8 us
  transfers between devices with their start and end apart: 73, of which 34 were waited for; matrix products, arithmetic and copies ran while one was open for 2% of the time, Pallas kernels for 24%

profile of v3, /device:TPU:0, one launch (start us, length us, event | category | flops | bytes accessed | tf_op | source)
XLA Modules:
  0.0 437.5 jit_solution(6864759933653663355)
XLA Ops:
  11.2 11.4 %collective-permute-done.refs_1_ = bf16[9,24,768]{2,1,0:T(8,128)(2,1)S(1)} collective-permute-done((bf16[9,24,768]{2,1,0:T(8,128)(2,1)S(1)}, bf16[9,24,768]{2,1,0:T(8,128)(2,1)S(1)}, u32[]{:S(2)}, u32[]{:S(2)}) %collective-permute-start) | collective-permute-done | bytes 331808 | tf_op jit(solution)/shard_map/ppermute | solution.py:658
  22.6 11.7 %collective-permute-done.1.refs_2_ = bf16[9,24,768]{2,1,0:T(8,128)(2,1)S(1)} collective-permute-done((bf16[9,24,768]{2,1,0:T(8,128)(2,1)S(1)}, bf16[9,24,768]{2,1,0:T(8,128)(2,1)S(1)}, u32[]{:S(2)}, u32[]{:S(2)}) %collective-permute-start.1) | collective-permute-done | bytes 331808 | tf_op jit(solution)/shard_map/ppermute | solution.py:658
  46.9 5.2 %collective-permute-start.4 = (bf16[656,256]{1,0:T(8,128)(2,1)}, bf16[656,256]{1,0:T(8,128)(2,1)}, u32[]{:S(2)}, u32[]{:S(2)}) collective-permute-start(bf16[656,256]{1,0:T(8,128)(2,1)} %get-tuple-element.172), channel_id=1, source_target_pairs={{0,2},{1,3},{2,0},{3,1},{4,6},{5,7},{6,4},{7,5},{8,10},{9,11},{10,... | collective-permute-start | bytes 1007624 | tf_op jit(solution)/shard_map/ppermute | solution.py:658
  52.2 8.1 %collective-permute-done.9.refs_8_.refs_4_ = bf16[4,96,768]{2,1,0:T(8,128)(2,1)S(1)} collective-permute-done((bf16[4,96,768]{2,1,0:T(8,128)(2,1)S(1)}, bf16[4,96,768]{2,1,0:T(8,128)(2,1)S(1)}, u32[]{:S(2)}, u32[]{:S(2)}) %collective-permute-start.9) | collective-permute-done | bytes 589856 | tf_op jit(solution)/shard_map/ppermute | solution.py:658
  60.3 7.6 %collective-permute-start.3 = (bf16[656,256]{1,0:T(8,128)(2,1)}, bf16[656,256]{1,0:T(8,128)(2,1)}, u32[]{:S(2)}, u32[]{:S(2)}) collective-permute-start(bf16[656,256]{1,0:T(8,128)(2,1)} %get-tuple-element.170), channel_id=1, source_target_pairs={{0,1},{1,0},{2,3},{3,2},{4,5},{5,4},{6,7},{7,6},{8,9},{9,8},{10,11... | collective-permute-start | bytes 1007624 | tf_op jit(solution)/shard_map/ppermute | solution.py:658
  75.4 5.8 %collective-permute-done.3.refs_1_ = bf16[656,256]{1,0:T(8,128)(2,1)} collective-permute-done((bf16[656,256]{1,0:T(8,128)(2,1)}, bf16[656,256]{1,0:T(8,128)(2,1)}, u32[]{:S(2)}, u32[]{:S(2)}) %collective-permute-start.3) | collective-permute-done | bytes 335904 | tf_op jit(solution)/shard_map/ppermute | solution.py:658
  87.3 10.5 %collective-permute-done.13.refs_1_ = bf16[24,24,256]{2,1,0:T(8,128)(2,1)S(1)} collective-permute-done((bf16[24,24,256]{2,1,0:T(8,128)(2,1)S(1)}, bf16[24,24,256]{2,1,0:T(8,128)(2,1)S(1)}, u32[]{:S(2)}, u32[]{:S(2)}) %collective-permute-start.13) | collective-permute-done | bytes 294944 | tf_op jit(solution)/shard_map/ppermute | solution.py:658
  105.9 14.0 %first.1 = (f32[8,768]{1,0:T(8,128)S(1)}, bf16[512,768]{1,0:T(8,128)(2,1)S(1)}, bf16[512,768]{1,0:T(8,128)(2,1)S(1)}, bf16[3,512,768]{2,1,0:T(8,128)(2,1)S(1)}, ...) custom-call(s32[4]{0:T(128)S(1)} %pad_add_fusion.at_ref, ...), custom_call_target="tpu_custom_call" | custom-call | flops 18400000000 | bytes 1048576 | tf_op jit(solution)/shard_map/first/pallas_call | solution.py:631
  122.1 11.2 %collective-permute-done.22.refs_8_.refs_4_ = bf16[5,96,768]{2,1,0:T(8,128)(2,1)S(1)} collective-permute-done((bf16[5,96,768]{2,1,0:T(8,128)(2,1)S(1)}, bf16[5,96,768]{2,1,0:T(8,128)(2,1)S(1)}, u32[]{:S(2)}, u32[]{:S(2)}) %collective-permute-start.22) | collective-permute-done | bytes 737312 | tf_op jit(solution)/shard_map/ppermute | solution.py:658
  137.7 11.6 %collective-permute-done.18.refs_3_ = bf16[2,128,768]{2,1,0:T(8,128)(2,1)S(1)} collective-permute-done((bf16[2,128,768]{2,1,0:T(8,128)(2,1)S(1)}, bf16[2,128,768]{2,1,0:T(8,128)(2,1)S(1)}, u32[]{:S(2)}, u32[]{:S(2)}) %collective-permute-start.18) | collective-permute-done | bytes 393248 | tf_op jit(solution)/shard_map/ppermute | solution.py:658
  149.3 17.4 %collective-permute-done.17.refs_2_ = bf16[2,128,768]{2,1,0:T(8,128)(2,1)S(1)} collective-permute-done((bf16[2,128,768]{2,1,0:T(8,128)(2,1)S(1)}, bf16[2,128,768]{2,1,0:T(8,128)(2,1)S(1)}, u32[]{:S(2)}, u32[]{:S(2)}) %collective-permute-start.17) | collective-permute-done | bytes 393248 | tf_op jit(solution)/shard_map/ppermute | solution.py:658
  167.1 11.1 %collective-permute-done.16.refs_1_ = bf16[2,128,768]{2,1,0:T(8,128)(2,1)S(1)} collective-permute-done((bf16[2,128,768]{2,1,0:T(8,128)(2,1)S(1)}, bf16[2,128,768]{2,1,0:T(8,128)(2,1)S(1)}, u32[]{:S(2)}, u32[]{:S(2)}) %collective-permute-start.16) | collective-permute-done | bytes 393248 | tf_op jit(solution)/shard_map/ppermute | solution.py:658
  179.8 17.0 %second.1 = (bf16[512,768]{1,0:T(8,128)(2,1)S(1)}, bf16[512,768]{1,0:T(8,128)(2,1)S(1)}, f32[512,768]{1,0:T(8,128)S(1)}, bf16[512,768]{1,0:T(8,128)(2,1)S(1)}, b...) custom-call(s32[4]{0:T(128)S(1)} %pad_add_fusion.at_ref, ...), custom_call_target="tpu_custom_call" | custom-call | flops 24149999616 | bytes 1048576 | tf_op jit(solution)/shard_map/second/pallas_call | solution.py:631
  214.1 23.8 %ffn.1 = (bf16[128,768]{1,0:T(8,128)(2,1)S(1)}, bf16[128,768]{1,0:T(8,128)(2,1)S(1)}, bf16[128,768]{1,0:T(8,128)(2,1)S(1)}, bf16[128,768]{1,0:T(8,128)(2,1)S(1)}...) custom-call(s32[4]{0:T(128)S(1)} %pad_add_fusion.at_ref, ...), custom_call_target="tpu_custom_call" | custom-call | flops 27599998976 | bytes 1048576 | tf_op jit(solution)/shard_map/ffn/pallas_call | solution.py:932
  254.9 15.9 %cross_back.1.refs_8_ = bf16[3,512,768]{2,1,0:T(8,128)(2,1)S(1)} custom-call(s32[4]{0:T(128)S(1)} %pad_add_fusion.at_ref, bf16[5,96,768]{2,1,0:T(8,128)(2,1)S(1)} %bitcast.75, bf16[5,96,768]{2,1,0:T(8,128)(2,1)S(1)} %collective-permute-done.19.refs_5_.refs_1_, bf16[5,96,768]{2,1,0:T(8,128)(2,1)S(1)} %collective-permute-done.20.refs_6_.refs_2_, ...), custom_call_target="tpu_custom_call" | custom-call | flops 20700000256 | bytes 1048576 | tf_op jit(solution)/shard_map/cross_back/pallas_call | solution.py:631
  272.3 8.5 %collective-permute-done.38.from_x = bf16[2,1152,256]{2,1,0:T(8,128)(2,1)S(1)} collective-permute-done((bf16[2,1152,256]{2,1,0:T(8,128)(2,1)S(1)}, bf16[2,1152,256]{2,1,0:T(8,128)(2,1)S(1)}, u32[]{:S(2)}, u32[]{:S(2)}) %collective-permute-start.38) | collective-permute-done | bytes 1179680 | tf_op jit(solution)/shard_map/ppermute | solution.py:658
  284.3 7.8 %second_back.1 = (bf16[128,768]{1,0:T(8,128)(2,1)S(1)}, bf16[128,768]{1,0:T(8,128)(2,1)S(1)}, bf16[128,768]{1,0:T(8,128)(2,1)S(1)}, bf16[128,768]{1,0:T(8,128)(2...) custom-call(s32[4]{0:T(128)S(1)} %pad_add_fusion.at_ref, ...), custom_call_target="tpu_custom_call" | custom-call | flops 13799999488 | bytes 1048576 | tf_op jit(solution)/shard_map/second_back/pallas_call | solution.py:631
  292.1 3.9 collective-permute-done.40.from_x
  307.0 15.7 %self_back.1 = (bf16[3,512,768]{2,1,0:T(8,128)(2,1)S(1)}, bf16[12,512,512]{2,1,0:T(8,128)(2,1)S(1)}) custom-call(s32[4]{0:T(128)S(1)} %pad_add_fusion.at_ref, bf16[5,96,768]{2,1,0:T(8,128)(2,1)S(1)} %bitcast.77, bf16[5,96,768]{2,1,0:T(8,128)(2,1)S(1)} %copy-done.4, bf16[5,96,768]{2,1,0:T(8,128)(2,1)S(1)} %collective-permute-done.20.refs_6_.refs_2_, ...), custom_call_target="tpu_custom_call" | custom-call | flops 23000000512 | bytes 1048576 | tf_op jit(solution)/shard_map/self_back/pallas_call | solution.py:631
  331.1 6.1 %first_back.1 = (bf16[128,768]{1,0:T(8,128)(2,1)S(1)}, bf16[128,768]{1,0:T(8,128)(2,1)S(1)}, bf16[128,768]{1,0:T(8,128)(2,1)S(1)}, bf16[128,768]{1,0:T(8,128)(2,...) custom-call(s32[4]{0:T(128)S(1)} %pad_add_fusion.at_ref, ...), custom_call_target="tpu_custom_call" | custom-call | flops 10350000128 | bytes 1048576 | tf_op jit(solution)/shard_map/first_back/pallas_call | solution.py:631
  337.1 4.1 collective-permute-done.49.refs_2_
  346.0 4.1 collective-permute-start.54
  360.6 11.4 %table.1 = f32[12,128]{1,0:T(8,128)S(1)} custom-call(bf16[12,512,512]{2,1,0:T(8,128)(2,1)S(1)} %copy-done.59, s32[512,512]{1,0:T(8,128)S(1)} %copy-done.55), custom_call_target="tpu_custom_call" | custom-call | flops 12650000384 | bytes 1048576 | tf_op jit(solution)/shard_map/table/pallas_call | solution.py:631
  377.9 6.3 %collective-permute-done.60.from_x = bf16[2,144,768]{2,1,0:T(8,128)(2,1)S(1)} collective-permute-done((bf16[2,144,768]{2,1,0:T(8,128)(2,1)S(1)}, bf16[2,144,768]{2,1,0:T(8,128)(2,1)S(1)}, u32[]{:S(2)}, u32[]{:S(2)}) %collective-permute-start.60) | collective-permute-done | bytes 442400 | tf_op jit(solution)/shard_map/ppermute | solution.py:658
  (453 shorter events, 183.5 us)
Async XLA Ops:
  37.9 34.6 %collective-permute-start.11 = (bf16[4,96,768]{2,1,0:T(8,128)(2,1)S(1)}, bf16[4,96,768]{2,1,0:T(8,128)(2,1)S(1)}, u32[]{:S(2)}, u32[]{:S(2)}) collective-permute-start(bf16[4,96,768]{2,1,0:T(8,128)(2,1)S(1)} %bitcast.79), channel_id=1, source_target_pairs={{0,24},{1,25},{2,26},{3,27},{4,28},{5,29},{6,30},{7,31},{8,16},{9,... | collective-permute-start | bytes 1769480 | tf_op jit(solution)/shard_map/ppermute | solution.py:658
  39.3 33.3 %collective-permute-start.7 = (bf16[4,96,768]{2,1,0:T(8,128)(2,1)S(1)}, bf16[4,96,768]{2,1,0:T(8,128)(2,1)S(1)}, u32[]{:S(2)}, u32[]{:S(2)}) collective-permute-start(bf16[4,96,768]{2,1,0:T(8,128)(2,1)S(1)} %bitcast.80), channel_id=1, source_target_pairs={{0,8},{1,9},{2,10},{3,11},{4,12},{5,13},{6,14},{7,15},{8,0},{9,1},... | collective-permute-start | bytes 1769480 | tf_op jit(solution)/shard_map/ppermute | solution.py:658
  44.5 28.7 %collective-permute-start.5 = (bf16[656,256]{1,0:T(8,128)(2,1)}, bf16[656,256]{1,0:T(8,128)(2,1)}, u32[]{:S(2)}, u32[]{:S(2)}) collective-permute-start(bf16[656,256]{1,0:T(8,128)(2,1)} %get-tuple-element.174), channel_id=1, source_target_pairs={{0,3},{1,2},{2,1},{3,0},{4,7},{5,6},{6,5},{7,4},{8,11},{9,10},{10,... | collective-permute-start | bytes 1007624 | tf_op jit(solution)/shard_map/ppermute | solution.py:658
  46.9 28.5 %collective-permute-start.4 = (bf16[656,256]{1,0:T(8,128)(2,1)}, bf16[656,256]{1,0:T(8,128)(2,1)}, u32[]{:S(2)}, u32[]{:S(2)}) collective-permute-start(bf16[656,256]{1,0:T(8,128)(2,1)} %get-tuple-element.172), channel_id=1, source_target_pairs={{0,2},{1,3},{2,0},{3,1},{4,6},{5,7},{6,4},{7,5},{8,10},{9,11},{10,... | collective-permute-start | bytes 1007624 | tf_op jit(solution)/shard_map/ppermute | solution.py:658
  72.7 26.5 %collective-permute-start.10 = (bf16[4,96,768]{2,1,0:T(8,128)(2,1)S(1)}, bf16[4,96,768]{2,1,0:T(8,128)(2,1)S(1)}, u32[]{:S(2)}, u32[]{:S(2)}) collective-permute-start(bf16[4,96,768]{2,1,0:T(8,128)(2,1)S(1)} %collective-permute-done.9.refs_8_.refs_4_), channel_id=1, source_target_pairs={{0,4},{1,5},{2,6},{3,7},{4,0},{5,1},{6,2},{7,3},{8,12},{9,13},{10,... | collective-permute-start | bytes 1769480 | tf_op jit(solution)/shard_map/ppermute | solution.py:658
  73.2 27.6 %collective-permute-start.12 = (bf16[4,96,768]{2,1,0:T(8,128)(2,1)S(1)}, bf16[4,96,768]{2,1,0:T(8,128)(2,1)S(1)}, u32[]{:S(2)}, u32[]{:S(2)}) collective-permute-start(bf16[4,96,768]{2,1,0:T(8,128)(2,1)S(1)} %collective-permute-done.11.refs_10_.refs_6_), channel_id=1, source_target_pairs={{0,4},{1,5},{2,6},{3,7},{4,0},{5,1},{6,2},{7,3},{8,12},{9,13},{10,... | collective-permute-start | bytes 1769480 | tf_op jit(solution)/shard_map/ppermute | solution.py:658
  75.4 26.4 %collective-permute-start.8 = (bf16[4,96,768]{2,1,0:T(8,128)(2,1)S(1)}, bf16[4,96,768]{2,1,0:T(8,128)(2,1)S(1)}, u32[]{:S(2)}, u32[]{:S(2)}) collective-permute-start(bf16[4,96,768]{2,1,0:T(8,128)(2,1)S(1)} %collective-permute-done.7.refs_6_.refs_2_), channel_id=1, source_target_pairs={{0,4},{1,5},{2,6},{3,7},{4,0},{5,1},{6,2},{7,3},{8,12},{9,13},{10,... | collective-permute-start | bytes 1769480 | tf_op jit(solution)/shard_map/ppermute | solution.py:658
  84.2 35.8 %collective-permute-start.14 = (bf16[24,24,256]{2,1,0:T(8,128)(2,1)S(1)}, bf16[24,24,256]{2,1,0:T(8,128)(2,1)S(1)}, u32[]{:S(2)}, u32[]{:S(2)}) collective-permute-start(bf16[24,24,256]{2,1,0:T(8,128)(2,1)S(1)} %pad_maximum_fusion.2.refs_0_), channel_id=1, source_target_pairs={{0,2},{1,3},{2,0},{3,1},{4,6},{5,7},{6,4},{7,5},{8,10},{9,11},{10,... | collective-permute-start | bytes 884744 | tf_op jit(solution)/shard_map/ppermute | solution.py:658
  100.7 32.6 %collective-permute-start.22 = (bf16[5,96,768]{2,1,0:T(8,128)(2,1)S(1)}, bf16[5,96,768]{2,1,0:T(8,128)(2,1)S(1)}, u32[]{:S(2)}, u32[]{:S(2)}) collective-permute-start(bf16[5,96,768]{2,1,0:T(8,128)(2,1)S(1)} %bitcast.71), channel_id=1, source_target_pairs={{0,16},{1,17},{2,18},{3,19},{4,20},{5,21},{6,22},{7,23},{8,24},{9,... | collective-permute-start | bytes 2211848 | tf_op jit(solution)/shard_map/ppermute | solution.py:658
  101.8 31.5 %collective-permute-start.24 = (bf16[5,96,768]{2,1,0:T(8,128)(2,1)S(1)}, bf16[5,96,768]{2,1,0:T(8,128)(2,1)S(1)}, u32[]{:S(2)}, u32[]{:S(2)}) collective-permute-start(bf16[5,96,768]{2,1,0:T(8,128)(2,1)S(1)} %bitcast.72), channel_id=1, source_target_pairs={{0,24},{1,25},{2,26},{3,27},{4,28},{5,29},{6,30},{7,31},{8,16},{9,... | collective-permute-start | bytes 2211848 | tf_op jit(solution)/shard_map/ppermute | solution.py:658
  133.3 33.3 %collective-permute-start.26 = (bf16[24,96,256]{2,1,0:T(8,128)(2,1)S(1)}, bf16[24,96,256]{2,1,0:T(8,128)(2,1)S(1)}, u32[]{:S(2)}, u32[]{:S(2)}) collective-permute-start(bf16[24,96,256]{2,1,0:T(8,128)(2,1)S(1)} %pad_maximum_fusion.refs_1_), channel_id=1, source_target_pairs={{0,8},{1,9},{2,10},{3,11},{4,12},{5,13},{6,14},{7,15},{8,0},{9,1},... | collective-permute-start | bytes 3538952 | tf_op jit(solution)/shard_map/ppermute | solution.py:658
  134.1 33.0 %collective-permute-start.27 = (bf16[24,96,256]{2,1,0:T(8,128)(2,1)S(1)}, bf16[24,96,256]{2,1,0:T(8,128)(2,1)S(1)}, u32[]{:S(2)}, u32[]{:S(2)}) collective-permute-start(bf16[24,96,256]{2,1,0:T(8,128)(2,1)S(1)} %pad_maximum_fusion.refs_1_), channel_id=1, source_target_pairs={{0,16},{1,17},{2,18},{3,19},{4,20},{5,21},{6,22},{7,23},{8,24},{9,... | collective-permute-start | bytes 3538952 | tf_op jit(solution)/shard_map/ppermute | solution.py:658
  137.6 29.0 %collective-permute-start.17 = (bf16[2,128,768]{2,1,0:T(8,128)(2,1)S(1)}, bf16[2,128,768]{2,1,0:T(8,128)(2,1)S(1)}, u32[]{:S(2)}, u32[]{:S(2)}) collective-permute-start(bf16[2,128,768]{2,1,0:T(8,128)(2,1)S(1)} %copy-done.33), channel_id=1, source_target_pairs={{0,2},{1,3},{2,0},{3,1},{4,6},{5,7},{6,4},{7,5},{8,10},{9,11},{10,... | collective-permute-start | bytes 1179656 | tf_op jit(solution)/shard_map/ppermute | solution.py:658
  137.7 42.1 %collective-permute-start.19 = (bf16[5,96,768]{2,1,0:T(8,128)(2,1)S(1)}, bf16[5,96,768]{2,1,0:T(8,128)(2,1)S(1)}, u32[]{:S(2)}, u32[]{:S(2)}) collective-permute-start(bf16[5,96,768]{2,1,0:T(8,128)(2,1)S(1)} %bitcast.73), channel_id=1, source_target_pairs={{0,4},{1,5},{2,6},{3,7},{4,0},{5,1},{6,2},{7,3},{8,12},{9,13},{10,... | collective-permute-start | bytes 2211848 | tf_op jit(solution)/shard_map/ppermute | solution.py:658
  149.3 30.5 %collective-permute-start.25 = (bf16[5,96,768]{2,1,0:T(8,128)(2,1)S(1)}, bf16[5,96,768]{2,1,0:T(8,128)(2,1)S(1)}, u32[]{:S(2)}, u32[]{:S(2)}) collective-permute-start(bf16[5,96,768]{2,1,0:T(8,128)(2,1)S(1)} %collective-permute-done.24.refs_10_.refs_6_), channel_id=1, source_target_pairs={{0,4},{1,5},{2,6},{3,7},{4,0},{5,1},{6,2},{7,3},{8,12},{9,13},{10,... | collective-permute-start | bytes 2211848 | tf_op jit(solution)/shard_map/ppermute | solution.py:658
  178.2 28.0 %collective-permute-start.31 = (bf16[24,96,256]{2,1,0:T(8,128)(2,1)S(1)}, bf16[24,96,256]{2,1,0:T(8,128)(2,1)S(1)}, u32[]{:S(2)}, u32[]{:S(2)}) collective-permute-start(bf16[24,96,256]{2,1,0:T(8,128)(2,1)S(1)} %pad_maximum_fusion.refs_1_), channel_id=1, source_target_pairs={{0,24},{1,25},{2,26},{3,27},{4,28},{5,29},{6,30},{7,31},{8,16},{9,... | collective-permute-start | bytes 3538952 | tf_op jit(solution)/shard_map/ppermute | solution.py:658
  240.3 30.5 %collective-permute-start.35 = (bf16[128,768]{1,0:T(8,128)(2,1)S(1)}, bf16[128,768]{1,0:T(8,128)(2,1)S(1)}, u32[]{:S(2)}, u32[]{:S(2)}) collective-permute-start(bf16[128,768]{1,0:T(8,128)(2,1)S(1)} %get-tuple-element.216), channel_id=1, source_target_pairs={{0,1},{1,0},{2,3},{3,2},{4,5},{5,4},{6,7},{7,6},{8,9},{9,8},{10,11... | collective-permute-start | bytes 589832 | tf_op jit(solution)/shard_map/ppermute | solution.py:658
  240.9 29.9 %collective-permute-start.36 = (bf16[128,768]{1,0:T(8,128)(2,1)S(1)}, bf16[128,768]{1,0:T(8,128)(2,1)S(1)}, u32[]{:S(2)}, u32[]{:S(2)}) collective-permute-start(bf16[128,768]{1,0:T(8,128)(2,1)S(1)} %get-tuple-element.217), channel_id=1, source_target_pairs={{0,2},{1,3},{2,0},{3,1},{4,6},{5,7},{6,4},{7,5},{8,10},{9,11},{10,... | collective-permute-start | bytes 589832 | tf_op jit(solution)/shard_map/ppermute | solution.py:658
  243.0 27.8 %collective-permute-start.37 = (bf16[128,768]{1,0:T(8,128)(2,1)S(1)}, bf16[128,768]{1,0:T(8,128)(2,1)S(1)}, u32[]{:S(2)}, u32[]{:S(2)}) collective-permute-start(bf16[128,768]{1,0:T(8,128)(2,1)S(1)} %get-tuple-element.218), channel_id=1, source_target_pairs={{0,3},{1,2},{2,1},{3,0},{4,7},{5,6},{6,5},{7,4},{8,11},{9,10},{10,... | collective-permute-start | bytes 589832 | tf_op jit(solution)/shard_map/ppermute | solution.py:658
  252.8 28.1 %collective-permute-start.38 = (bf16[2,1152,256]{2,1,0:T(8,128)(2,1)S(1)}, bf16[2,1152,256]{2,1,0:T(8,128)(2,1)S(1)}, u32[]{:S(2)}, u32[]{:S(2)}) collective-permute-start(bf16[2,1152,256]{2,1,0:T(8,128)(2,1)S(1)} %get-tuple-element.222), channel_id=1, source_target_pairs={{0,8},{1,9},{2,10},{3,11},{4,12},{5,13},{6,14},{7,15},{8,0},{9,1},... | collective-permute-start | bytes 3538952 | tf_op jit(solution)/shard_map/ppermute | solution.py:658
  253.4 27.7 %collective-permute-start.39 = (bf16[2,1152,256]{2,1,0:T(8,128)(2,1)S(1)}, bf16[2,1152,256]{2,1,0:T(8,128)(2,1)S(1)}, u32[]{:S(2)}, u32[]{:S(2)}) collective-permute-start(bf16[2,1152,256]{2,1,0:T(8,128)(2,1)S(1)} %get-tuple-element.223), channel_id=1, source_target_pairs={{0,16},{1,17},{2,18},{3,19},{4,20},{5,21},{6,22},{7,23},{8,24},{9,... | collective-permute-start | bytes 3538952 | tf_op jit(solution)/shard_map/ppermute | solution.py:658
  346.0 28.2 %collective-permute-start.54 = (bf16[120,768]{1,0:T(8,128)(2,1)S(1)}, bf16[120,768]{1,0:T(8,128)(2,1)S(1)}, u32[]{:S(2)}, u32[]{:S(2)}) collective-permute-start(bf16[120,768]{1,0:T(8,128)(2,1)S(1)} %get-tuple-element.274), channel_id=1, source_target_pairs={{0,1},{1,0},{2,3},{3,2},{4,5},{5,4},{6,7},{7,6},{8,9},{9,8},{10,11... | collective-permute-start | bytes 552968 | tf_op jit(solution)/shard_map/ppermute | solution.py:658
  375.4 39.4 %collective-permute-start.59 = (bf16[128,768]{1,0:T(8,128)(2,1)S(1)}, bf16[128,768]{1,0:T(8,128)(2,1)S(1)}, u32[]{:S(2)}, u32[]{:S(2)}) collective-permute-start(bf16[128,768]{1,0:T(8,128)(2,1)S(1)} %get-tuple-element.284), channel_id=1, source_target_pairs={{0,3},{1,2},{2,1},{3,0},{4,7},{5,6},{6,5},{7,4},{8,11},{9,10},{10,... | collective-permute-start | bytes 589832 | tf_op jit(solution)/shard_map/ppermute | solution.py:658
  377.6 37.2 %collective-permute-start.58 = (bf16[128,768]{1,0:T(8,128)(2,1)S(1)}, bf16[128,768]{1,0:T(8,128)(2,1)S(1)}, u32[]{:S(2)}, u32[]{:S(2)}) collective-permute-start(bf16[128,768]{1,0:T(8,128)(2,1)S(1)} %get-tuple-element.282), channel_id=1, source_target_pairs={{0,2},{1,3},{2,0},{3,1},{4,6},{5,7},{6,4},{7,5},{8,10},{9,11},{10,... | collective-permute-start | bytes 589832 | tf_op jit(solution)/shard_map/ppermute | solution.py:658
  (160 other events, 2250.7 us)
